TPU v7x, 32 devices: a whole 2x2x4 slice. The times are simulated.
32 devices in a mesh: dp: 2 (over x), row: 4 (over z), col: 4 (over y, core).
Axes of the slice: x: 2, y: 2, z: 4, core: 2. Of those that a mesh axis runs over, the one named last changes fastest.
Arguments:
- inputs: bfloat16 [2304, 4, 384], P(('dp', 'col'), 'row'), may hold values from -6 to 6
- cotangent: bfloat16 [2304, 4, 384], P(('dp', 'col'), 'row'), may hold values from -6 to 6
- slot_mask: int32 [8], replicated, may hold values from 0 to 1, as said below
- region_ids: int32 [24, 24], replicated, may hold values from 0 to 8, as said below
- offset_index: int32 [144, 144], replicated, may hold values from 0 to 528, as said below
- first_gain: float32 [768], P('row'), may hold values from 0.5 to 1.5
- first_shift: float32 [768], P('row'), may hold values from -1.75 to 1.75
- query_key_value: bfloat16 [384, 3, 4, 384], P('row', None, 'col'), may hold values from -0.21875 to 0.21875
- query_value_bias: float32 [2, 768], P(None, 'col'), may hold values from -3 to 3
- position_table: float32 [529, 24], P(None, 'col'), may hold values from -6 to 6
- output_weight: bfloat16 [384, 4, 384], P('col', 'row'), may hold values from -0.625 to 0.625
- output_bias: float32 [768], P('row'), may hold values from -1.75 to 1.75
- second_gain: float32 [768], P('row'), may hold values from 0.5 to 1.5
- second_shift: float32 [768], P('row'), may hold values from -1.75 to 1.75
- expand_weight: bfloat16 [768, 3072], P('row', 'col'), may hold values from -0.21875 to 0.21875
- expand_bias: float32 [3072], P('col'), may hold values from -1.75 to 1.75
- contract_weight: bfloat16 [1536, 4, 384], P('col', 'row'), may hold values from -0.109375 to 0.109375
- contract_bias: float32 [768], P('row'), may hold values from -1.75 to 1.75
Outputs:
- layer_output: bfloat16 [2304, 4, 384], P(('dp', 'col'), 'row')
- input_gradient: float32 [2304, 4, 384], P(('dp', 'col'), 'row')
- first_gain_gradient: float32 [768], P('row')
- first_shift_gradient: float32 [768], P('row')
- query_key_value_gradient: float32 [384, 3, 4, 384], P('row', None, 'col')
- query_value_bias_gradient: float32 [2, 768], P(None, 'col')
- position_table_gradient: float32 [529, 24], P(None, 'col')
- output_weight_gradient: float32 [384, 4, 384], P('col', 'row')
- output_bias_gradient: float32 [768], P('row')
- second_gain_gradient: float32 [768], P('row')
- second_shift_gradient: float32 [768], P('row')
- expand_weight_gradient: float32 [768, 3072], P('row', 'col')
- expand_bias_gradient: float32 [3072], P('col')
- contract_weight_gradient: float32 [1536, 4, 384], P('col', 'row')
- contract_bias_gradient: float32 [768], P('row')
Inputs may be any that keep to these rules, and one draw needn't show every extreme that they name: `slot_mask`: 1 on the first slots and 0 on the rest; at least one slot of each kind. `region_ids`: 3 times a band of the token's row plus a band of its column; bands 0, 1, 2 cut at two drawn places along each side, each band non-empty. `offset_index`: a one-to-one relabelling of the offset between two window positions: equal offsets give equal entries, and every entry appears.
All inputs are finite; a program needn't handle non-finite values.
Results may differ from a plain program's by a relative error of at most 0.012.
Values may be sent and summed in bfloat16 or wider, within the bound.
No kernel may reach another device: no remote copies, remote signals or barrier semaphores. Data moves between devices by JAX's collectives and lax.ppermute only.
A program may use at most 128 MiB of HBM per device.

v0:
```python
import types

import jax
import jax.numpy as jnp
from jax import lax
from jax.experimental import pallas as pl
from jax.experimental.pallas import tpu as pltpu
from jax.sharding import PartitionSpec as P

HEAD_DIM = 32
SIDE = 24
WIN = 12
SHIFT = 6
REL = 529
CELLS = WIN * WIN
NORM_EPS = 1e-05
MASK_FILL = -100.0
BF = jnp.bfloat16
F32 = jnp.float32
NT = (((1,), (1,)), ((), ()))
TN = (((0,), (0,)), ((), ()))
BLOCK = 192
WIDTH = 768
HALF = 384
GROUP = 4
TOKENS = GROUP * CELLS
HEADS = BLOCK // HEAD_DIM
VMEM_MIB = 24
ORDER_MIB = 60
ROOT_HALF = 0.7071067811865476
ROOT_TWO_PI_INV = 0.3989422804014327


def dot(a, b):
    return jnp.dot(a, b, preferred_element_type=F32)


def dot_nt(a, b):
    return lax.dot_general(a, b, NT, preferred_element_type=F32)


def dot_tn(a, b):
    return lax.dot_general(a, b, TN, preferred_element_type=F32)


def iota(shape, dim):
    return lax.broadcasted_iota(jnp.int32, shape, dim)


def aligned(value, step):
    return pl.multiple_of(value, step)


MICROS = 10


def cost_of(kernel):
    micros = 0.01 if kernel in CHEAP else MICROS
    return pl.CostEstimate(flops=int(micros * 1.1e9), bytes_accessed=int(micros * 3.6e6), transcendentals=0)


def run(kernel, outs, scratch, *arrays, scalars=(), mib=VMEM_MIB, after=()):
    vmem = pl.BlockSpec(memory_space=pltpu.VMEM)
    smem = pl.BlockSpec(memory_space=pltpu.SMEM)
    anywhere = pl.BlockSpec(memory_space=pl.ANY)
    given = len(scalars) + len(arrays)
    made = given + len(after) + len(outs)

    def body(*refs):
        dp = lax.axis_index("dp")
        ids = (dp % 2, lax.axis_index("row"), lax.axis_index("col"), dp)
        kernel(ids, *refs[:given], *refs[given + len(after) : made], *refs[made + 1 :])
        refs[made][...] = jnp.zeros(refs[made].shape, F32)

    return pl.pallas_call(
        body,
        out_shape=[jax.ShapeDtypeStruct(shape, dtype) for shape, dtype in (*outs, ((8, 128), F32))],
        in_specs=[smem] * len(scalars) + [vmem] * len(arrays) + [anywhere] * len(after),
        out_specs=[vmem] * (len(outs) + 1),
        scratch_shapes=[pltpu.VMEM(shape, dtype) for shape, dtype in scratch],
        compiler_params=pltpu.CompilerParams(vmem_limit_bytes=mib * 1024 * 1024),
        cost_estimate=cost_of(kernel),
        name=kernel.__name__,
    )(*scalars, *arrays, *after)


def place(window, position):
    row = (position * 171) >> 11
    col = position - row * WIN
    row = row + (window // 2) * WIN + SHIFT
    col = col + (window % 2) * WIN + SHIFT
    row = jnp.where(row >= SIDE, row - SIDE, row)
    col = jnp.where(col >= SIDE, col - SIDE, col)
    token = row * SIDE + col
    return token >> 1, token & 1


def window_rows(paired_even, paired_odd, window, begin, rows):
    count = paired_even.shape[0]
    half, parity = place(window, iota((rows, count), 0) + begin)
    hit = half == iota((rows, count), 1)
    pick_even = jnp.where(hit & (parity == 0), 1.0, 0.0).astype(BF)
    pick_odd = jnp.where(hit & (parity == 1), 1.0, 0.0).astype(BF)
    return dot(pick_even, paired_even) + dot(pick_odd, paired_odd)


LINES = CELLS // 2
FIRST = 2 * CELLS // 2 + 16
QUARTER = BLOCK // 4
STACK = HEADS * CELLS + 32
CHUNKS = ((0, 256), (256, 256), (512, 256), (768, 128))
ATT = 2 * CELLS


def order_kernel(ids, vectors, paired, cotangent, joined, out_own, o0, o1, o2, o3, held):
    z = ids[1]
    sources = [(v[:, :BLOCK], v[:, BLOCK:]) for v in (paired, cotangent)]
    held[...] = jnp.zeros(held.shape, F32)
    whole = vectors[...]
    high = whole.astype(BF).astype(F32)
    rest = whole - high
    middle = rest.astype(BF).astype(F32)
    begin = aligned(ids[0] * QUARTER, 16)
    for s, out in enumerate((o0, o1, o2, o3)):
        held[s, 2 * LINES : 2 * LINES + 6, :BLOCK] = high
        held[s, 2 * LINES : 2 * LINES + 6, BLOCK:] = middle
        held[s, 2 * LINES + 8 : 2 * LINES + 14, :BLOCK] = rest - middle
        for n, (even, odd) in enumerate(sources):
            for k in range(2):
                held[s, n * LINES : (n + 1) * LINES, k * BLOCK : (k + 1) * BLOCK] = window_rows(
                    even, odd, (z + s) % GROUP, k * LINES, LINES
                )
        out[0:FIRST, :] = held[s].astype(BF)
        for part in range(3):
            out[FIRST + part * QUARTER : FIRST + (part + 1) * QUARTER, :] = joined[part, pl.ds(begin, QUARTER), :]
        out[FIRST + 3 * QUARTER :, :] = out_own[pl.ds(begin, QUARTER), :]


def unpack_kernel(ids, slots, a, b, c, d, tokens, vectors, stack):
    flag = slots[ids[3] * GROUP + ids[2]] != 0
    vectors[...] = jnp.zeros(vectors.shape, F32)
    for s, piece in enumerate((a, b, c, d)):
        lanes = slice(s * BLOCK, (s + 1) * BLOCK)
        whole = piece[0:FIRST, :].astype(F32)
        for n in range(2):
            part = whole[n * LINES : (n + 1) * LINES]
            part = jnp.concatenate([part[:, :BLOCK], part[:, BLOCK:]], axis=0)
            if n == 1:
                part = jnp.where(flag, part, jnp.zeros_like(part))
            tokens[n * CELLS : (n + 1) * CELLS, lanes] = part.astype(BF)
        line = 2 * LINES
        vectors[0:6, lanes] = (
            whole[line : line + 6, :BLOCK] + whole[line : line + 6, BLOCK:] + whole[line + 8 : line + 14, :BLOCK]
        )
        if s > 0:
            stack[s - 1] = piece[FIRST:, :]


def couple_kernel(ids, a, b, out):
    out[0] = a[...]
    out[1] = b[...]


def half_kernel(ids, whole, out):
    rows = out.shape[0]
    out[...] = whole[pl.ds(aligned(ids[0] * rows, 16), rows), :]


def pass_kernel(ids, whole, out):
    out[...] = whole[...]


def stack_kernel(ids, a, b, c, out):
    for s, piece in enumerate((a, b, c)):
        out[s] = piece[...]


def restore_halves(ids, pieces):
    z = ids[1]
    count = SIDE * SIDE // 2
    even = odd = None
    for s in range(GROUP):
        half, parity = place((z + s) % GROUP, iota((count, CELLS), 1))
        hit = half == iota((count, CELLS), 0)
        pick_even = jnp.where(hit & (parity == 0), 1.0, 0.0).astype(BF)
        pick_odd = jnp.where(hit & (parity == 1), 1.0, 0.0).astype(BF)
        piece = pieces[s]
        more_even = dot(pick_even, piece)
        more_odd = dot(pick_odd, piece)
        even = more_even if even is None else even + more_even
        odd = more_odd if odd is None else odd + more_odd
    return even, odd


def restore_kernel(ids, a, b, c, d, out):
    even, odd = restore_halves(ids, [window_piece(v[v.shape[0] - EXTRA :, :]) for v in (a, b, c, d)])
    out[:, :BLOCK] = even.astype(BF)
    out[:, BLOCK:] = odd.astype(BF)


def restore_wide_kernel(ids, a, b, c, d, out, whole):
    even, odd = restore_halves(ids, [window_piece(v[v.shape[0] - EXTRA :, :]) for v in (a, b, c, d)])
    whole[:, :BLOCK] = even
    whole[:, BLOCK:] = odd
    count = whole.shape[0]
    for k in range(3):
        out[pl.ds(k, count, stride=3), :] = whole[:, k * 128 : (k + 1) * 128]


def pair_picks(rows):
    low = iota((rows, rows // 2), 0)
    high = iota((rows, rows // 2), 1)
    pick_even = jnp.where(low == 2 * high, 1.0, 0.0).astype(BF)
    pick_odd = jnp.where(low == 2 * high + 1, 1.0, 0.0).astype(BF)
    return pick_even, pick_odd


def hidden_perm():
    natural = iota((WIDTH, WIDTH), 0)
    split = iota((WIDTH, WIDTH), 1)
    wanted = jnp.where(split < HALF, 2 * split, 2 * split - (WIDTH - 1))
    return jnp.where(natural == wanted, 1.0, 0.0).astype(BF)


def put_halves(ids, held, s, where, rows, mine, other):
    x = ids[0]
    held[(s, *where, pl.ds(aligned(x * rows, 16), rows), slice(None))] = mine
    held[(s, *where, pl.ds(aligned((1 - x) * rows, 16), rows), slice(None))] = other


def first_weights_kernel(ids, own, own_out, mine, other, out, out_square, held):
    pick_even, pick_odd = pair_picks(BLOCK)
    for part in range(4):
        held[0, part] = own[part] if part < 3 else own_out[...]
        lines = slice(part * QUARTER, (part + 1) * QUARTER)
        for s in range(1, GROUP):
            put_halves(ids, held, s, (part,), QUARTER, mine[s - 1, lines, :], other[s - 1, lines, :])
    for s in range(GROUP):
        for part in range(4):
            block = (dot(pick_even, held[s, part, :, :BLOCK]) + dot(pick_odd, held[s, part, :, BLOCK:])).astype(BF)
            if part < 3:
                out[part, s * BLOCK : (s + 1) * BLOCK, :] = block
            else:
                out_square[:, s * BLOCK : (s + 1) * BLOCK] = block


def expand_weights_kernel(ids, own, mine, other, bias, out, out_bias, held, rows):
    perm = hidden_perm()
    held[0] = own[...]
    for s in range(1, GROUP):
        put_halves(ids, held, s, (), BLOCK // 2, mine[s - 1], other[s - 1])
    for s in range(GROUP):
        out[s * BLOCK : (s + 1) * BLOCK, :] = dot(held[s], perm).astype(BF)
    high = bias[...].astype(BF).astype(F32)
    rest = bias[...] - high
    middle = rest.astype(BF).astype(F32)
    rows[...] = jnp.zeros(rows.shape, F32)
    rows[0:1, :] = high
    rows[1:2, :] = middle
    rows[2:3, :] = rest - middle
    found = dot(rows[...].astype(BF), perm)
    out_bias[...] = found[0:1] + found[1:2] + found[2:3]


def contract_weights_kernel(ids, own, m1, m2, m3, out):
    for s, piece in enumerate((own, m1, m2, m3)):
        for q in range(2):
            out[q * HALF : (q + 1) * HALF, s * BLOCK : (s + 1) * BLOCK] = piece[:, q * BLOCK : (q + 1) * BLOCK]


def entry_hits(offset, index):
    row = offset[pl.ds(index, 1), :]
    return jnp.where(iota((REL, CELLS), 0) == row, 1.0, 0.0).astype(BF)


STRIP = 3 * 128
FAR = WIN - 1
SPAN = FAR * WIN


def lane_col():
    lane = iota((8, STRIP), 1)
    return lane - ((lane * 171) >> 11) * WIN


def bias_kernel(ids, table, offset, labels, labels_t, out, parts, strips, mask):
    z = ids[1]
    parts[...] = jnp.zeros(parts.shape, F32)
    whole = table[...]
    high = whole.astype(BF).astype(F32)
    rest = whole - high
    middle = rest.astype(BF).astype(F32)
    parts[0:HEADS, :] = high
    parts[8 : 8 + HEADS, :] = middle
    parts[16 : 16 + HEADS, :] = rest - middle
    split = parts[...].astype(BF)
    row_label = labels[pl.ds(z, 1), :]
    col_label = jnp.sum(jnp.where(iota((CELLS, GROUP), 1) == z, labels_t[...], 0), axis=1, keepdims=True)
    mask[...] = jnp.where(row_label == col_label, 0.0, MASK_FILL)
    sides = []
    for c in (FAR, 0):
        rows = []
        for r in (FAR, 0):
            found = dot(split, entry_hits(offset, r * WIN + c))
            rows.append((found[0:8] + found[8:16]) + found[16:24])
        sides.append(
            jnp.concatenate([rows[0], rows[1][:, WIN:], jnp.zeros((8, STRIP - CELLS - SPAN), F32)], axis=1)
        )
    col = lane_col()
    for c in range(WIN):
        near = pltpu.roll(sides[0], (STRIP - (FAR - c)) % STRIP, 1)
        far = pltpu.roll(sides[1], c, 1)
        strips[c] = jnp.where(col <= c, near, far)
    for h in range(HEADS):
        strip = strips[:, h, :]
        for r in range(WIN):
            begin = (FAR - r) * WIN
            out[r * WIN : (r + 1) * WIN, h * CELLS : (h + 1) * CELLS] = (
                strip[:, begin : begin + CELLS] + mask[r * WIN : (r + 1) * WIN, :]
            )
    out[:, HEADS * CELLS :] = jnp.zeros((CELLS, STACK - HEADS * CELLS), F32)


def table_sums(grads, offset, strips, wide):
    for h in range(HEADS):
        wide[h] = jnp.zeros(wide.shape[1:], F32)
        for r in range(WIN):
            begin = (FAR - r) * WIN
            wide[h, :, begin : begin + CELLS] += grads[r * WIN : (r + 1) * WIN, h * CELLS : (h + 1) * CELLS]
        strips[:, h, :] = wide[h]
    col = lane_col()
    zero = jnp.zeros((8, STRIP), F32)
    near = far = zero
    for c in range(WIN):
        strip = strips[c]
        near = near + pltpu.roll(jnp.where(col <= c, strip, zero), FAR - c, 1)
        far = far + pltpu.roll(jnp.where(col <= c, zero, strip), (STRIP - c) % STRIP, 1)
    total = None
    for c, side in ((FAR, near), (0, far)):
        upper = side[:, 0:CELLS]
        lower = jnp.concatenate([jnp.zeros((8, WIN), F32), side[:, CELLS : CELLS + SPAN]], axis=1)
        for r, piece in ((FAR, upper), (0, lower)):
            high = piece.astype(BF).astype(F32)
            both = jnp.concatenate([high, piece - high], axis=0).astype(BF)
            found = dot_nt(both, entry_hits(offset, r * WIN + c))
            total = found if total is None else total + found
    return total[0:8] + total[8:16]


def norm_stats(values):
    centre = jnp.mean(values, axis=-1, keepdims=True)
    moved = values - centre
    inverse = lax.rsqrt(jnp.mean(moved * moved, axis=-1, keepdims=True) + NORM_EPS)
    return moved * inverse, inverse


def turned(block):
    return block.astype(F32).T.astype(BF)


def stack_heads(block, lane_head, out):
    for h in range(HEADS):
        out[h * CELLS : (h + 1) * CELLS, :] = jnp.where(lane_head == h, block, jnp.zeros_like(block))
    out[HEADS * CELLS :, :] = jnp.zeros((STACK - HEADS * CELLS, BLOCK), BF)


def pick_heads(wide, held):
    for h in range(HEADS):
        lines = slice(h * HEAD_DIM, (h + 1) * HEAD_DIM)
        held[lines, :] = wide[lines, h * CELLS : (h + 1) * CELLS]
    return held[...].T


def attend_kernel(ids, *refs):
    pieces = refs[0:2]
    vectors, weights, head_bias, bias, out_weight = refs[2:7]
    tokens, normed, queries, keys, values, probs, attended = refs[7:14]
    stacked, held = refs[14:16]
    gain = vectors[0:1, :]
    shift = vectors[1:2, :]
    for j in range(GROUP):
        tokens[j * CELLS : (j + 1) * CELLS, :] = pieces[j & 1][j >> 1, 0:CELLS, :]

    @pl.loop(0, GROUP)
    def _(w):
        rows = pl.ds(aligned(w * CELLS, 16), CELLS)
        scaled, _ = norm_stats(tokens[rows, :].astype(F32))
        normed[rows, :] = (scaled * gain + shift).astype(BF)

    scale = float(HEAD_DIM) ** (-0.5)
    whole = normed[...]
    queries[...] = ((dot(whole, weights[0]) + head_bias[0:1, :]) * scale).astype(BF)
    keys[...] = dot(whole, weights[1]).astype(BF)
    values[...] = (dot(whole, weights[2]) + head_bias[1:2, :]).astype(BF)
    lane_head = iota((CELLS, BLOCK), 1) // HEAD_DIM
    for w in range(GROUP):
        rows = pl.ds(w * CELLS, CELLS)
        key = keys[rows, :]
        stack_heads(queries[rows, :], lane_head, stacked.at[w])
        for begin, count in CHUNKS:
            scores = dot_nt(key, stacked[w, begin : begin + count, :]) + bias[:, begin : begin + count]
            powers = jnp.exp(scores - jnp.max(scores, axis=0, keepdims=True))
            share = powers * (1.0 / jnp.sum(powers, axis=0, keepdims=True))
            probs[w, :, begin : begin + count] = share.astype(BF)
        total = pick_heads(dot(turned(values[rows, :]), probs[w]), held.at[w])
        attended[(w & 1) * CELLS : (w & 1) * CELLS + CELLS, (w >> 1) * BLOCK : (w >> 1) * BLOCK + BLOCK] = (
            total.astype(BF)
        )
    for k in range(2):
        attended[ATT + k * BLOCK : ATT + (k + 1) * BLOCK, :] = out_weight[:, k * HALF : (k + 1) * HALF]


def expand_kernel(ids, *refs):
    tokens = refs[0]
    attended = refs[1:3]
    vectors, weights, hidden_bias = refs[3:6]
    middle, normed, hidden, slope = refs[6:10]
    joined, square = refs[10:12]
    for j in range(GROUP):
        source = attended[j & 1]
        for k in range(2):
            square[j * BLOCK : (j + 1) * BLOCK, k * HALF : (k + 1) * HALF] = source[
                j >> 1, ATT + k * BLOCK : ATT + (k + 1) * BLOCK, :
            ]
        for i in range(GROUP):
            k = i ^ j
            joined[i * CELLS : (i + 1) * CELLS, j * BLOCK : (j + 1) * BLOCK] = source[
                j >> 1, (k & 1) * CELLS : (k & 1) * CELLS + CELLS, (k >> 1) * BLOCK : (k >> 1) * BLOCK + BLOCK
            ]
    out_bias = vectors[2:3, :]
    gain = vectors[3:4, :]
    shift = vectors[4:5, :]

    @pl.loop(0, 2)
    def _(t):
        rows = pl.ds(aligned(t * (TOKENS // 2), 16), TOKENS // 2)
        mid = tokens[rows, :].astype(F32) + dot(joined[rows, :], square[...]) + out_bias
        middle[rows, :] = mid
        scaled, _ = norm_stats(mid)
        second = (scaled * gain + shift).astype(BF)
        normed[rows, :] = second
        pre = dot(second, weights[...]) + hidden_bias[...]
        bell = 0.5 * (1.0 + lax.erf(pre * ROOT_HALF))
        hidden[rows, :] = (pre * bell).astype(BF)
        slope[rows, :] = bell + pre * (ROOT_TWO_PI_INV * jnp.exp(-0.5 * pre * pre))


def split_slots(product, keep, send):
    keep[0:CELLS, :] = product[0:CELLS].astype(keep.dtype)
    keep[CELLS:, :] = product[2 * CELLS : 3 * CELLS].astype(keep.dtype)
    send[0:CELLS, :] = product[CELLS : 2 * CELLS].astype(send.dtype)
    send[CELLS:, :] = product[3 * CELLS :].astype(send.dtype)


def hidden_back_kernel(ids, u0, u1, contract, slope, expand, upstream, pre_grad, keep, send):
    for j in range(GROUP):
        upstream[j * CELLS : (j + 1) * CELLS, :] = (u0, u1)[j & 1][j >> 1, CELLS:, :]
    pre_grad[...] = (dot_nt(upstream[...], contract[...]) * slope[...]).astype(BF)
    split_slots(dot_nt(pre_grad[...], expand[...]), keep, send)


def contract_grads_kernel(ids, u0, u1, hidden, o0, o1, o2, o3, upstream):
    for j in range(GROUP):
        upstream[j * CELLS : (j + 1) * CELLS, :] = (u0, u1)[j & 1][j >> 1, CELLS:, :]
    up = upstream[...]
    for q in range(2):
        block = dot_tn(hidden[:, q * HALF : (q + 1) * HALF], up).astype(BF)
        for s, out in enumerate((o0, o1, o2, o3)):
            out[:, q * BLOCK : (q + 1) * BLOCK] = block[:, s * BLOCK : (s + 1) * BLOCK]


def expand_grads_kernel(
    ids, upstream, hidden, normed, pre_grad, contract, keep, send, keep_out, send_out, sums, whole_e,
):
    x = ids[0]
    mixed = dot_tn(normed[...], pre_grad[...]).astype(BF)
    whole_e[...] = dot_nt(mixed, hidden_perm()).astype(BF)
    lines = BLOCK // 2
    for s in range(GROUP):
        for out, side in ((keep, x), (send, 1 - x)):
            out[s] = whole_e[pl.ds(aligned(s * BLOCK + side * lines, 16), lines), :]
    split_slots(dot(hidden[...], contract[...]), keep_out, send_out)
    sums[...] = jnp.zeros(sums.shape, F32)
    sums[0:1, :] = jnp.sum(pre_grad[...].astype(F32), axis=0, keepdims=True)
    sums[1:2, :] = jnp.sum(upstream[0:CELLS, :].astype(F32), axis=0, keepdims=True)


def attend_back_kernel(ids, *refs):
    even_total, odd_total, middle, upstream = refs[0:4]
    vectors, out_weights, queries, keys, values, probs, weights = refs[4:11]
    own_mid, mid_low, joined, bias_grad, keep, send, sums = refs[11:18]
    attended_grad, stacked, stacked_grad, scores, held = refs[18:23]
    gain = vectors[3:4, :]
    sums[...] = jnp.zeros(sums.shape, F32)
    for w in range(GROUP):
        rows = pl.ds(w * CELLS, CELLS)
        source = (even_total, odd_total)[w & 1]
        grad = source[(w >> 1) * CELLS : (w >> 1) * CELLS + CELLS, :].astype(F32)
        scaled, inverse = norm_stats(middle[rows, :])
        e = grad * gain
        part = e - jnp.mean(e, axis=-1, keepdims=True) - scaled * jnp.mean(e * scaled, axis=-1, keepdims=True)
        mid = upstream[rows, :].astype(F32) + inverse * part
        low = mid.astype(BF)
        mid_low[rows, :] = low
        if w == 0:
            own_mid[...] = mid
            sums[0:1, :] = jnp.sum(low.astype(F32), axis=0, keepdims=True)
            sums[1:2, :] = jnp.sum(grad * scaled, axis=0, keepdims=True)
            sums[2:3, :] = jnp.sum(grad, axis=0, keepdims=True)
    attended_grad[...] = dot_nt(mid_low[...], out_weights[...]).astype(BF)
    lane_head = iota((CELLS, BLOCK), 1) // HEAD_DIM
    scale = float(HEAD_DIM) ** (-0.5)
    for w in range(GROUP):
        rows = pl.ds(w * CELLS, CELLS)
        key = keys[rows, :]
        value = values[rows, :]
        stack_heads(queries[rows, :], lane_head, stacked.at[w])
        stack_heads(attended_grad[rows, :], lane_head, stacked_grad.at[w])
        for begin, count in CHUNKS:
            lanes = slice(begin, begin + count)
            share = probs[w, :, lanes].astype(F32)
            product = share * dot_nt(value, stacked_grad[w, lanes, :])
            score = (product - share * jnp.sum(product, axis=0, keepdims=True)).astype(BF)
            scores[w, :, lanes] = score
            if w == 0:
                bias_grad[:, lanes] = score.astype(F32)
            else:
                bias_grad[:, lanes] += score.astype(F32)
        value_grad = dot(probs[w], stacked_grad[w])
        key_grad = dot(scores[w], stacked[w])
        query_grad = pick_heads(dot(turned(key), scores[w]), held.at[w])
        joined[0, rows, :] = (query_grad * scale).astype(BF)
        joined[1, rows, :] = key_grad.astype(BF)
        joined[2, rows, :] = value_grad.astype(BF)
    product = dot_nt(joined[0], weights[0]) + dot_nt(joined[1], weights[1]) + dot_nt(joined[2], weights[2])
    split_slots(product, keep, send)


SMALL = 16


def joined_grads_kernel(
    ids, normed, joined, attended, mid_low, tokens, keep_in, send_in, hidden_sums, mid_sums,
    bias_grad, offset, keep, send, row_sums, whole_q, whole_o, small, small_low, strips, strip_sums,
):
    x = ids[0]
    whole = normed[...]
    picks = pair_picks(BLOCK)
    for part in range(3):
        natural = dot_tn(whole, joined[part]).astype(BF)
        for s in range(GROUP):
            for q in range(2):
                whole_q[part, s * (BLOCK // 2) : (s + 1) * (BLOCK // 2), q * BLOCK : (q + 1) * BLOCK] = dot_tn(
                    picks[q], natural[s * BLOCK : (s + 1) * BLOCK]
                ).astype(BF)
    low = mid_low[...]
    total = None
    for k in range(2):
        left = attended[0:ATT, k * BLOCK : (k + 1) * BLOCK]
        product = dot_tn(left, low[2 * k * CELLS : (2 * k + 2) * CELLS])
        total = product if total is None else total + product
    wide = total.astype(BF)
    for q in range(2):
        lines = dot_tn(picks[q], wide).astype(BF)
        for s in range(GROUP):
            whole_o[s, :, q * BLOCK : (q + 1) * BLOCK] = lines[:, s * BLOCK : (s + 1) * BLOCK]
    gains = shifts = None
    for w in range(GROUP):
        source = (keep_in, send_in)[w & 1]
        grad = source[(w >> 1) * CELLS : (w >> 1) * CELLS + CELLS, :].astype(F32)
        scaled, _ = norm_stats(tokens[w * CELLS : (w + 1) * CELLS, :].astype(F32))
        more_gains = jnp.sum(grad * scaled, axis=0, keepdims=True)
        more_shifts = jnp.sum(grad, axis=0, keepdims=True)
        gains = more_gains if gains is None else gains + more_gains
        shifts = more_shifts if shifts is None else shifts + more_shifts
    small[...] = jnp.zeros(small.shape, F32)
    table = table_sums(bias_grad, offset, strips, strip_sums)
    for s in range(GROUP):
        small[s, 0:1, :] = hidden_sums[0:1, :HALF]
        small[s, 1:2, :] = hidden_sums[0:1, HALF:]
        for part in range(3):
            small[s, 2 + part : 3 + part, 0:BLOCK] = jnp.sum(joined[part].astype(F32), axis=0, keepdims=True)
        small[s, 5 : 5 + HEADS, :] = table[0:HEADS, 0:HALF]
        small[s, 11 : 11 + HEADS, 0 : REL - HALF] = table[0:HEADS, HALF:REL]
    row_sums[...] = jnp.zeros(row_sums.shape, F32)
    row_sums[0:1, :] = hidden_sums[1:2, :]
    row_sums[1:4, :] = mid_sums[0:3, :]
    row_sums[4:5, :] = gains
    row_sums[5:6, :] = shifts
    small_low[...] = small[...].astype(BF)
    rows = BLOCK // 4
    for s in range(GROUP):
        begin = s * (BLOCK // 2)
        for out, side in ((keep, x), (send, 1 - x)):
            for part in range(3):
                out[s, part * rows : (part + 1) * rows, :] = whole_q[part, pl.ds(aligned(begin + side * rows, 16), rows), :]
            out[s, 3 * rows : 4 * rows, :] = whole_o[s, pl.ds(aligned(side * rows, 16), rows), :]
            out[s, 4 * rows :, :] = small_low[s, pl.ds(aligned(side * SMALL, 16), SMALL), :]


EXTRA = 80


def window_lines(result, s, held):
    lanes = slice(s * BLOCK, (s + 1) * BLOCK)
    held[s, 0:LINES, :BLOCK] = result[0:LINES, lanes]
    held[s, 0:LINES, BLOCK:] = result[LINES:, lanes]
    held[s, LINES:, :] = jnp.zeros((EXTRA - LINES, HALF), F32)


def window_piece(lines):
    whole = lines.astype(F32)
    return jnp.concatenate([whole[0:LINES, :BLOCK], whole[0:LINES, BLOCK:]], axis=0).astype(BF)


def expand_pack_kernel(ids, keep, came, middle, pair, came_out, vectors, o0, o1, o2, o3, held):
    total = pair[0:CELLS, :].astype(F32) + came_out[...].astype(F32)
    result = middle[0:CELLS, :] + total + vectors[5:6, :]
    lines = BLOCK // 2
    for s, out in enumerate((o0, o1, o2, o3)):
        both = keep[s].astype(F32) + came[s].astype(F32)
        out[0:lines, :] = both[:, :HALF].astype(BF)
        out[lines : 2 * lines, :] = both[:, HALF:].astype(BF)
        window_lines(result, s, held)
        out[2 * lines :, :] = held[s].astype(BF)


def row_sum_kernel(ids, mine, other, out):
    out[...] = mine[...] + other[...]


def joined_pack_kernel(ids, keep, came, pair, came_in, tokens, own_mid, vectors, row_sums, row_came, o0, o1, o2, o3, held):
    total = pair[0:CELLS, :].astype(F32) + came_in[...].astype(F32)
    scaled, inverse = norm_stats(tokens[0:CELLS, :].astype(F32))
    e = total * vectors[0:1, :]
    part = e - jnp.mean(e, axis=-1, keepdims=True) - scaled * jnp.mean(e * scaled, axis=-1, keepdims=True)
    result = own_mid[...] + inverse * part
    totals = row_sums[...] + row_came[...]
    rows = keep.shape[1]
    for s, out in enumerate((o0, o1, o2, o3)):
        out[0:rows, :] = (keep[s].astype(F32) + came[s].astype(F32)).astype(BF)
        window_lines(result, s, held)
        held[s, LINES:, :BLOCK] = totals[:, s * BLOCK : (s + 1) * BLOCK]
        out[rows:, :] = held[s].astype(BF)


def ordered_sum(ids, pieces, rows, held):
    z = ids[1]
    for s, piece in enumerate(pieces):
        held[(z + s) % GROUP] = piece[0:rows, :]
    return (
        ((held[0].astype(F32) + held[1].astype(F32)) + held[2].astype(F32)) + held[3].astype(F32)
    ).astype(BF)


def ordered_sum_kernel(ids, a, b, c, d, out, held):
    out[...] = ordered_sum(ids, (a, b, c, d), out.shape[0], held)


def joined_sum_kernel(ids, a, b, c, d, out, held, lines):
    rows = held.shape[1]
    pieces = (a, b, c, d)
    out[0:rows, :] = ordered_sum(ids, pieces, rows, held)
    for s, piece in enumerate(pieces):
        lines[(ids[1] + s) % GROUP] = piece[rows + EXTRA - 16 :, :].astype(F32)
    out[rows:, :] = (((lines[0] + lines[1]) + lines[2]) + lines[3]).astype(BF)


def expand_sum_kernel(ids, mine_c, a, b, c, d, out, held):
    out[0:HALF, :] = mine_c[...]
    out[HALF:, :] = ordered_sum(ids, (a, b, c, d), BLOCK, held)


def half_sum_kernel(ids, keep, came, out):
    out[...] = (keep[...] + came[...].astype(F32)).astype(BF)


def cross_sum_kernel(ids, kept, came, out):
    for k in range(2):
        mine = slice(k * CELLS, (k + 1) * CELLS)
        theirs = slice((1 - k) * CELLS, (2 - k) * CELLS)
        out[mine, :] = (kept[mine, :].astype(F32) + came[theirs, :].astype(F32)).astype(BF)


def wide_store(out, piece, begin, step, offset):
    count = piece.shape[0]
    for k in range(3):
        out[pl.ds(begin * step + offset + k, count, stride=step), :] = piece[:, k * 128 : (k + 1) * 128]


def finish_hidden_kernel(ids, mine, other, out_c, out_e):
    x = ids[0]
    wide_store(out_c, mine[0:HALF, :].astype(F32) + other[0:HALF, :].astype(F32), 0, 3, 0)
    lines = BLOCK // 2
    for piece, side in ((mine, x), (other, 1 - x)):
        for k in range(2):
            out_e[pl.ds(aligned(side * lines, 8), lines), k * HALF : (k + 1) * HALF] = piece[
                HALF + k * lines : HALF + (k + 1) * lines, :
            ].astype(F32)


def finish_joined_kernel(ids, mine, other, out_q, out_o, out_hidden, out_heads, out_table, r0, r1, r2, r3, r4, r5, small, line):
    x = ids[0]
    for piece, side in ((mine, x), (other, 1 - x)):
        for part in range(3):
            wide_store(out_q, piece[part * QUARTER : (part + 1) * QUARTER, :].astype(F32), side * QUARTER, 9, part * 3)
        wide_store(out_o, piece[3 * QUARTER : 4 * QUARTER, :].astype(F32), side * QUARTER, 3, 0)
        small[pl.ds(aligned(side * SMALL, 8), SMALL), :] = piece[4 * QUARTER : 4 * QUARTER + SMALL, :].astype(F32)
    line[...] = jnp.zeros(line.shape, F32)
    line[0:1, :HALF] = small[0:1, :]
    line[0:1, HALF:] = small[1:2, :]
    out_hidden[...] = dot_nt(line[...].astype(BF), hidden_perm())[0:1]
    out_heads[0:1, :] = small[2:3, :BLOCK]
    out_heads[1:2, :] = small[4:5, :BLOCK]
    out_table[:, :HALF] = small[5 : 5 + HEADS, :]
    out_table[:, HALF:] = small[11 : 11 + HEADS, 0 : REL - HALF]
    ends = []
    for piece in (mine, other):
        ends.append(piece[4 * QUARTER + SMALL :, :BLOCK].astype(F32)[8:16])
    total = ends[0] + ends[1]
    for n, out in enumerate((r0, r1, r2, r3, r4, r5)):
        out[...] = total[n : n + 1]


CHEAP = (attend_kernel, expand_weights_kernel, ordered_sum_kernel, expand_pack_kernel)


def local_program(dp_size, row_size, col_size):
    def turn(value, shift):
        return lax.ppermute(value, "row", [(i, (i + shift) % row_size) for i in range(row_size)])

    def flip(value, bits):
        return lax.ppermute(value, "col", [(i, i ^ bits) for i in range(col_size)])

    def swap(value, bits=1):
        return lax.ppermute(value, "dp", [(i, i ^ bits) for i in range(dp_size)])

    def swap_rest(value):
        bits = 2
        while bits < dp_size:
            value = (value.astype(F32) + swap(value, bits).astype(F32)).astype(value.dtype)
            bits *= 2
        return value

    def turn_all(value):
        return [turn(value, s) for s in range(1, row_size)]

    def give_back(slots):
        return [slots[0]] + [turn(slots[s], -s) for s in range(1, row_size)]

    def local(
        inputs, cotangent, slot_mask, region_ids, offset_index, first_gain, first_shift,
        query_key_value, query_value_bias, position_table, output_weight, output_bias,
        second_gain, second_shift, expand_weight, expand_bias, contract_weight, contract_bias,
    ):
        joined_own = query_key_value.reshape(BLOCK // 2, 3, HALF).transpose(1, 0, 2)
        out_own = output_weight.reshape(BLOCK // 2, HALF)
        contract_own = contract_weight.reshape(HALF, HALF)
        vector_own = jnp.stack([first_gain, first_shift, output_bias, second_gain, second_shift, contract_bias])
        last = []

        def step(kernel, outs, scratch, *arrays, **given):
            results = run(kernel, outs, scratch, *arrays, after=tuple(last), **given)
            last[:] = [results[-1]]
            return results[:-1]

        v = types.SimpleNamespace()
        two = (2 * CELLS, WIDTH)
        wide = (TOKENS, WIDTH)
        rows_j = BLOCK + SMALL

        def stage_order():
            slots = step(
                order_kernel, [((FIRST + BLOCK, HALF), BF)] * GROUP, [((GROUP, FIRST, HALF), F32)],
                vector_own, inputs.reshape(2 * CELLS, HALF), cotangent.reshape(2 * CELLS, HALF),
                joined_own, out_own, mib=ORDER_MIB,
            )
            v.slots = [slots[0]] + [turn(slots[s], s) for s in range(1, row_size)]

        def stage_bias():
            labels = region_ids.reshape(2, WIN, 2, WIN).transpose(0, 2, 1, 3).reshape(GROUP, CELLS)
            (v.bias,) = step(
                bias_kernel, [((CELLS, STACK), F32)],
                [((24, REL), F32), ((WIN, 8, STRIP), F32), ((CELLS, CELLS), F32)],
                position_table.T, offset_index.T, labels, labels.T,
            )

        def stage_unpack():
            v.own, v.vectors, v.first = step(
                unpack_kernel, [(two, BF), ((8, WIDTH), F32), ((3, BLOCK, HALF), BF)], [],
                *v.slots, scalars=(slot_mask,),
            )
            v.first_other = swap(v.first)
            v.across = flip(v.own, 2)

        def stage_half():
            (half,) = step(half_kernel, [((BLOCK // 2, WIDTH), BF)], [], expand_weight)
            v.expand_mine = turn_all(half)

        def stage_stack():
            (v.expand,) = step(stack_kernel, [((3, BLOCK // 2, WIDTH), BF)], [], *v.expand_mine)
            v.expand_other = swap(v.expand)

        def stage_couple():
            (both,) = step(couple_kernel, [((2, *two), BF)], [], v.own, v.across)
            v.tokens = (both, flip(both, 1))

        def stage_first():
            v.joined_w, v.out_w = step(
                first_weights_kernel, [((3, WIDTH, BLOCK), BF), ((BLOCK, WIDTH), BF)],
                [((GROUP, 4, BLOCK // 2, HALF), BF)], joined_own, out_own, v.first, v.first_other,
            )

        def stage_pass():
            (passed,) = step(pass_kernel, [((HALF, HALF), BF)], [], contract_own)
            v.contract = turn_all(passed)

        def stage_attend():
            v.x, v.n1, v.q, v.k, v.v, v.p, v.att = step(
                attend_kernel,
                [(wide, BF)] * 2 + [((TOKENS, BLOCK), BF)] * 3
                + [((GROUP, CELLS, STACK), BF), ((ATT + HALF, HALF), BF)],
                [((GROUP, STACK, BLOCK), BF), ((GROUP, BLOCK, CELLS), F32)], *v.tokens, v.vectors, v.joined_w, query_value_bias, v.bias, v.out_w,
            )
            v.att_across = flip(v.att, 2)

        def stage_expand_w():
            v.expand_w, v.hidden_bias = step(
                expand_weights_kernel, [((WIDTH, WIDTH), BF), ((1, WIDTH), F32)],
                [((GROUP, BLOCK, WIDTH), BF), ((8, WIDTH), F32)],
                expand_weight, v.expand, v.expand_other, expand_bias.reshape(1, WIDTH),
            )

        def stage_couple_att():
            (both,) = step(couple_kernel, [((2, ATT + HALF, HALF), BF)], [], v.att, v.att_across)
            v.attended = (both, flip(both, 1))

        def stage_expand():
            v.middle, v.n2, v.hidden, v.slope = step(
                expand_kernel, [(wide, F32), (wide, BF), (wide, BF), (wide, F32)],
                [(wide, BF), ((WIDTH, WIDTH), BF)],
                v.x, *v.attended, v.vectors, v.expand_w, v.hidden_bias,
            )

        def stage_contract_g():
            parts = step(
                contract_grads_kernel, [((HALF, HALF), BF)] * GROUP, [(wide, BF)], *v.tokens, v.hidden
            )
            v.parts_c = give_back(parts)

        def stage_contract_w():
            (v.contract_w,) = step(
                contract_weights_kernel, [((WIDTH, WIDTH), BF)], [], contract_own, *v.contract
            )

        def stage_hidden():
            v.up, v.pre, v.keep_n, send = step(
                hidden_back_kernel, [(wide, BF)] * 2 + [(two, F32), (two, BF)], [],
                *v.tokens, v.contract_w, v.slope, v.expand_w,
            )
            v.came_n = flip(send, 1)

        def stage_half_sum():
            (v.even,) = step(half_sum_kernel, [(two, BF)], [], v.keep_n, v.came_n)
            v.even_came = flip(v.even, 2)

        def stage_expand_g():
            v.keep_e, send_e, v.keep_out, send_out, v.hidden_sums = step(
                expand_grads_kernel,
                [((GROUP, BLOCK // 2, WIDTH), BF)] * 2 + [(two, F32), (two, BF), ((8, WIDTH), F32)],
                [((WIDTH, WIDTH), BF)],
                v.up, v.hidden, v.n2, v.pre, v.contract_w,
            )
            v.came_e = swap(send_e)
            v.came_out = flip(send_out, 1)

        def stage_cross():
            (v.even_total,) = step(cross_sum_kernel, [(two, BF)], [], v.even, v.even_came)
            v.odd_total = flip(v.even_total, 1)

        def stage_out_sum():
            (v.pair_out,) = step(half_sum_kernel, [(two, BF)], [], v.keep_out, v.came_out)
            v.far_out = flip(v.pair_out[CELLS:], 2)

        def stage_attend_b():
            v.own_mid, v.mid_low, v.joined_g, v.bias_g, v.keep_i, send, v.mid_sums = step(
                attend_back_kernel,
                [((CELLS, WIDTH), F32), (wide, BF), ((3, TOKENS, BLOCK), BF),
                 ((CELLS, STACK), F32), (two, F32), (two, BF), ((8, WIDTH), F32)],
                [((TOKENS, BLOCK), BF), ((GROUP, STACK, BLOCK), BF), ((GROUP, STACK, BLOCK), BF),
                 ((GROUP, CELLS, STACK), BF), ((GROUP, BLOCK, CELLS), F32)],
                v.even_total, v.odd_total, v.middle, v.up, v.vectors, v.out_w,
                v.q, v.k, v.v, v.p, v.joined_w,
            )
            v.send_i = send
            v.came_i = flip(send, 1)

        def stage_contract_s():
            (v.mine_c,) = step(
                ordered_sum_kernel, [((HALF, HALF), BF)], [((GROUP, HALF, HALF), BF)], *v.parts_c
            )

        def stage_expand_p():
            parts = step(
                expand_pack_kernel, [((BLOCK + EXTRA, HALF), BF)] * GROUP, [((GROUP, EXTRA, HALF), F32)],
                v.keep_e, v.came_e, v.middle, v.pair_out, v.far_out, v.vectors,
            )
            v.parts_e = give_back(parts)

        def stage_in_sum():
            (v.pair_in,) = step(half_sum_kernel, [(two, BF)], [], v.keep_i, v.came_i)
            v.far_in = flip(v.pair_in[CELLS:], 2)

        def stage_joined():
            v.keep_j, send, v.row_sums = step(
                joined_grads_kernel, [((GROUP, rows_j, HALF), BF)] * 2 + [((8, WIDTH), F32)],
                [((3, HALF, HALF), BF), ((GROUP, BLOCK // 2, HALF), BF),
                 ((GROUP, 2 * SMALL, HALF), F32), ((GROUP, 2 * SMALL, HALF), BF),
                 ((WIN, 8, STRIP), F32), ((HEADS, WIN, STRIP), F32)],
                v.n1, v.joined_g, v.att, v.mid_low, v.x, v.keep_i, v.send_i,
                v.hidden_sums, v.mid_sums, v.bias_g, offset_index.T,
            )
            v.came_j = swap(send)
            v.row_came = flip(v.row_sums, 1)

        def stage_rows():
            (v.row_pair,) = step(row_sum_kernel, [((8, WIDTH), F32)], [], v.row_sums, v.row_came)
            v.row_far = flip(v.row_pair, 2)

        def stage_expand_s():
            (mine,) = step(
                expand_sum_kernel, [((HALF + BLOCK, HALF), BF)], [((GROUP, BLOCK, HALF), BF)],
                v.mine_c, *v.parts_e,
            )
            v.mine_h = swap_rest(mine)
            v.other_h = swap(v.mine_h)

        def stage_joined_p():
            parts = step(
                joined_pack_kernel, [((rows_j + EXTRA, HALF), BF)] * GROUP, [((GROUP, EXTRA, HALF), F32)],
                v.keep_j, v.came_j, v.pair_in, v.far_in, v.x, v.own_mid, v.vectors,
                v.row_pair, v.row_far,
            )
            v.parts_j = give_back(parts)

        def stage_restore():
            (v.layer_output,) = step(restore_kernel, [((2 * CELLS, HALF), BF)], [], *v.parts_e)

        def stage_finish_h():
            v.out_c, v.out_e = step(
                finish_hidden_kernel, [((HALF * 3, 128), F32), ((BLOCK, WIDTH), F32)], [],
                v.mine_h, v.other_h,
            )

        def stage_joined_s():
            (mine,) = step(
                joined_sum_kernel, [((rows_j + 16, HALF), BF)],
                [((GROUP, rows_j, HALF), BF), ((GROUP, 16, HALF), F32)], *v.parts_j
            )
            v.mine_j = swap_rest(mine)
            v.other_j = swap(v.mine_j)

        def stage_restore_w():
            (v.input_gradient,) = step(
                restore_wide_kernel, [((6 * CELLS, 128), F32)], [((2 * CELLS, HALF), F32)], *v.parts_j
            )

        def stage_finish_j():
            v.out_q, v.out_o, v.out_hidden, v.out_heads, v.out_table, *v.rows = step(
                finish_joined_kernel,
                [((BLOCK // 2 * 9, 128), F32), ((BLOCK // 2 * 3, 128), F32), ((1, WIDTH), F32),
                 ((2, BLOCK), F32), ((HEADS, REL), F32)] + [((1, BLOCK), F32)] * 6,
                [((2 * SMALL, HALF), F32), ((8, WIDTH), F32)],
                v.mine_j, v.other_j,
            )

        stage_order()
        stage_bias()
        stage_unpack()
        stage_half()
        stage_stack()
        stage_pass()
        stage_couple()
        stage_first()
        stage_attend()
        stage_expand_w()
        stage_contract_w()
        stage_couple_att()
        stage_expand()
        stage_contract_g()
        stage_hidden()
        stage_half_sum()
        stage_expand_g()
        stage_cross()
        stage_out_sum()
        stage_attend_b()
        stage_joined()
        stage_contract_s()
        stage_expand_p()
        stage_in_sum()
        stage_rows()
        stage_expand_s()
        stage_joined_p()
        stage_restore()
        stage_finish_h()
        stage_joined_s()
        stage_restore_w()
        stage_finish_j()
        rows = [row.reshape(BLOCK) for row in v.rows]
        return (
            v.layer_output.reshape(inputs.shape),
            v.input_gradient.reshape(inputs.shape),
            rows[4],
            rows[5],
            v.out_q.reshape(query_key_value.shape),
            v.out_heads,
            v.out_table.T,
            v.out_o.reshape(output_weight.shape),
            rows[1],
            rows[2],
            rows[3],
            v.out_e,
            v.out_hidden.reshape(WIDTH),
            v.out_c.reshape(contract_weight.shape),
            rows[0],
        )

    return local


def solution(mesh):
    in_specs = (
        P(("dp", "col"), "row", None),
        P(("dp", "col"), "row", None),
        P(),
        P(),
        P(),
        P("row"),
        P("row"),
        P("row", None, "col", None),
        P(None, "col"),
        P(None, "col"),
        P("col", "row", None),
        P("row"),
        P("row"),
        P("row"),
        P("row", "col"),
        P("col"),
        P("col", "row", None),
        P("row"),
    )
    out_specs = (
        P(("dp", "col"), "row", None),
        P(("dp", "col"), "row", None),
        P("row"),
        P("row"),
        P("row", None, "col", None),
        P(None, "col"),
        P(None, "col"),
        P("col", "row", None),
        P("row"),
        P("row"),
        P("row"),
        P("row", "col"),
        P("col"),
        P("col", "row", None),
        P("row"),
    )
    local = local_program(mesh.shape["dp"], mesh.shape["row"], mesh.shape["col"])
    return jax.shard_map(local, mesh=mesh, in_specs=in_specs, out_specs=out_specs, check_vma=False)
```

profile of v0, /device:TPU:0, one launch (start us, length us, event | category | flops | bytes accessed | tf_op | source)
XLA Modules:
  0.0 170.2 jit_solution(129630240782019714)
XLA Ops:
  0.6 1.4 stack.27.refs_0_
  2.0 3.7 %order_kernel.1 = (bf16[352,384]{1,0:T(8,128)(2,1)}, bf16[352,384]{1,0:T(8,128)(2,1)}, bf16[352,384]{1,0:T(8,128)(2,1)}, bf16[352,384]{1,0:T(8,128)(2,1)}, f32[8,128]{1,0:T(8,128)}) custom-call(f32[6,192]{1,0:T(8,128)} %stack.27.refs_0_, bf16[288,384]{1,0:T(8,128)(2,1)} %bitcast.48, bf16[288,384]{1,0:T(8,128)(2,1)} %bitcast.49, ...), custom_call_target="tpu_custom_call" | custom-call | flops 11000000512 | bytes 36000000 | tf_op jit(solution)/shard_map/order_kernel/pallas_call | solution.py:75
  5.7 3.0 %collective-permute-start = (bf16[352,384]{1,0:T(8,128)(2,1)}, bf16[352,384]{1,0:T(8,128)(2,1)S(1)}, u32[]{:S(2)}, u32[]{:S(2)}) collective-permute-start(bf16[352,384]{1,0:T(8,128)(2,1)} %get-tuple-element.130), channel_id=1, source_target_pairs={{0,4},{4,8},{8,12},{12,0},{1,5},{5,9},{9,13},{13,1},{2,6},{6,10},{... | collective-permute-start | bytes 811016 | tf_op jit(solution)/shard_map/ppermute | solution.py:730
  8.7 2.6 %collective-permute-start.1 = (bf16[352,384]{1,0:T(8,128)(2,1)}, bf16[352,384]{1,0:T(8,128)(2,1)S(1)}, u32[]{:S(2)}, u32[]{:S(2)}) collective-permute-start(bf16[352,384]{1,0:T(8,128)(2,1)} %get-tuple-element.131), channel_id=1, source_target_pairs={{0,8},{4,12},{8,0},{12,4},{1,9},{5,13},{9,1},{13,5},{2,10},{6,14},... | collective-permute-start | bytes 811016 | tf_op jit(solution)/shard_map/ppermute | solution.py:730
  11.3 1.4 collective-permute-start.2
  13.8 1.9 %bias_kernel.1 = (f32[144,896]{1,0:T(8,128)S(1)}, f32[8,128]{1,0:T(8,128)S(1)}) custom-call(f32[6,529]{1,0:T(8,128)S(1)} %bitcast.40, s32[144,144]{1,0:T(8,128)S(1)} %bitcast.31, s32[4,144]{1,0:T(4,128)S(1)} %reshape.95.refs_2_, s32[144,4]{1,0:T(8,128)S(1)} %bitcast.33, f32[8,128]{1,0:T(8,128)S(1)} %copy-done.8), custom_call_target="tpu_custom_call" | custom-call | flops 11000000512 | bytes 36000000 | tf_op jit(solution)/shard_map/bias_kernel/pallas_call | solution.py:75
  15.7 2.7 %collective-permute-done.refs_2_ = bf16[352,384]{1,0:T(8,128)(2,1)S(1)} collective-permute-done((bf16[352,384]{1,0:T(8,128)(2,1)}, bf16[352,384]{1,0:T(8,128)(2,1)S(1)}, u32[]{:S(2)}, u32[]{:S(2)}) %collective-permute-start) | collective-permute-done | bytes 270368 | tf_op jit(solution)/shard_map/ppermute | solution.py:730
  18.4 10.8 %collective-permute-done.1.refs_3_ = bf16[352,384]{1,0:T(8,128)(2,1)S(1)} collective-permute-done((bf16[352,384]{1,0:T(8,128)(2,1)}, bf16[352,384]{1,0:T(8,128)(2,1)S(1)}, u32[]{:S(2)}, u32[]{:S(2)}) %collective-permute-start.1) | collective-permute-done | bytes 270368 | tf_op jit(solution)/shard_map/ppermute | solution.py:730
  30.2 7.3 %collective-permute-start.6 = (bf16[96,768]{1,0:T(8,128)(2,1)S(1)}, bf16[96,768]{1,0:T(8,128)(2,1)S(1)}, u32[]{:S(2)}, u32[]{:S(2)}) collective-permute-start(bf16[96,768]{1,0:T(8,128)(2,1)S(1)} %get-tuple-element.137), channel_id=1, source_target_pairs={{0,12},{4,0},{8,4},{12,8},{1,13},{5,1},{9,5},{13,9},{2,14},{6,2},{... | collective-permute-start | bytes 442376 | tf_op jit(solution)/shard_map/ppermute | solution.py:730
  38.2 1.5 collective-permute-start.3
  39.7 1.5 collective-permute-start.12
  41.8 9.3 %collective-permute-done.5.refs_1_ = bf16[96,768]{1,0:T(8,128)(2,1)S(1)} collective-permute-done((bf16[96,768]{1,0:T(8,128)(2,1)S(1)}, bf16[96,768]{1,0:T(8,128)(2,1)S(1)}, u32[]{:S(2)}, u32[]{:S(2)}) %collective-permute-start.5) | collective-permute-done | bytes 147488 | tf_op jit(solution)/shard_map/ppermute | solution.py:730
  53.1 1.9 %collective-permute-start.8 = (bf16[384,384]{1,0:T(8,128)(2,1)S(1)}, bf16[384,384]{1,0:T(8,128)(2,1)S(1)}, u32[]{:S(2)}, u32[]{:S(2)}) collective-permute-start(bf16[384,384]{1,0:T(8,128)(2,1)S(1)} %get-tuple-element.142), channel_id=1, source_target_pairs={{0,4},{4,8},{8,12},{12,0},{1,5},{5,9},{9,13},{13,1},{2,6},{6,10},{... | collective-permute-start | bytes 884744 | tf_op jit(solution)/shard_map/ppermute | solution.py:730
  55.1 1.5 collective-permute-start.11
  57.6 1.1 first_weights_kernel.1
  59.1 3.9 %attend_kernel.1 = (bf16[576,768]{1,0:T(8,128)(2,1)S(1)}, bf16[576,768]{1,0:T(8,128)(2,1)S(1)}, bf16[576,192]{1,0:T(8,128)(2,1)S(1)}, bf16[576,192]{1,0:T(8,128)...) custom-call(bf16[2,288,768]{2,1,0:T(8,128)(2,1)S(1)} %get-tuple-elem, ...), custom_call_target="tpu_custom_call" | custom-call | flops 11000000 | bytes 36000 | tf_op jit(solution)/shard_map/attend_kernel/pallas_call | solution.py:75
  63.1 1.6 collective-permute-start.13
  64.7 1.0 collective-permute-done.11.refs_2_
  65.6 1.4 expand_weights_kernel.1
  67.1 11.5 %collective-permute-done.9.refs_2_ = bf16[384,384]{1,0:T(8,128)(2,1)S(1)} collective-permute-done((bf16[384,384]{1,0:T(8,128)(2,1)S(1)}, bf16[384,384]{1,0:T(8,128)(2,1)S(1)}, u32[]{:S(2)}, u32[]{:S(2)}) %collective-permute-start.9) | collective-permute-done | bytes 294944 | tf_op jit(solution)/shard_map/ppermute | solution.py:730
  79.0 2.6 %collective-permute-done.14.refs_2_ = bf16[2,672,384]{2,1,0:T(8,128)(2,1)S(1)} collective-permute-done((bf16[2,672,384]{2,1,0:T(8,128)(2,1)S(1)}, bf16[2,672,384]{2,1,0:T(8,128)(2,1)S(1)}, u32[]{:S(2)}, u32[]{:S(2)}) %collective-permute-start.14) | collective-permute-done | bytes 1032224 | tf_op jit(solution)/shard_map/ppermute | solution.py:733
  81.6 3.4 %expand_kernel.1 = (f32[576,768]{1,0:T(8,128)S(1)}, bf16[576,768]{1,0:T(8,128)(2,1)S(1)}, bf16[576,768]{1,0:T(8,128)(2,1)S(1)}, f32[576,768]{1,0:T(8,128)S(1)}, f32[8,128]{1,0:T(8,128)S(1)}) custom-call(bf16[576,768]{1,0:T(8,128)(2,1)S(1)} %get-tuple-element.154.refs_0_.refs_4_, bf16[2,672,384]{2,1,0:T(8,128)(2,1)S(1)} %get-tuple-element.157.refs_1_, ...), custom_call_target="tpu_custom_call" | custom-call | flops 11000000512 | bytes 36000000 | tf_op jit(solution)/shard_map/expand_kernel/pallas_call | solution.py:75
  85.0 1.2 contract_grads_kernel.1
  86.2 1.7 %hidden_back_kernel.1 = (bf16[576,768]{1,0:T(8,128)(2,1)S(1)}, bf16[576,768]{1,0:T(8,128)(2,1)S(1)}, f32[288,768]{1,0:T(8,128)S(1)}, bf16[288,768]{1,0:T(8,128)(2,1)S(1)}, f32[8,128]{1,0:T(8,128)S(1)}) custom-call(bf16[2,288,768]{2,1,0:T(8,128)(2,1)S(1)} %get-tuple-element.141.refs_0_, bf16[2,288,768]{2,1,0:T(8,128)(2,1)S(1)} %collective-permute-done.7.refs_1_, ...), custom_call_target="tpu_custom_call" | custom-call | flops 11000000512 | bytes 36000000 | tf_op jit(solution)/shard_map/hidden_back_kernel/pallas_call | solution.py:75
  88.2 2.0 %collective-permute-start.21 = (bf16[384,384]{1,0:T(8,128)(2,1)S(1)}, bf16[384,384]{1,0:T(8,128)(2,1)S(1)}, u32[]{:S(2)}, u32[]{:S(2)}) collective-permute-start(bf16[384,384]{1,0:T(8,128)(2,1)S(1)} %get-tuple-element.183), channel_id=1, source_target_pairs={{0,8},{4,12},{8,0},{12,4},{1,9},{5,13},{9,1},{13,5},{2,10},{6,14},... | collective-permute-start | bytes 884744 | tf_op jit(solution)/shard_map/ppermute | solution.py:730
  90.1 2.0 %collective-permute-start.22 = (bf16[384,384]{1,0:T(8,128)(2,1)S(1)}, bf16[384,384]{1,0:T(8,128)(2,1)S(1)}, u32[]{:S(2)}, u32[]{:S(2)}) collective-permute-start(bf16[384,384]{1,0:T(8,128)(2,1)S(1)} %get-tuple-element.184), channel_id=1, source_target_pairs={{0,4},{4,8},{8,12},{12,0},{1,5},{5,9},{9,13},{13,1},{2,6},{6,10},{... | collective-permute-start | bytes 884744 | tf_op jit(solution)/shard_map/ppermute | solution.py:730
  92.3 1.6 collective-permute-start.18
  93.9 3.1 %expand_grads_kernel.1 = (bf16[4,96,768]{2,1,0:T(8,128)(2,1)S(1)}, bf16[4,96,768]{2,1,0:T(8,128)(2,1)S(1)}, f32[288,768]{1,0:T(8,128)S(1)}, bf16[288,768]{1,0:T(...) custom-call(bf16[576,768]{1,0:T(8,128)(2,1)S(1)} %get-tuple-element.165.refs_0_.refs_3_, ...), custom_call_target="tpu_custom_call" | custom-call | flops 11000000512 | bytes 36000000 | tf_op jit(solution)/shard_map/expand_grads_kernel/pallas_call | solution.py:75
  97.1 6.9 %collective-permute-done.18.refs_1_ = bf16[288,768]{1,0:T(8,128)(2,1)S(1)} collective-permute-done((bf16[288,768]{1,0:T(8,128)(2,1)S(1)}, bf16[288,768]{1,0:T(8,128)(2,1)S(1)}, u32[]{:S(2)}, u32[]{:S(2)}) %collective-permute-start.18) | collective-permute-done | bytes 442400 | tf_op jit(solution)/shard_map/ppermute | solution.py:733
  103.9 1.5 collective-permute-start.16
  105.8 1.6 collective-permute-done.23.refs_1_
  107.4 1.5 collective-permute-start.19
  108.9 4.4 %attend_back_kernel.1 = (f32[144,768]{1,0:T(8,128)S(1)}, bf16[576,768]{1,0:T(8,128)(2,1)S(1)}, bf16[3,576,192]{2,1,0:T(8,128)(2,1)S(1)}, f32[144,896]{1,0:T(8,12...) custom-call(bf16[288,768]{1,0:T(8,128)(2,1)S(1)} %get-tuple-element., ...), custom_call_target="tpu_custom_call" | custom-call | flops 11000000512 | bytes 36000000 | tf_op jit(solution)/shard_map/attend_back_kernel/pallas_call | solution.py:75
  113.4 4.6 %joined_grads_kernel.1 = (bf16[4,208,384]{2,1,0:T(8,128)(2,1)S(1)}, bf16[4,208,384]{2,1,0:T(8,128)(2,1)S(1)}, f32[8,768]{1,0:T(8,128)S(1)}, f32[8,128]{1,0:T(8,128)S(1)}) custom-call(bf16[576,768]{1,0:T(8,128)(2,1)S(1)} %get-tuple-element.185.refs_0_, bf16[3,576,192]{2,1,0:T(8,128)(2,1)S(1)} %get-tuple-element.192.refs_1_, ...), custom_call_target="tpu_custom_call" | custom-call | flops 11000000512 | bytes 36000000 | tf_op jit(solution)/shard_map/joined_grads_kernel/pallas_call | solution.py:75
  119.6 2.1 %collective-permute-start.24 = (bf16[272,384]{1,0:T(8,128)(2,1)S(1)}, bf16[272,384]{1,0:T(8,128)(2,1)S(1)}, u32[]{:S(2)}, u32[]{:S(2)}) collective-permute-start(bf16[272,384]{1,0:T(8,128)(2,1)S(1)} %get-tuple-element.203), channel_id=1, source_target_pairs={{0,12},{4,0},{8,4},{12,8},{1,13},{5,1},{9,5},{13,9},{2,14},{6,2},{... | collective-permute-start | bytes 626696 | tf_op jit(solution)/shard_map/ppermute | solution.py:730
  123.3 1.1 collective-permute-start.31
  124.4 3.0 %collective-permute-done.24.refs_2_.refs_1_ = bf16[272,384]{1,0:T(8,128)(2,1)S(1)} collective-permute-done((bf16[272,384]{1,0:T(8,128)(2,1)S(1)}, bf16[272,384]{1,0:T(8,128)(2,1)S(1)}, u32[]{:S(2)}, u32[]{:S(2)}) %collective-permute-start.24) | collective-permute-done | bytes 208928 | tf_op jit(solution)/shard_map/ppermute | solution.py:730
  127.9 12.0 %collective-permute-done.25.refs_3_.refs_2_ = bf16[272,384]{1,0:T(8,128)(2,1)S(1)} collective-permute-done((bf16[272,384]{1,0:T(8,128)(2,1)S(1)}, bf16[272,384]{1,0:T(8,128)(2,1)S(1)}, u32[]{:S(2)}, u32[]{:S(2)}) %collective-permute-start.25) | collective-permute-done | bytes 208928 | tf_op jit(solution)/shard_map/ppermute | solution.py:730
  141.5 1.1 collective-permute-start.32
  142.6 2.6 %collective-permute-start.33 = (bf16[288,384]{1,0:T(8,128)(2,1)S(1)}, bf16[288,384]{1,0:T(8,128)(2,1)S(1)}, u32[]{:S(2)}, u32[]{:S(2)}) collective-permute-start(bf16[288,384]{1,0:T(8,128)(2,1)S(1)} %get-tuple-element.221), channel_id=1, source_target_pairs={{0,8},{4,12},{8,0},{12,4},{1,9},{5,13},{9,1},{13,5},{2,10},{6,14},... | collective-permute-start | bytes 663560 | tf_op jit(solution)/shard_map/ppermute | solution.py:730
  146.0 1.3 restore_kernel.1
  147.3 4.1 %collective-permute-done.35.refs_1_ = bf16[576,384]{1,0:T(8,128)(2,1)S(1)} collective-permute-done((bf16[576,384]{1,0:T(8,128)(2,1)S(1)}, bf16[576,384]{1,0:T(8,128)(2,1)S(1)}, u32[]{:S(2)}, u32[]{:S(2)}) %collective-permute-start.35) | collective-permute-done | bytes 442400 | tf_op jit(solution)/shard_map/ppermute | solution.py:736
  151.4 1.1 finish_hidden_kernel.1
  152.6 10.1 %collective-permute-done.33.refs_2_ = bf16[288,384]{1,0:T(8,128)(2,1)S(1)} collective-permute-done((bf16[288,384]{1,0:T(8,128)(2,1)S(1)}, bf16[288,384]{1,0:T(8,128)(2,1)S(1)}, u32[]{:S(2)}, u32[]{:S(2)}) %collective-permute-start.33) | collective-permute-done | bytes 221216 | tf_op jit(solution)/shard_map/ppermute | solution.py:730
  162.9 1.6 collective-permute-start.36
  164.5 1.4 restore_wide_kernel.1
  165.9 2.5 %collective-permute-done.36.refs_1_ = bf16[224,384]{1,0:T(8,128)(2,1)S(1)} collective-permute-done((bf16[224,384]{1,0:T(8,128)(2,1)S(1)}, bf16[224,384]{1,0:T(8,128)(2,1)S(1)}, u32[]{:S(2)}, u32[]{:S(2)}) %collective-permute-start.36) | collective-permute-done | bytes 172064 | tf_op jit(solution)/shard_map/ppermute | solution.py:736
  168.4 1.2 finish_joined_kernel.1
  (92 shorter events, 14.9 us)
Async XLA Ops:
  2.0 10.6 %copy-start.10 = (s32[24,24]{1,0:T(8,128)S(1)}, s32[24,24]{1,0:T(8,128)}, u32[]{:S(2)}) copy-start(s32[24,24]{1,0:T(8,128)} %param.21) | copy-start | bytes 6916
  2.0 10.9 %copy-start.9 = (s32[144,144]{1,0:T(8,128)S(1)}, s32[144,144]{1,0:T(8,128)}, u32[]{:S(2)}) copy-start(s32[144,144]{1,0:T(8,128)} %param.22) | copy-start | bytes 248836
  2.0 11.1 %copy-start.5 = (f32[529,6]{0,1:T(8,128)S(1)}, f32[529,6]{0,1:T(8,128)}, u32[]{:S(2)}) copy-start(f32[529,6]{0,1:T(8,128)} %param.27) | copy-start | bytes 38092
  5.7 12.7 %collective-permute-start = (bf16[352,384]{1,0:T(8,128)(2,1)}, bf16[352,384]{1,0:T(8,128)(2,1)S(1)}, u32[]{:S(2)}, u32[]{:S(2)}) collective-permute-start(bf16[352,384]{1,0:T(8,128)(2,1)} %get-tuple-element.130), channel_id=1, source_target_pairs={{0,4},{4,8},{8,12},{12,0},{1,5},{5,9},{9,13},{13,1},{2,6},{6,10},{... | collective-permute-start | bytes 811016 | tf_op jit(solution)/shard_map/ppermute | solution.py:730
  8.7 20.4 %collective-permute-start.1 = (bf16[352,384]{1,0:T(8,128)(2,1)}, bf16[352,384]{1,0:T(8,128)(2,1)S(1)}, u32[]{:S(2)}, u32[]{:S(2)}) collective-permute-start(bf16[352,384]{1,0:T(8,128)(2,1)} %get-tuple-element.131), channel_id=1, source_target_pairs={{0,8},{4,12},{8,0},{12,4},{1,9},{5,13},{9,1},{13,5},{2,10},{6,14},... | collective-permute-start | bytes 811016 | tf_op jit(solution)/shard_map/ppermute | solution.py:730
  11.3 17.9 %collective-permute-start.2 = (bf16[352,384]{1,0:T(8,128)(2,1)}, bf16[352,384]{1,0:T(8,128)(2,1)S(1)}, u32[]{:S(2)}, u32[]{:S(2)}) collective-permute-start(bf16[352,384]{1,0:T(8,128)(2,1)} %get-tuple-element.132), channel_id=1, source_target_pairs={{0,12},{4,0},{8,4},{12,8},{1,13},{5,1},{9,5},{13,9},{2,14},{6,2},{... | collective-permute-start | bytes 811016 | tf_op jit(solution)/shard_map/ppermute | solution.py:730
  13.8 15.4 %copy-start.6 = (s32[8]{0:T(128)S(1)}, s32[8]{0:T(128)}, u32[]{:S(2)}) copy-start(s32[8]{0:T(128)} %refs_0_.3) | copy-start | bytes 100
  13.8 15.4 %copy-start.7 = (bf16[352,384]{1,0:T(8,128)(2,1)S(1)}, bf16[352,384]{1,0:T(8,128)(2,1)}, u32[]{:S(2)}) copy-start(bf16[352,384]{1,0:T(8,128)(2,1)} %get-tuple-element.129.refs_1_) | copy-start | bytes 811012
  29.2 1.0 copy-start
  30.1 8.0 %copy-start.11 = (f32[768]{0:T(1024)S(1)}, f32[768]{0:T(1024)}, u32[]{:S(2)}) copy-start(f32[768]{0:T(1024)} %param.33) | copy-start | bytes 9220
  30.2 11.6 %collective-permute-start.6 = (bf16[96,768]{1,0:T(8,128)(2,1)S(1)}, bf16[96,768]{1,0:T(8,128)(2,1)S(1)}, u32[]{:S(2)}, u32[]{:S(2)}) collective-permute-start(bf16[96,768]{1,0:T(8,128)(2,1)S(1)} %get-tuple-element.137), channel_id=1, source_target_pairs={{0,12},{4,0},{8,4},{12,8},{1,13},{5,1},{9,5},{13,9},{2,14},{6,2},{... | collective-permute-start | bytes 442376 | tf_op jit(solution)/shard_map/ppermute | solution.py:730
  37.5 13.6 %collective-permute-start.5 = (bf16[96,768]{1,0:T(8,128)(2,1)S(1)}, bf16[96,768]{1,0:T(8,128)(2,1)S(1)}, u32[]{:S(2)}, u32[]{:S(2)}) collective-permute-start(bf16[96,768]{1,0:T(8,128)(2,1)S(1)} %get-tuple-element.137), channel_id=1, source_target_pairs={{0,8},{4,12},{8,0},{12,4},{1,9},{5,13},{9,1},{13,5},{2,10},{6,14},... | collective-permute-start | bytes 442376 | tf_op jit(solution)/shard_map/ppermute | solution.py:730
  37.9 13.2 %collective-permute-start.4 = (bf16[96,768]{1,0:T(8,128)(2,1)S(1)}, bf16[96,768]{1,0:T(8,128)(2,1)S(1)}, u32[]{:S(2)}, u32[]{:S(2)}) collective-permute-start(bf16[96,768]{1,0:T(8,128)(2,1)S(1)} %get-tuple-element.137), channel_id=1, source_target_pairs={{0,4},{4,8},{8,12},{12,0},{1,5},{5,9},{9,13},{13,1},{2,6},{6,10},{... | collective-permute-start | bytes 442376 | tf_op jit(solution)/shard_map/ppermute | solution.py:730
  38.2 16.9 %collective-permute-start.3 = (bf16[288,768]{1,0:T(8,128)(2,1)S(1)}, bf16[288,768]{1,0:T(8,128)(2,1)S(1)}, u32[]{:S(2)}, u32[]{:S(2)}) collective-permute-start(bf16[288,768]{1,0:T(8,128)(2,1)S(1)} %get-tuple-element.135.refs_0_), channel_id=1, source_target_pairs={{0,2},{1,3},{2,0},{3,1},{4,6},{5,7},{6,4},{7,5},{8,10},{9,11},{10,... | collective-permute-start | bytes 1327112 | tf_op jit(solution)/shard_map/ppermute | solution.py:733
  39.7 16.9 %collective-permute-start.12 = (bf16[3,192,384]{2,1,0:T(8,128)(2,1)S(1)}, bf16[3,192,384]{2,1,0:T(8,128)(2,1)S(1)}, u32[]{:S(2)}, u32[]{:S(2)}) collective-permute-start(bf16[3,192,384]{2,1,0:T(8,128)(2,1)S(1)} %get-tuple-element.145.refs_2_), channel_id=1, source_target_pairs={{0,16},{16,0},{1,17},{17,1},{2,18},{18,2},{3,19},{19,3},{4,20},{20... | collective-permute-start | bytes 1327112 | tf_op jit(solution)/shard_map/ppermute | solution.py:736
  51.2 1.0 copy-start.2
  52.2 14.9 %collective-permute-start.10 = (bf16[384,384]{1,0:T(8,128)(2,1)S(1)}, bf16[384,384]{1,0:T(8,128)(2,1)S(1)}, u32[]{:S(2)}, u32[]{:S(2)}) collective-permute-start(bf16[384,384]{1,0:T(8,128)(2,1)S(1)} %get-tuple-element.142), channel_id=1, source_target_pairs={{0,12},{4,0},{8,4},{12,8},{1,13},{5,1},{9,5},{13,9},{2,14},{6,2},{... | collective-permute-start | bytes 884744 | tf_op jit(solution)/shard_map/ppermute | solution.py:730
  52.2 26.3 %collective-permute-start.9 = (bf16[384,384]{1,0:T(8,128)(2,1)S(1)}, bf16[384,384]{1,0:T(8,128)(2,1)S(1)}, u32[]{:S(2)}, u32[]{:S(2)}) collective-permute-start(bf16[384,384]{1,0:T(8,128)(2,1)S(1)} %get-tuple-element.142), channel_id=1, source_target_pairs={{0,8},{4,12},{8,0},{12,4},{1,9},{5,13},{9,1},{13,5},{2,10},{6,14},... | collective-permute-start | bytes 884744 | tf_op jit(solution)/shard_map/ppermute | solution.py:730
  53.1 25.4 %collective-permute-start.8 = (bf16[384,384]{1,0:T(8,128)(2,1)S(1)}, bf16[384,384]{1,0:T(8,128)(2,1)S(1)}, u32[]{:S(2)}, u32[]{:S(2)}) collective-permute-start(bf16[384,384]{1,0:T(8,128)(2,1)S(1)} %get-tuple-element.142), channel_id=1, source_target_pairs={{0,4},{4,8},{8,12},{12,0},{1,5},{5,9},{9,13},{13,1},{2,6},{6,10},{... | collective-permute-start | bytes 884744 | tf_op jit(solution)/shard_map/ppermute | solution.py:730
  55.1 10.6 %collective-permute-start.11 = (bf16[3,96,768]{2,1,0:T(8,128)(2,1)S(1)}, bf16[3,96,768]{2,1,0:T(8,128)(2,1)S(1)}, u32[]{:S(2)}, u32[]{:S(2)}) collective-permute-start(bf16[3,96,768]{2,1,0:T(8,128)(2,1)S(1)} %get-tuple-element.143.refs_1_), channel_id=1, source_target_pairs={{0,16},{16,0},{1,17},{17,1},{2,18},{18,2},{3,19},{19,3},{4,20},{20... | collective-permute-start | bytes 1327112 | tf_op jit(solution)/shard_map/ppermute | solution.py:736
  56.6 0.9 copy-start.3
  56.6 1.0 copy-start.4
  56.6 2.5 %collective-permute-start.7 = (bf16[2,288,768]{2,1,0:T(8,128)(2,1)S(1)}, bf16[2,288,768]{2,1,0:T(8,128)(2,1)S(1)}, u32[]{:S(2)}, u32[]{:S(2)}) collective-permute-start(bf16[2,288,768]{2,1,0:T(8,128)(2,1)S(1)} %get-tuple-element.141.refs_0_), channel_id=1, source_target_pairs={{0,1},{1,0},{2,3},{3,2},{4,5},{5,4},{6,7},{7,6},{8,9},{9,8},{10,11... | collective-permute-start | bytes 2654216 | tf_op jit(solution)/shard_map/ppermute | solution.py:733
  57.6 1.6 copy-start.1
  63.1 15.7 %collective-permute-start.13 = (bf16[672,384]{1,0:T(8,128)(2,1)S(1)}, bf16[672,384]{1,0:T(8,128)(2,1)S(1)}, u32[]{:S(2)}, u32[]{:S(2)}) collective-permute-start(bf16[672,384]{1,0:T(8,128)(2,1)S(1)} %get-tuple-element.155.refs_0_.refs_2_), channel_id=1, source_target_pairs={{0,2},{1,3},{2,0},{3,1},{4,6},{5,7},{6,4},{7,5},{8,10},{9,11},{10,... | collective-permute-start | bytes 1548296 | tf_op jit(solution)/shard_map/ppermute | solution.py:733
  78.9 2.7 %collective-permute-start.14 = (bf16[2,672,384]{2,1,0:T(8,128)(2,1)S(1)}, bf16[2,672,384]{2,1,0:T(8,128)(2,1)S(1)}, u32[]{:S(2)}, u32[]{:S(2)}) collective-permute-start(bf16[2,672,384]{2,1,0:T(8,128)(2,1)S(1)} %get-tuple-element.157.refs_1_), channel_id=1, source_target_pairs={{0,1},{1,0},{2,3},{3,2},{4,5},{5,4},{6,7},{7,6},{8,9},{9,8},{10,11... | collective-permute-start | bytes 3096584 | tf_op jit(solution)/shard_map/ppermute | solution.py:733
  87.9 4.2 %collective-permute-start.15 = (bf16[288,768]{1,0:T(8,128)(2,1)S(1)}, bf16[288,768]{1,0:T(8,128)(2,1)S(1)}, u32[]{:S(2)}, u32[]{:S(2)}) collective-permute-start(bf16[288,768]{1,0:T(8,128)(2,1)S(1)} %get-tuple-element.169), channel_id=1, source_target_pairs={{0,1},{1,0},{2,3},{3,2},{4,5},{5,4},{6,7},{7,6},{8,9},{9,8},{10,11... | collective-permute-start | bytes 1327112 | tf_op jit(solution)/shard_map/ppermute | solution.py:733
  88.1 25.2 %collective-permute-start.20 = (bf16[384,384]{1,0:T(8,128)(2,1)S(1)}, bf16[384,384]{1,0:T(8,128)(2,1)S(1)}, u32[]{:S(2)}, u32[]{:S(2)}) collective-permute-start(bf16[384,384]{1,0:T(8,128)(2,1)S(1)} %get-tuple-element.182), channel_id=1, source_target_pairs={{0,12},{4,0},{8,4},{12,8},{1,13},{5,1},{9,5},{13,9},{2,14},{6,2},{... | collective-permute-start | bytes 884744 | tf_op jit(solution)/shard_map/ppermute | solution.py:730
  88.2 29.9 %collective-permute-start.21 = (bf16[384,384]{1,0:T(8,128)(2,1)S(1)}, bf16[384,384]{1,0:T(8,128)(2,1)S(1)}, u32[]{:S(2)}, u32[]{:S(2)}) collective-permute-start(bf16[384,384]{1,0:T(8,128)(2,1)S(1)} %get-tuple-element.183), channel_id=1, source_target_pairs={{0,8},{4,12},{8,0},{12,4},{1,9},{5,13},{9,1},{13,5},{2,10},{6,14},... | collective-permute-start | bytes 884744 | tf_op jit(solution)/shard_map/ppermute | solution.py:730
  90.1 28.5 %collective-permute-start.22 = (bf16[384,384]{1,0:T(8,128)(2,1)S(1)}, bf16[384,384]{1,0:T(8,128)(2,1)S(1)}, u32[]{:S(2)}, u32[]{:S(2)}) collective-permute-start(bf16[384,384]{1,0:T(8,128)(2,1)S(1)} %get-tuple-element.184), channel_id=1, source_target_pairs={{0,4},{4,8},{8,12},{12,0},{1,5},{5,9},{9,13},{13,1},{2,6},{6,10},{... | collective-permute-start | bytes 884744 | tf_op jit(solution)/shard_map/ppermute | solution.py:730
  92.3 11.7 %collective-permute-start.18 = (bf16[288,768]{1,0:T(8,128)(2,1)S(1)}, bf16[288,768]{1,0:T(8,128)(2,1)S(1)}, u32[]{:S(2)}, u32[]{:S(2)}) collective-permute-start(bf16[288,768]{1,0:T(8,128)(2,1)S(1)} %get-tuple-element.177.refs_0_), channel_id=1, source_target_pairs={{0,2},{1,3},{2,0},{3,1},{4,6},{5,7},{6,4},{7,5},{8,10},{9,11},{10,... | collective-permute-start | bytes 1327112 | tf_op jit(solution)/shard_map/ppermute | solution.py:733
  97.0 8.5 %collective-permute-start.17 = (bf16[288,768]{1,0:T(8,128)(2,1)S(1)}, bf16[288,768]{1,0:T(8,128)(2,1)S(1)}, u32[]{:S(2)}, u32[]{:S(2)}) collective-permute-start(bf16[288,768]{1,0:T(8,128)(2,1)S(1)} %get-tuple-element.176), channel_id=1, source_target_pairs={{0,1},{1,0},{2,3},{3,2},{4,5},{5,4},{6,7},{7,6},{8,9},{9,8},{10,11... | collective-permute-start | bytes 1327112 | tf_op jit(solution)/shard_map/ppermute | solution.py:733
  103.9 15.4 %collective-permute-start.16 = (bf16[4,96,768]{2,1,0:T(8,128)(2,1)S(1)}, bf16[4,96,768]{2,1,0:T(8,128)(2,1)S(1)}, u32[]{:S(2)}, u32[]{:S(2)}) collective-permute-start(bf16[4,96,768]{2,1,0:T(8,128)(2,1)S(1)} %get-tuple-element.173), channel_id=1, source_target_pairs={{0,16},{16,0},{1,17},{17,1},{2,18},{18,2},{3,19},{19,3},{4,20},{20... | collective-permute-start | bytes 1769480 | tf_op jit(solution)/shard_map/ppermute | solution.py:736
  105.5 1.9 %collective-permute-start.23 = (bf16[288,768]{1,0:T(8,128)(2,1)S(1)}, bf16[288,768]{1,0:T(8,128)(2,1)S(1)}, u32[]{:S(2)}, u32[]{:S(2)}) collective-permute-start(bf16[288,768]{1,0:T(8,128)(2,1)S(1)} %get-tuple-element.186.refs_0_), channel_id=1, source_target_pairs={{0,1},{1,0},{2,3},{3,2},{4,5},{5,4},{6,7},{7,6},{8,9},{9,8},{10,11... | collective-permute-start | bytes 1327112 | tf_op jit(solution)/shard_map/ppermute | solution.py:733
  107.4 11.9 %collective-permute-start.19 = (bf16[144,768]{1,0:T(8,128)(2,1)S(1)}, bf16[144,768]{1,0:T(8,128)(2,1)S(1)}, u32[]{:S(2)}, u32[]{:S(2)}) collective-permute-start(bf16[144,768]{1,0:T(8,128)(2,1)S(1)} %slice.6), channel_id=1, source_target_pairs={{0,2},{1,3},{2,0},{3,1},{4,6},{5,7},{6,4},{7,5},{8,10},{9,11},{10,... | collective-permute-start | bytes 663560 | tf_op jit(solution)/shard_map/ppermute | solution.py:733
  113.4 9.3 %collective-permute-start.28 = (bf16[288,768]{1,0:T(8,128)(2,1)S(1)}, bf16[288,768]{1,0:T(8,128)(2,1)S(1)}, u32[]{:S(2)}, u32[]{:S(2)}) collective-permute-start(bf16[288,768]{1,0:T(8,128)(2,1)S(1)} %get-tuple-element.195.refs_6_), channel_id=1, source_target_pairs={{0,1},{1,0},{2,3},{3,2},{4,5},{5,4},{6,7},{7,6},{8,9},{9,8},{10,11... | collective-permute-start | bytes 1327112 | tf_op jit(solution)/shard_map/ppermute | solution.py:733
  118.0 5.3 %collective-permute-start.30 = (f32[8,768]{1,0:T(8,128)S(1)}, f32[8,768]{1,0:T(8,128)S(1)}, u32[]{:S(2)}, u32[]{:S(2)}) collective-permute-start(f32[8,768]{1,0:T(8,128)S(1)} %get-tuple-element.211.refs_0_), channel_id=1, source_target_pairs={{0,1},{1,0},{2,3},{3,2},{4,5},{5,4},{6,7},{7,6},{8,9},{9,8},{10,11... | collective-permute-start | bytes 73736 | tf_op jit(solution)/shard_map/ppermute | solution.py:733
  119.6 7.8 %collective-permute-start.24 = (bf16[272,384]{1,0:T(8,128)(2,1)S(1)}, bf16[272,384]{1,0:T(8,128)(2,1)S(1)}, u32[]{:S(2)}, u32[]{:S(2)}) collective-permute-start(bf16[272,384]{1,0:T(8,128)(2,1)S(1)} %get-tuple-element.203), channel_id=1, source_target_pairs={{0,12},{4,0},{8,4},{12,8},{1,13},{5,1},{9,5},{13,9},{2,14},{6,2},{... | collective-permute-start | bytes 626696 | tf_op jit(solution)/shard_map/ppermute | solution.py:730
  121.8 18.2 %collective-permute-start.25 = (bf16[272,384]{1,0:T(8,128)(2,1)S(1)}, bf16[272,384]{1,0:T(8,128)(2,1)S(1)}, u32[]{:S(2)}, u32[]{:S(2)}) collective-permute-start(bf16[272,384]{1,0:T(8,128)(2,1)S(1)} %get-tuple-element.204), channel_id=1, source_target_pairs={{0,8},{4,12},{8,0},{12,4},{1,9},{5,13},{9,1},{13,5},{2,10},{6,14},... | collective-permute-start | bytes 626696 | tf_op jit(solution)/shard_map/ppermute | solution.py:730
  121.8 18.2 %collective-permute-start.26 = (bf16[272,384]{1,0:T(8,128)(2,1)S(1)}, bf16[272,384]{1,0:T(8,128)(2,1)S(1)}, u32[]{:S(2)}, u32[]{:S(2)}) collective-permute-start(bf16[272,384]{1,0:T(8,128)(2,1)S(1)} %get-tuple-element.205), channel_id=1, source_target_pairs={{0,4},{4,8},{8,12},{12,0},{1,5},{5,9},{9,13},{13,1},{2,6},{6,10},{... | collective-permute-start | bytes 626696 | tf_op jit(solution)/shard_map/ppermute | solution.py:730
  122.7 18.1 %collective-permute-start.27 = (bf16[4,208,384]{2,1,0:T(8,128)(2,1)S(1)}, bf16[4,208,384]{2,1,0:T(8,128)(2,1)S(1)}, u32[]{:S(2)}, u32[]{:S(2)}) collective-permute-start(bf16[4,208,384]{2,1,0:T(8,128)(2,1)S(1)} %get-tuple-element.207), channel_id=1, source_target_pairs={{0,16},{16,0},{1,17},{17,1},{2,18},{18,2},{3,19},{19,3},{4,20},{20... | collective-permute-start | bytes 1916936 | tf_op jit(solution)/shard_map/ppermute | solution.py:736
  123.3 17.4 %collective-permute-start.31 = (f32[8,768]{1,0:T(8,128)S(1)}, f32[8,768]{1,0:T(8,128)S(1)}, u32[]{:S(2)}, u32[]{:S(2)}) collective-permute-start(f32[8,768]{1,0:T(8,128)S(1)} %get-tuple-element.213.refs_7_), channel_id=1, source_target_pairs={{0,2},{1,3},{2,0},{3,1},{4,6},{5,7},{6,4},{7,5},{8,10},{9,11},{10,... | collective-permute-start | bytes 73736 | tf_op jit(solution)/shard_map/ppermute | solution.py:733
  127.4 13.3 %collective-permute-start.29 = (bf16[144,768]{1,0:T(8,128)(2,1)S(1)}, bf16[144,768]{1,0:T(8,128)(2,1)S(1)}, u32[]{:S(2)}, u32[]{:S(2)}) collective-permute-start(bf16[144,768]{1,0:T(8,128)(2,1)S(1)} %slice.7), channel_id=1, source_target_pairs={{0,2},{1,3},{2,0},{3,1},{4,6},{5,7},{6,4},{7,5},{8,10},{9,11},{10,... | collective-permute-start | bytes 663560 | tf_op jit(solution)/shard_map/ppermute | solution.py:733
  140.1 11.3 %collective-permute-start.35 = (bf16[576,384]{1,0:T(8,128)(2,1)S(1)}, bf16[576,384]{1,0:T(8,128)(2,1)S(1)}, u32[]{:S(2)}, u32[]{:S(2)}) collective-permute-start(bf16[576,384]{1,0:T(8,128)(2,1)S(1)} %get-tuple-element.223.refs_0_), channel_id=1, source_target_pairs={{0,16},{16,0},{1,17},{17,1},{2,18},{18,2},{3,19},{19,3},{4,20},{20... | collective-permute-start | bytes 1327112 | tf_op jit(solution)/shard_map/ppermute | solution.py:736
  141.5 11.1 %collective-permute-start.32 = (bf16[288,384]{1,0:T(8,128)(2,1)S(1)}, bf16[288,384]{1,0:T(8,128)(2,1)S(1)}, u32[]{:S(2)}, u32[]{:S(2)}) collective-permute-start(bf16[288,384]{1,0:T(8,128)(2,1)S(1)} %get-tuple-element.220), channel_id=1, source_target_pairs={{0,12},{4,0},{8,4},{12,8},{1,13},{5,1},{9,5},{13,9},{2,14},{6,2},{... | collective-permute-start | bytes 663560 | tf_op jit(solution)/shard_map/ppermute | solution.py:730
  142.6 20.2 %collective-permute-start.33 = (bf16[288,384]{1,0:T(8,128)(2,1)S(1)}, bf16[288,384]{1,0:T(8,128)(2,1)S(1)}, u32[]{:S(2)}, u32[]{:S(2)}) collective-permute-start(bf16[288,384]{1,0:T(8,128)(2,1)S(1)} %get-tuple-element.221), channel_id=1, source_target_pairs={{0,8},{4,12},{8,0},{12,4},{1,9},{5,13},{9,1},{13,5},{2,10},{6,14},... | collective-permute-start | bytes 663560 | tf_op jit(solution)/shard_map/ppermute | solution.py:730
  145.1 17.6 %collective-permute-start.34 = (bf16[288,384]{1,0:T(8,128)(2,1)S(1)}, bf16[288,384]{1,0:T(8,128)(2,1)S(1)}, u32[]{:S(2)}, u32[]{:S(2)}) collective-permute-start(bf16[288,384]{1,0:T(8,128)(2,1)S(1)} %get-tuple-element.222), channel_id=1, source_target_pairs={{0,4},{4,8},{8,12},{12,0},{1,5},{5,9},{9,13},{13,1},{2,6},{6,10},{... | collective-permute-start | bytes 663560 | tf_op jit(solution)/shard_map/ppermute | solution.py:730
  162.9 5.5 %collective-permute-start.36 = (bf16[224,384]{1,0:T(8,128)(2,1)S(1)}, bf16[224,384]{1,0:T(8,128)(2,1)S(1)}, u32[]{:S(2)}, u32[]{:S(2)}) collective-permute-start(bf16[224,384]{1,0:T(8,128)(2,1)S(1)} %get-tuple-element.228.refs_0_), channel_id=1, source_target_pairs={{0,16},{16,0},{1,17},{17,1},{2,18},{18,2},{3,19},{19,3},{4,20},{20... | collective-permute-start | bytes 516104 | tf_op jit(solution)/shard_map/ppermute | solution.py:736
  (1 other events, 0.7 us)
where the time goes:
time: 171 us; the launch traced here: 170 us
  waiting for transfers between devices  79.3 us (46%)
  starting transfers between devices  45.5 us (27%)
  Pallas kernels  39.5 us (23%)
  local copies, waits for them, and re-layouts  4.28 us (3%)
    ppermute x18, waiting for transfers between devices, turn(): lax.ppermute(value, 'row', [(i, (i + shift) % row_size) for i in range(ro...  60.1 us
    pallas_call x32, Pallas kernels, run(): pl.pallas_call(body, out_shape=[jax.ShapeDtypeStruct(shape, dtype) for sh...  39.5 us
    ppermute x18, starting transfers between devices, turn(): lax.ppermute(value, 'row', [(i, (i + shift) % row_size) for i in range(ro...  29.4 us
    ppermute x13, waiting for transfers between devices, flip(): return lax.ppermute(value, 'col', [(i, i ^ bits) for i in range(col_size)])  11.6 us
    ppermute x13, starting transfers between devices, flip(): return lax.ppermute(value, 'col', [(i, i ^ bits) for i in range(col_size)])  8.88 us
    ppermute x6, waiting for transfers between devices, swap(): return lax.ppermute(value, 'dp', [(i, i ^ bits) for i in range(dp_size)])  7.66 us
    ppermute x6, starting transfers between devices, swap(): return lax.ppermute(value, 'dp', [(i, i ^ bits) for i in range(dp_size)])  7.16 us
  transfers between devices with their start and end apart: 37, of which 15 were waited for; matrix products, arithmetic and copies ran while one was open for 0% of the time, Pallas kernels for 16%

commit v1 on v0

--- a/solution.py
+++ b/solution.py
@@ -25,6 +25,7 @@
 GROUP = 4
 TOKENS = GROUP * CELLS
 HEADS = BLOCK // HEAD_DIM
+STACK_TAKES = False
 VMEM_MIB = 24
 ORDER_MIB = 60
 ROOT_HALF = 0.7071067811865476
@@ -95,15 +96,6 @@
     return token >> 1, token & 1
 
 
-def window_rows(paired_even, paired_odd, window, begin, rows):
-    count = paired_even.shape[0]
-    half, parity = place(window, iota((rows, count), 0) + begin)
-    hit = half == iota((rows, count), 1)
-    pick_even = jnp.where(hit & (parity == 0), 1.0, 0.0).astype(BF)
-    pick_odd = jnp.where(hit & (parity == 1), 1.0, 0.0).astype(BF)
-    return dot(pick_even, paired_even) + dot(pick_odd, paired_odd)
-
-
 LINES = CELLS // 2
 FIRST = 2 * CELLS // 2 + 16
 QUARTER = BLOCK // 4
@@ -112,24 +104,35 @@
 ATT = 2 * CELLS
 
 
-def order_kernel(ids, vectors, paired, cotangent, joined, out_own, o0, o1, o2, o3, held):
+def order_kernel(
+    ids, g0, g1, g2, g3, g4, g5, paired, cotangent, joined, out_own, o0, o1, o2, o3, held, vectors
+):
+    for n, vector in enumerate((g0, g1, g2, g3, g4, g5)):
+        vectors[n : n + 1, :] = vector[...]
     z = ids[1]
-    sources = [(v[:, :BLOCK], v[:, BLOCK:]) for v in (paired, cotangent)]
-    held[...] = jnp.zeros(held.shape, F32)
+    count = paired.shape[0]
+    picks = []
+    for s in range(GROUP):
+        half, parity = place((z + s) % GROUP, iota((CELLS, count), 0))
+        hit = half == iota((CELLS, count), 1)
+        picks.append([jnp.where(hit & (parity == q), 1.0, 0.0).astype(BF) for q in range(2)])
+    even, odd = [jnp.concatenate([pick[q] for pick in picks], axis=0) for q in range(2)]
+    rows = [dot(even, v[:, :BLOCK]) + dot(odd, v[:, BLOCK:]) for v in (paired, cotangent)]
     whole = vectors[...]
     high = whole.astype(BF).astype(F32)
     rest = whole - high
     middle = rest.astype(BF).astype(F32)
     begin = aligned(ids[0] * QUARTER, 16)
     for s, out in enumerate((o0, o1, o2, o3)):
+        held[s, 2 * LINES :, :] = jnp.zeros((FIRST - 2 * LINES, HALF), F32)
         held[s, 2 * LINES : 2 * LINES + 6, :BLOCK] = high
         held[s, 2 * LINES : 2 * LINES + 6, BLOCK:] = middle
         held[s, 2 * LINES + 8 : 2 * LINES + 14, :BLOCK] = rest - middle
-        for n, (even, odd) in enumerate(sources):
+        for n in range(2):
             for k in range(2):
-                held[s, n * LINES : (n + 1) * LINES, k * BLOCK : (k + 1) * BLOCK] = window_rows(
-                    even, odd, (z + s) % GROUP, k * LINES, LINES
-                )
+                held[s, n * LINES : (n + 1) * LINES, k * BLOCK : (k + 1) * BLOCK] = rows[n][
+                    s * CELLS + k * LINES : s * CELLS + (k + 1) * LINES
+                ]
         out[0:FIRST, :] = held[s].astype(BF)
         for part in range(3):
             out[FIRST + part * QUARTER : FIRST + (part + 1) * QUARTER, :] = joined[part, pl.ds(begin, QUARTER), :]
@@ -159,6 +162,14 @@
 def couple_kernel(ids, a, b, out):
     out[0] = a[...]
     out[1] = b[...]
+
+
+def couple_out_kernel(ids, a, b, out):
+    couple_kernel(ids, a, b, out)
+
+
+def couple_att_kernel(ids, a, b, out):
+    couple_kernel(ids, a, b, out)
 
 
 def half_kernel(ids, whole, out):
@@ -373,9 +384,9 @@
 
 def attend_kernel(ids, *refs):
     pieces = refs[0:2]
-    vectors, weights, head_bias, bias, out_weight = refs[2:7]
-    tokens, normed, queries, keys, values, probs, attended = refs[7:14]
-    stacked, held = refs[14:16]
+    vectors, weights, head_bias, bias = refs[2:6]
+    tokens, normed, queries, keys, values, probs, attended = refs[6:13]
+    stacked, held = refs[13:15]
     gain = vectors[0:1, :]
     shift = vectors[1:2, :]
     for j in range(GROUP):
@@ -406,25 +417,20 @@
         attended[(w & 1) * CELLS : (w & 1) * CELLS + CELLS, (w >> 1) * BLOCK : (w >> 1) * BLOCK + BLOCK] = (
             total.astype(BF)
         )
-    for k in range(2):
-        attended[ATT + k * BLOCK : ATT + (k + 1) * BLOCK, :] = out_weight[:, k * HALF : (k + 1) * HALF]
 
 
 def expand_kernel(ids, *refs):
     tokens = refs[0]
     attended = refs[1:3]
-    vectors, weights, hidden_bias = refs[3:6]
-    middle, normed, hidden, slope = refs[6:10]
-    joined, square = refs[10:12]
+    out_weights = refs[3:5]
+    vectors, weights, hidden_bias = refs[5:8]
+    middle, normed, hidden, slope = refs[8:12]
+    joined, square = refs[12:14]
     for j in range(GROUP):
-        source = attended[j & 1]
-        for k in range(2):
-            square[j * BLOCK : (j + 1) * BLOCK, k * HALF : (k + 1) * HALF] = source[
-                j >> 1, ATT + k * BLOCK : ATT + (k + 1) * BLOCK, :
-            ]
+        square[j * BLOCK : (j + 1) * BLOCK, :] = out_weights[j & 1][j >> 1]
         for i in range(GROUP):
             k = i ^ j
-            joined[i * CELLS : (i + 1) * CELLS, j * BLOCK : (j + 1) * BLOCK] = source[
+            joined[i * CELLS : (i + 1) * CELLS, j * BLOCK : (j + 1) * BLOCK] = attended[j & 1][
                 j >> 1, (k & 1) * CELLS : (k & 1) * CELLS + CELLS, (k >> 1) * BLOCK : (k >> 1) * BLOCK + BLOCK
             ]
     out_bias = vectors[2:3, :]
@@ -447,9 +453,9 @@
 
 def split_slots(product, keep, send):
     keep[0:CELLS, :] = product[0:CELLS].astype(keep.dtype)
-    keep[CELLS:, :] = product[2 * CELLS : 3 * CELLS].astype(keep.dtype)
+    keep[CELLS : 2 * CELLS, :] = product[2 * CELLS : 3 * CELLS].astype(keep.dtype)
     send[0:CELLS, :] = product[CELLS : 2 * CELLS].astype(send.dtype)
-    send[CELLS:, :] = product[3 * CELLS :].astype(send.dtype)
+    send[CELLS : 2 * CELLS, :] = product[3 * CELLS :].astype(send.dtype)
 
 
 def hidden_back_kernel(ids, u0, u1, contract, slope, expand, upstream, pre_grad, keep, send):
@@ -474,22 +480,31 @@
 ):
     x = ids[0]
     mixed = dot_tn(normed[...], pre_grad[...]).astype(BF)
-    whole_e[...] = dot_nt(mixed, hidden_perm()).astype(BF)
+    perm = hidden_perm()
+    whole_e[...] = dot_nt(mixed, perm).astype(BF)
     lines = BLOCK // 2
     for s in range(GROUP):
         for out, side in ((keep, x), (send, 1 - x)):
             out[s] = whole_e[pl.ds(aligned(s * BLOCK + side * lines, 16), lines), :]
     split_slots(dot(hidden[...], contract[...]), keep_out, send_out)
     sums[...] = jnp.zeros(sums.shape, F32)
-    sums[0:1, :] = jnp.sum(pre_grad[...].astype(F32), axis=0, keepdims=True)
+    total = jnp.sum(pre_grad[...].astype(F32), axis=0, keepdims=True)
+    high = total.astype(BF).astype(F32)
+    middle = (total - high).astype(BF).astype(F32)
+    sums[0:1, :] = high
+    sums[1:2, :] = middle
+    sums[2:3, :] = total - high - middle
+    found = dot_nt(sums[...].astype(BF), perm)
+    sums[0:1, :] = found[0:1] + found[1:2] + found[2:3]
     sums[1:2, :] = jnp.sum(upstream[0:CELLS, :].astype(F32), axis=0, keepdims=True)
 
 
 def attend_back_kernel(ids, *refs):
     even_total, odd_total, middle, upstream = refs[0:4]
     vectors, out_weights, queries, keys, values, probs, weights = refs[4:11]
-    own_mid, mid_low, joined, bias_grad, keep, send, sums = refs[11:18]
-    attended_grad, stacked, stacked_grad, scores, held = refs[18:23]
+    tokens, hidden_sums = refs[11:13]
+    own_mid, mid_low, joined, bias_grad, keep, send = refs[13:19]
+    attended_grad, stacked, stacked_grad, scores, held, sums = refs[19:25]
     gain = vectors[3:4, :]
     sums[...] = jnp.zeros(sums.shape, F32)
     for w in range(GROUP):
@@ -504,9 +519,10 @@
         mid_low[rows, :] = low
         if w == 0:
             own_mid[...] = mid
-            sums[0:1, :] = jnp.sum(low.astype(F32), axis=0, keepdims=True)
-            sums[1:2, :] = jnp.sum(grad * scaled, axis=0, keepdims=True)
-            sums[2:3, :] = jnp.sum(grad, axis=0, keepdims=True)
+            sums[0:1, :] = hidden_sums[1:2, :]
+            sums[1:2, :] = jnp.sum(low.astype(F32), axis=0, keepdims=True)
+            sums[2:3, :] = jnp.sum(grad * scaled, axis=0, keepdims=True)
+            sums[3:4, :] = jnp.sum(grad, axis=0, keepdims=True)
     attended_grad[...] = dot_nt(mid_low[...], out_weights[...]).astype(BF)
     lane_head = iota((CELLS, BLOCK), 1) // HEAD_DIM
     scale = float(HEAD_DIM) ** (-0.5)
@@ -534,14 +550,27 @@
         joined[2, rows, :] = value_grad.astype(BF)
     product = dot_nt(joined[0], weights[0]) + dot_nt(joined[1], weights[1]) + dot_nt(joined[2], weights[2])
     split_slots(product, keep, send)
+    gains = shifts = None
+    for w in range(GROUP):
+        grad = product[w * CELLS : (w + 1) * CELLS]
+        scaled, _ = norm_stats(tokens[w * CELLS : (w + 1) * CELLS, :].astype(F32))
+        more_gains = jnp.sum(grad * scaled, axis=0, keepdims=True)
+        more_shifts = jnp.sum(grad, axis=0, keepdims=True)
+        gains = more_gains if gains is None else gains + more_gains
+        shifts = more_shifts if shifts is None else shifts + more_shifts
+    sums[4:5, :] = gains
+    sums[5:6, :] = shifts
+    low = sums[...].astype(BF)
+    keep[2 * CELLS :, :] = low.astype(F32)
+    send[2 * CELLS :, :] = low
 
 
 SMALL = 16
 
 
 def joined_grads_kernel(
-    ids, normed, joined, attended, mid_low, tokens, keep_in, send_in, hidden_sums, mid_sums,
-    bias_grad, offset, keep, send, row_sums, whole_q, whole_o, small, small_low, strips, strip_sums,
+    ids, normed, joined, attended, mid_low, hidden_sums,
+    bias_grad, offset, keep, send, whole_q, whole_o, small, small_low, strips, strip_sums,
 ):
     x = ids[0]
     whole = normed[...]
@@ -564,15 +593,6 @@
         lines = dot_tn(picks[q], wide).astype(BF)
         for s in range(GROUP):
             whole_o[s, :, q * BLOCK : (q + 1) * BLOCK] = lines[:, s * BLOCK : (s + 1) * BLOCK]
-    gains = shifts = None
-    for w in range(GROUP):
-        source = (keep_in, send_in)[w & 1]
-        grad = source[(w >> 1) * CELLS : (w >> 1) * CELLS + CELLS, :].astype(F32)
-        scaled, _ = norm_stats(tokens[w * CELLS : (w + 1) * CELLS, :].astype(F32))
-        more_gains = jnp.sum(grad * scaled, axis=0, keepdims=True)
-        more_shifts = jnp.sum(grad, axis=0, keepdims=True)
-        gains = more_gains if gains is None else gains + more_gains
-        shifts = more_shifts if shifts is None else shifts + more_shifts
     small[...] = jnp.zeros(small.shape, F32)
     table = table_sums(bias_grad, offset, strips, strip_sums)
     for s in range(GROUP):
@@ -582,11 +602,6 @@
             small[s, 2 + part : 3 + part, 0:BLOCK] = jnp.sum(joined[part].astype(F32), axis=0, keepdims=True)
         small[s, 5 : 5 + HEADS, :] = table[0:HEADS, 0:HALF]
         small[s, 11 : 11 + HEADS, 0 : REL - HALF] = table[0:HEADS, HALF:REL]
-    row_sums[...] = jnp.zeros(row_sums.shape, F32)
-    row_sums[0:1, :] = hidden_sums[1:2, :]
-    row_sums[1:4, :] = mid_sums[0:3, :]
-    row_sums[4:5, :] = gains
-    row_sums[5:6, :] = shifts
     small_low[...] = small[...].astype(BF)
     rows = BLOCK // 4
     for s in range(GROUP):
@@ -625,17 +640,13 @@
         out[2 * lines :, :] = held[s].astype(BF)
 
 
-def row_sum_kernel(ids, mine, other, out):
-    out[...] = mine[...] + other[...]
-
-
-def joined_pack_kernel(ids, keep, came, pair, came_in, tokens, own_mid, vectors, row_sums, row_came, o0, o1, o2, o3, held):
-    total = pair[0:CELLS, :].astype(F32) + came_in[...].astype(F32)
+def joined_pack_kernel(ids, keep, came, pair, came_in, tokens, own_mid, vectors, o0, o1, o2, o3, held):
+    total = pair[0:CELLS, :].astype(F32) + came_in[0:CELLS, :].astype(F32)
     scaled, inverse = norm_stats(tokens[0:CELLS, :].astype(F32))
     e = total * vectors[0:1, :]
     part = e - jnp.mean(e, axis=-1, keepdims=True) - scaled * jnp.mean(e * scaled, axis=-1, keepdims=True)
     result = own_mid[...] + inverse * part
-    totals = row_sums[...] + row_came[...]
+    totals = (pair[2 * CELLS :, :].astype(F32) + came_in[CELLS:, :].astype(F32))[0:8]
     rows = keep.shape[1]
     for s, out in enumerate((o0, o1, o2, o3)):
         out[0:rows, :] = (keep[s].astype(F32) + came[s].astype(F32)).astype(BF)
@@ -673,6 +684,10 @@
 
 def half_sum_kernel(ids, keep, came, out):
     out[...] = (keep[...] + came[...].astype(F32)).astype(BF)
+
+
+def input_sum_kernel(ids, keep, came, out):
+    half_sum_kernel(ids, keep, came, out)
 
 
 def cross_sum_kernel(ids, kept, came, out):
@@ -699,17 +714,15 @@
             ].astype(F32)
 
 
-def finish_joined_kernel(ids, mine, other, out_q, out_o, out_hidden, out_heads, out_table, r0, r1, r2, r3, r4, r5, small, line):
+def finish_joined_kernel(ids, mine, other, out_q, out_o, out_hidden, out_heads, out_table, r0, r1, r2, r3, r4, r5, small):
     x = ids[0]
     for piece, side in ((mine, x), (other, 1 - x)):
         for part in range(3):
             wide_store(out_q, piece[part * QUARTER : (part + 1) * QUARTER, :].astype(F32), side * QUARTER, 9, part * 3)
         wide_store(out_o, piece[3 * QUARTER : 4 * QUARTER, :].astype(F32), side * QUARTER, 3, 0)
         small[pl.ds(aligned(side * SMALL, 8), SMALL), :] = piece[4 * QUARTER : 4 * QUARTER + SMALL, :].astype(F32)
-    line[...] = jnp.zeros(line.shape, F32)
-    line[0:1, :HALF] = small[0:1, :]
-    line[0:1, HALF:] = small[1:2, :]
-    out_hidden[...] = dot_nt(line[...].astype(BF), hidden_perm())[0:1]
+    for k in range(6):
+        out_hidden[k : k + 1, :] = small[k // 3 : k // 3 + 1, (k % 3) * 128 : (k % 3 + 1) * 128]
     out_heads[0:1, :] = small[2:3, :BLOCK]
     out_heads[1:2, :] = small[4:5, :BLOCK]
     out_table[:, :HALF] = small[5 : 5 + HEADS, :]
@@ -722,7 +735,7 @@
         out[...] = total[n : n + 1]
 
 
-CHEAP = (attend_kernel, expand_weights_kernel, ordered_sum_kernel, expand_pack_kernel)
+CHEAP = (couple_kernel, first_weights_kernel, pass_kernel, attend_kernel, expand_weights_kernel, couple_out_kernel, couple_att_kernel, ordered_sum_kernel, expand_pack_kernel)
 
 
 def local_program(dp_size, row_size, col_size):
@@ -756,7 +769,10 @@
         joined_own = query_key_value.reshape(BLOCK // 2, 3, HALF).transpose(1, 0, 2)
         out_own = output_weight.reshape(BLOCK // 2, HALF)
         contract_own = contract_weight.reshape(HALF, HALF)
-        vector_own = jnp.stack([first_gain, first_shift, output_bias, second_gain, second_shift, contract_bias])
+        vectors_own = [
+            vector.reshape(1, BLOCK)
+            for vector in (first_gain, first_shift, output_bias, second_gain, second_shift, contract_bias)
+        ]
         last = []
 
         def step(kernel, outs, scratch, *arrays, **given):
@@ -766,13 +782,14 @@
 
         v = types.SimpleNamespace()
         two = (2 * CELLS, WIDTH)
+        more = (2 * CELLS + 16, WIDTH)
         wide = (TOKENS, WIDTH)
         rows_j = BLOCK + SMALL
 
         def stage_order():
             slots = step(
-                order_kernel, [((FIRST + BLOCK, HALF), BF)] * GROUP, [((GROUP, FIRST, HALF), F32)],
-                vector_own, inputs.reshape(2 * CELLS, HALF), cotangent.reshape(2 * CELLS, HALF),
+                order_kernel, [((FIRST + BLOCK, HALF), BF)] * GROUP, [((GROUP, FIRST, HALF), F32), ((6, BLOCK), F32)],
+                *vectors_own, inputs.reshape(2 * CELLS, HALF), cotangent.reshape(2 * CELLS, HALF),
                 joined_own, out_own, mib=ORDER_MIB,
             )
             v.slots = [slots[0]] + [turn(slots[s], s) for s in range(1, row_size)]
@@ -798,6 +815,7 @@
             v.expand_mine = turn_all(half)
 
         def stage_stack():
+            last.extend(v.tokens[1:] if STACK_TAKES else ())
             (v.expand,) = step(stack_kernel, [((3, BLOCK // 2, WIDTH), BF)], [], *v.expand_mine)
             v.expand_other = swap(v.expand)
 
@@ -811,6 +829,12 @@
                 [((GROUP, 4, BLOCK // 2, HALF), BF)], joined_own, out_own, v.first, v.first_other,
             )
 
+            v.out_across = flip(v.out_w, 2)
+
+        def stage_couple_ow():
+            (both,) = step(couple_out_kernel, [((2, BLOCK, WIDTH), BF)], [], v.out_w, v.out_across)
+            v.out_square = (both, flip(both, 1))
+
         def stage_pass():
             (passed,) = step(pass_kernel, [((HALF, HALF), BF)], [], contract_own)
             v.contract = turn_all(passed)
@@ -819,8 +843,8 @@
             v.x, v.n1, v.q, v.k, v.v, v.p, v.att = step(
                 attend_kernel,
                 [(wide, BF)] * 2 + [((TOKENS, BLOCK), BF)] * 3
-                + [((GROUP, CELLS, STACK), BF), ((ATT + HALF, HALF), BF)],
-                [((GROUP, STACK, BLOCK), BF), ((GROUP, BLOCK, CELLS), F32)], *v.tokens, v.vectors, v.joined_w, query_value_bias, v.bias, v.out_w,
+                + [((GROUP, CELLS, STACK), BF), ((ATT, HALF), BF)],
+                [((GROUP, STACK, BLOCK), BF), ((GROUP, BLOCK, CELLS), F32)], *v.tokens, v.vectors, v.joined_w, query_value_bias, v.bias,
             )
             v.att_across = flip(v.att, 2)
 
@@ -832,14 +856,14 @@
             )
 
         def stage_couple_att():
-            (both,) = step(couple_kernel, [((2, ATT + HALF, HALF), BF)], [], v.att, v.att_across)
+            (both,) = step(couple_att_kernel, [((2, ATT, HALF), BF)], [], v.att, v.att_across)
             v.attended = (both, flip(both, 1))
 
         def stage_expand():
             v.middle, v.n2, v.hidden, v.slope = step(
                 expand_kernel, [(wide, F32), (wide, BF), (wide, BF), (wide, F32)],
                 [(wide, BF), ((WIDTH, WIDTH), BF)],
-                v.x, *v.attended, v.vectors, v.expand_w, v.hidden_bias,
+                v.x, *v.attended, *v.out_square, v.vectors, v.expand_w, v.hidden_bias,
             )
 
         def stage_contract_g():
@@ -883,16 +907,15 @@
             v.far_out = flip(v.pair_out[CELLS:], 2)
 
         def stage_attend_b():
-            v.own_mid, v.mid_low, v.joined_g, v.bias_g, v.keep_i, send, v.mid_sums = step(
+            v.own_mid, v.mid_low, v.joined_g, v.bias_g, v.keep_i, send = step(
                 attend_back_kernel,
                 [((CELLS, WIDTH), F32), (wide, BF), ((3, TOKENS, BLOCK), BF),
-                 ((CELLS, STACK), F32), (two, F32), (two, BF), ((8, WIDTH), F32)],
+                 ((CELLS, STACK), F32), (more, F32), (more, BF)],
                 [((TOKENS, BLOCK), BF), ((GROUP, STACK, BLOCK), BF), ((GROUP, STACK, BLOCK), BF),
-                 ((GROUP, CELLS, STACK), BF), ((GROUP, BLOCK, CELLS), F32)],
+                 ((GROUP, CELLS, STACK), BF), ((GROUP, BLOCK, CELLS), F32), ((16, WIDTH), F32)],
                 v.even_total, v.odd_total, v.middle, v.up, v.vectors, v.out_w,
-                v.q, v.k, v.v, v.p, v.joined_w,
-            )
-            v.send_i = send
+                v.q, v.k, v.v, v.p, v.joined_w, v.x, v.hidden_sums,
+            )
             v.came_i = flip(send, 1)
 
         def stage_contract_s():
@@ -908,24 +931,18 @@
             v.parts_e = give_back(parts)
 
         def stage_in_sum():
-            (v.pair_in,) = step(half_sum_kernel, [(two, BF)], [], v.keep_i, v.came_i)
+            (v.pair_in,) = step(input_sum_kernel, [(more, BF)], [], v.keep_i, v.came_i)
             v.far_in = flip(v.pair_in[CELLS:], 2)
 
         def stage_joined():
-            v.keep_j, send, v.row_sums = step(
-                joined_grads_kernel, [((GROUP, rows_j, HALF), BF)] * 2 + [((8, WIDTH), F32)],
+            v.keep_j, send = step(
+                joined_grads_kernel, [((GROUP, rows_j, HALF), BF)] * 2,
                 [((3, HALF, HALF), BF), ((GROUP, BLOCK // 2, HALF), BF),
                  ((GROUP, 2 * SMALL, HALF), F32), ((GROUP, 2 * SMALL, HALF), BF),
                  ((WIN, 8, STRIP), F32), ((HEADS, WIN, STRIP), F32)],
-                v.n1, v.joined_g, v.att, v.mid_low, v.x, v.keep_i, v.send_i,
-                v.hidden_sums, v.mid_sums, v.bias_g, offset_index.T,
+                v.n1, v.joined_g, v.att, v.mid_low, v.hidden_sums, v.bias_g, offset_index.T,
             )
             v.came_j = swap(send)
-            v.row_came = flip(v.row_sums, 1)
-
-        def stage_rows():
-            (v.row_pair,) = step(row_sum_kernel, [((8, WIDTH), F32)], [], v.row_sums, v.row_came)
-            v.row_far = flip(v.row_pair, 2)
 
         def stage_expand_s():
             (mine,) = step(
@@ -939,7 +956,6 @@
             parts = step(
                 joined_pack_kernel, [((rows_j + EXTRA, HALF), BF)] * GROUP, [((GROUP, EXTRA, HALF), F32)],
                 v.keep_j, v.came_j, v.pair_in, v.far_in, v.x, v.own_mid, v.vectors,
-                v.row_pair, v.row_far,
             )
             v.parts_j = give_back(parts)
 
@@ -968,9 +984,9 @@
         def stage_finish_j():
             v.out_q, v.out_o, v.out_hidden, v.out_heads, v.out_table, *v.rows = step(
                 finish_joined_kernel,
-                [((BLOCK // 2 * 9, 128), F32), ((BLOCK // 2 * 3, 128), F32), ((1, WIDTH), F32),
+                [((BLOCK // 2 * 9, 128), F32), ((BLOCK // 2 * 3, 128), F32), ((6, 128), F32),
                  ((2, BLOCK), F32), ((HEADS, REL), F32)] + [((1, BLOCK), F32)] * 6,
-                [((2 * SMALL, HALF), F32), ((8, WIDTH), F32)],
+                [((2 * SMALL, HALF), F32)],
                 v.mine_j, v.other_j,
             )
 
@@ -978,14 +994,15 @@
         stage_bias()
         stage_unpack()
         stage_half()
-        stage_stack()
-        stage_pass()
         stage_couple()
         stage_first()
+        stage_pass()
+        stage_stack()
         stage_attend()
+        stage_couple_ow()
         stage_expand_w()
+        stage_couple_att()
         stage_contract_w()
-        stage_couple_att()
         stage_expand()
         stage_contract_g()
         stage_hidden()
@@ -994,11 +1011,10 @@
         stage_cross()
         stage_out_sum()
         stage_attend_b()
-        stage_joined()
         stage_contract_s()
         stage_expand_p()
+        stage_joined()
         stage_in_sum()
-        stage_rows()
         stage_expand_s()
         stage_joined_p()
         stage_restore()

time: 171 us -> 166 us (0.971)
  starting transfers between devices: 45.5 us -> 41.9 us
  waiting for transfers between devices: 79.3 us -> 82.8 us
  local copies, waits for them, and re-layouts: 4.28 us -> 1.15 us
    ppermute x6, waiting for transfers between devices: 7.66 us -> 13.2 us  [swap(): return lax.ppermute(value, 'dp', [(i, i ^ bits) for i in range(dp_size)])]
    ppermute x13, starting transfers between devices: 8.88 us -> 6.3 us  [flip(): return lax.ppermute(value, 'col', [(i, i ^ bits) for i in range(col_size)])]
    unnamed x25, local copies, waits for them, and re-layouts: 2.6 us -> 0.83 us
  transfers between devices with their start and end apart: 37 -> 37, of which waited for: 15 -> 17; matrix products, arithmetic and copies ran while one was open for 0% -> 0% of each run, Pallas kernels for 16% -> 16%
where the time goes in v1:
time: 166 us
  waiting for transfers between devices  82.8 us (50%)
  starting transfers between devices  41.9 us (25%)
  Pallas kernels  38.9 us (23%)
    ppermute x18, waiting for transfers between devices, turn(): lax.ppermute(value, 'row', [(i, (i + shift) % row_size) for i in range(ro...  59.3 us
    pallas_call x32, Pallas kernels, run(): pl.pallas_call(body, out_shape=[jax.ShapeDtypeStruct(shape, dtype) for sh...  38.9 us
    ppermute x18, starting transfers between devices, turn(): lax.ppermute(value, 'row', [(i, (i + shift) % row_size) for i in range(ro...  28.9 us
    ppermute x6, waiting for transfers between devices, swap(): return lax.ppermute(value, 'dp', [(i, i ^ bits) for i in range(dp_size)])  13.2 us
    ppermute x13, waiting for transfers between devices, flip(): return lax.ppermute(value, 'col', [(i, i ^ bits) for i in range(col_size)])  10.3 us
    ppermute x6, starting transfers between devices, swap(): return lax.ppermute(value, 'dp', [(i, i ^ bits) for i in range(dp_size)])  6.63 us
    ppermute x13, starting transfers between devices, flip(): return lax.ppermute(value, 'col', [(i, i ^ bits) for i in range(col_size)])  6.3 us
  transfers between devices with their start and end apart: 37, of which 17 were waited for; matrix products, arithmetic and copies ran while one was open for 0% of the time, Pallas kernels for 16%

profile of v1, /device:TPU:0, one launch (start us, length us, event | category | flops | bytes accessed | tf_op | source)
XLA Modules:
  0.0 165.9 jit_solution(5710697331009277654)
XLA Ops:
  0.7 3.4 %order_kernel.1 = (bf16[352,384]{1,0:T(8,128)(2,1)}, bf16[352,384]{1,0:T(8,128)(2,1)}, bf16[352,384]{1,0:T(8,128)(2,1)}, bf16[352,384]{1,0:T(8,128)(2,1)}, f32[8,128]{1,0:T(8,128)}) custom-call(f32[1,192]{1,0:T(1,128)} %bitcast.45, f32[1,192]{1,0:T(1,128)} %bitcast.46, f32[1,192]{1,0:T(1,128)} %bitcast.47, f32[1,192]{1,0:T(1,128)} %bitcast.48, ...), custom_call_target="tpu_custom_call" | custom-call | flops 11000000512 | bytes 36000000 | tf_op jit(solution)/shard_map/order_kernel/pallas_call | solution.py:76
  4.1 3.0 %collective-permute-start = (bf16[352,384]{1,0:T(8,128)(2,1)}, bf16[352,384]{1,0:T(8,128)(2,1)S(1)}, u32[]{:S(2)}, u32[]{:S(2)}) collective-permute-start(bf16[352,384]{1,0:T(8,128)(2,1)} %get-tuple-element.128), channel_id=1, source_target_pairs={{0,4},{4,8},{8,12},{12,0},{1,5},{5,9},{9,13},{13,1},{2,6},{6,10},{... | collective-permute-start | bytes 811016 | tf_op jit(solution)/shard_map/ppermute | solution.py:743
  7.1 2.6 %collective-permute-start.1 = (bf16[352,384]{1,0:T(8,128)(2,1)}, bf16[352,384]{1,0:T(8,128)(2,1)S(1)}, u32[]{:S(2)}, u32[]{:S(2)}) collective-permute-start(bf16[352,384]{1,0:T(8,128)(2,1)} %get-tuple-element.129), channel_id=1, source_target_pairs={{0,8},{4,12},{8,0},{12,4},{1,9},{5,13},{9,1},{13,5},{2,10},{6,14},... | collective-permute-start | bytes 811016 | tf_op jit(solution)/shard_map/ppermute | solution.py:743
  9.7 1.4 collective-permute-start.2
  12.1 1.9 %bias_kernel.1 = (f32[144,896]{1,0:T(8,128)S(1)}, f32[8,128]{1,0:T(8,128)S(1)}) custom-call(f32[6,529]{1,0:T(8,128)S(1)} %bitcast.41, s32[144,144]{1,0:T(8,128)S(1)} %bitcast.36, s32[4,144]{1,0:T(4,128)S(1)} %reshape.119.refs_2_, s32[144,4]{1,0:T(8,128)S(1)} %bitcast.40, f32[8,128]{1,0:T(8,128)S(1)} %copy-done.8), custom_call_target="tpu_custom_call" | custom-call | flops 11000000512 | bytes 36000000 | tf_op jit(solution)/shard_map/bias_kernel/pallas_call | solution.py:76
  14.0 2.7 %collective-permute-done.refs_2_ = bf16[352,384]{1,0:T(8,128)(2,1)S(1)} collective-permute-done((bf16[352,384]{1,0:T(8,128)(2,1)}, bf16[352,384]{1,0:T(8,128)(2,1)S(1)}, u32[]{:S(2)}, u32[]{:S(2)}) %collective-permute-start) | collective-permute-done | bytes 270368 | tf_op jit(solution)/shard_map/ppermute | solution.py:743
  16.8 10.8 %collective-permute-done.1.refs_3_ = bf16[352,384]{1,0:T(8,128)(2,1)S(1)} collective-permute-done((bf16[352,384]{1,0:T(8,128)(2,1)}, bf16[352,384]{1,0:T(8,128)(2,1)S(1)}, u32[]{:S(2)}, u32[]{:S(2)}) %collective-permute-start.1) | collective-permute-done | bytes 270368 | tf_op jit(solution)/shard_map/ppermute | solution.py:743
  27.5 0.9 unpack_kernel.1
  28.5 1.6 collective-permute-start.3
  30.1 1.5 collective-permute-start.5
  31.6 7.3 %collective-permute-start.11 = (bf16[96,768]{1,0:T(8,128)(2,1)S(1)}, bf16[96,768]{1,0:T(8,128)(2,1)S(1)}, u32[]{:S(2)}, u32[]{:S(2)}) collective-permute-start(bf16[96,768]{1,0:T(8,128)(2,1)S(1)} %get-tuple-element.144), channel_id=1, source_target_pairs={{0,12},{4,0},{8,4},{12,8},{1,13},{5,1},{9,5},{13,9},{2,14},{6,2},{... | collective-permute-start | bytes 442376 | tf_op jit(solution)/shard_map/ppermute | solution.py:743
  39.6 0.9 collective-permute-done.3.refs_1_
  40.6 1.2 collective-permute-done.5.refs_3_
  41.8 1.1 first_weights_kernel.1
  43.5 8.5 %collective-permute-done.10.refs_1_ = bf16[96,768]{1,0:T(8,128)(2,1)S(1)} collective-permute-done((bf16[96,768]{1,0:T(8,128)(2,1)S(1)}, bf16[96,768]{1,0:T(8,128)(2,1)S(1)}, u32[]{:S(2)}, u32[]{:S(2)}) %collective-permute-start.10) | collective-permute-done | bytes 147488 | tf_op jit(solution)/shard_map/ppermute | solution.py:743
  53.5 2.0 %collective-permute-start.6 = (bf16[384,384]{1,0:T(8,128)(2,1)S(1)}, bf16[384,384]{1,0:T(8,128)(2,1)S(1)}, u32[]{:S(2)}, u32[]{:S(2)}) collective-permute-start(bf16[384,384]{1,0:T(8,128)(2,1)S(1)} %get-tuple-element.140), channel_id=1, source_target_pairs={{0,4},{4,8},{8,12},{12,0},{1,5},{5,9},{9,13},{13,1},{2,6},{6,10},{... | collective-permute-start | bytes 884744 | tf_op jit(solution)/shard_map/ppermute | solution.py:743
  55.6 3.9 %attend_kernel.1 = (bf16[576,768]{1,0:T(8,128)(2,1)S(1)}, bf16[576,768]{1,0:T(8,128)(2,1)S(1)}, bf16[576,192]{1,0:T(8,128)(2,1)S(1)}, bf16[576,192]{1,0:T(8,128)...) custom-call(bf16[2,288,768]{2,1,0:T(8,128)(2,1)S(1)} %get-tuple-elem, ...), custom_call_target="tpu_custom_call" | custom-call | flops 11000000 | bytes 36000 | tf_op jit(solution)/shard_map/attend_kernel/pallas_call | solution.py:76
  60.1 2.9 %collective-permute-done.13.refs_2_ = bf16[3,96,768]{2,1,0:T(8,128)(2,1)S(1)} collective-permute-done((bf16[3,96,768]{2,1,0:T(8,128)(2,1)S(1)}, bf16[3,96,768]{2,1,0:T(8,128)(2,1)S(1)}, u32[]{:S(2)}, u32[]{:S(2)}) %collective-permute-start.13) | collective-permute-done | bytes 442400 | tf_op jit(solution)/shard_map/ppermute | solution.py:749
  63.1 1.4 expand_weights_kernel.1
  64.5 1.0 collective-permute-done.12.refs_1_
  65.7 13.4 %collective-permute-done.7.refs_2_ = bf16[384,384]{1,0:T(8,128)(2,1)S(1)} collective-permute-done((bf16[384,384]{1,0:T(8,128)(2,1)S(1)}, bf16[384,384]{1,0:T(8,128)(2,1)S(1)}, u32[]{:S(2)}, u32[]{:S(2)}) %collective-permute-start.7) | collective-permute-done | bytes 294944 | tf_op jit(solution)/shard_map/ppermute | solution.py:743
  79.3 3.4 %expand_kernel.1 = (f32[576,768]{1,0:T(8,128)S(1)}, bf16[576,768]{1,0:T(8,128)(2,1)S(1)}, bf16[576,768]{1,0:T(8,128)(2,1)S(1)}, f32[576,768]{1,0:T(8,128)S(1)}, f32[8,128]{1,0:T(8,128)S(1)}) custom-call(bf16[576,768]{1,0:T(8,128)(2,1)S(1)} %get-tuple-element.155.refs_0_.refs_11_.refs_4_, bf16[2,288,384]{2,1,0:T(8,128)(2,1)S(1)} %get-tuple-element.156.refs_1_, ...), custom_call_target="tpu_custom_call" | custom-call | flops 11000000512 | bytes 36000000 | tf_op jit(solution)/shard_map/expand_kernel/pallas_call | solution.py:76
  82.8 1.2 contract_grads_kernel.1
  84.0 1.7 %hidden_back_kernel.1 = (bf16[576,768]{1,0:T(8,128)(2,1)S(1)}, bf16[576,768]{1,0:T(8,128)(2,1)S(1)}, f32[288,768]{1,0:T(8,128)S(1)}, bf16[288,768]{1,0:T(8,128)(2,1)S(1)}, f32[8,128]{1,0:T(8,128)S(1)}) custom-call(bf16[2,288,768]{2,1,0:T(8,128)(2,1)S(1)} %get-tuple-element.136.refs_0_, bf16[2,288,768]{2,1,0:T(8,128)(2,1)S(1)} %collective-permute-done.4.refs_1_, ...), custom_call_target="tpu_custom_call" | custom-call | flops 11000000512 | bytes 36000000 | tf_op jit(solution)/shard_map/hidden_back_kernel/pallas_call | solution.py:76
  85.8 1.6 collective-permute-start.23
  87.4 1.9 %collective-permute-start.24 = (bf16[384,384]{1,0:T(8,128)(2,1)S(1)}, bf16[384,384]{1,0:T(8,128)(2,1)S(1)}, u32[]{:S(2)}, u32[]{:S(2)}) collective-permute-start(bf16[384,384]{1,0:T(8,128)(2,1)S(1)} %get-tuple-element.184), channel_id=1, source_target_pairs={{0,4},{4,8},{8,12},{12,0},{1,5},{5,9},{9,13},{13,1},{2,6},{6,10},{... | collective-permute-start | bytes 884744 | tf_op jit(solution)/shard_map/ppermute | solution.py:743
  89.4 1.6 collective-permute-start.20
  91.0 3.5 %expand_grads_kernel.1 = (bf16[4,96,768]{2,1,0:T(8,128)(2,1)S(1)}, bf16[4,96,768]{2,1,0:T(8,128)(2,1)S(1)}, f32[288,768]{1,0:T(8,128)S(1)}, bf16[288,768]{1,0:T(...) custom-call(bf16[576,768]{1,0:T(8,128)(2,1)S(1)} %get-tuple-element.165.refs_0_.refs_3_, ...), custom_call_target="tpu_custom_call" | custom-call | flops 11000000512 | bytes 36000000 | tf_op jit(solution)/shard_map/expand_grads_kernel/pallas_call | solution.py:76
  94.6 6.6 %collective-permute-done.20.refs_1_ = bf16[288,768]{1,0:T(8,128)(2,1)S(1)} collective-permute-done((bf16[288,768]{1,0:T(8,128)(2,1)S(1)}, bf16[288,768]{1,0:T(8,128)(2,1)S(1)}, u32[]{:S(2)}, u32[]{:S(2)}) %collective-permute-start.20) | collective-permute-done | bytes 442400 | tf_op jit(solution)/shard_map/ppermute | solution.py:746
  101.2 1.3 collective-permute-start.18
  102.8 1.7 %collective-permute-done.25.refs_1_ = bf16[288,768]{1,0:T(8,128)(2,1)S(1)} collective-permute-done((bf16[288,768]{1,0:T(8,128)(2,1)S(1)}, bf16[288,768]{1,0:T(8,128)(2,1)S(1)}, u32[]{:S(2)}, u32[]{:S(2)}) %collective-permute-start.25) | collective-permute-done | bytes 442400 | tf_op jit(solution)/shard_map/ppermute | solution.py:746
  105.2 4.8 %attend_back_kernel.1 = (f32[144,768]{1,0:T(8,128)S(1)}, bf16[576,768]{1,0:T(8,128)(2,1)S(1)}, bf16[3,576,192]{2,1,0:T(8,128)(2,1)S(1)}, f32[144,896]{1,0:T(8,12...) custom-call(bf16[288,768]{1,0:T(8,128)(2,1)S(1)} %get-tuple-element.185.refs_0_, ...), custom_call_target="tpu_custom_call" | custom-call | flops 11000000512 | bytes 36000000 | tf_op jit(solution)/shard_map/attend_back_kernel/pallas_call | solution.py:76
  110.1 3.8 %collective-permute-done.23.refs_2_ = bf16[384,384]{1,0:T(8,128)(2,1)S(1)} collective-permute-done((bf16[384,384]{1,0:T(8,128)(2,1)S(1)}, bf16[384,384]{1,0:T(8,128)(2,1)S(1)}, u32[]{:S(2)}, u32[]{:S(2)}) %collective-permute-start.23) | collective-permute-done | bytes 294944 | tf_op jit(solution)/shard_map/ppermute | solution.py:743
  115.4 2.3 %collective-permute-start.26 = (bf16[272,384]{1,0:T(8,128)(2,1)S(1)}, bf16[272,384]{1,0:T(8,128)(2,1)S(1)}, u32[]{:S(2)}, u32[]{:S(2)}) collective-permute-start(bf16[272,384]{1,0:T(8,128)(2,1)S(1)} %get-tuple-element.195), channel_id=1, source_target_pairs={{0,12},{4,0},{8,4},{12,8},{1,13},{5,1},{9,5},{13,9},{2,14},{6,2},{... | collective-permute-start | bytes 626696 | tf_op jit(solution)/shard_map/ppermute | solution.py:743
  117.8 1.2 collective-permute-start.28
  119.0 4.2 %joined_grads_kernel.1 = (bf16[4,208,384]{2,1,0:T(8,128)(2,1)S(1)}, bf16[4,208,384]{2,1,0:T(8,128)(2,1)S(1)}, f32[8,128]{1,0:T(8,128)S(1)}) custom-call(bf16[576,768]{1,0:T(8,128)(2,1)S(1)} %get-tuple-element.198.refs_0_, bf16[3,576,192]{2,1,0:T(8,128)(2,1)S(1)} %get-tuple-element.199.refs_1_, bf16[288,384]{1,0:T(8,128)(2,1)S(1)} %get-tuple-element.147.refs_0_.refs_2_, ...), custom_call_target="tpu_custom_call" | custom-call | flops 11000000512 | bytes 36000000 | tf_op jit(solution)/shard_map/joined_grads_kernel/pallas_call | solution.py:76
  123.1 1.2 collective-permute-start.29
  124.5 0.9 collective-permute-start.31
  125.4 9.5 %collective-permute-done.27.refs_3_.refs_2_ = bf16[272,384]{1,0:T(8,128)(2,1)S(1)} collective-permute-done((bf16[272,384]{1,0:T(8,128)(2,1)S(1)}, bf16[272,384]{1,0:T(8,128)(2,1)S(1)}, u32[]{:S(2)}, u32[]{:S(2)}) %collective-permute-start.27) | collective-permute-done | bytes 208928 | tf_op jit(solution)/shard_map/ppermute | solution.py:743
  135.2 1.2 collective-permute-start.35
  136.4 3.4 %collective-permute-done.29.refs_1_ = bf16[4,208,384]{2,1,0:T(8,128)(2,1)S(1)} collective-permute-done((bf16[4,208,384]{2,1,0:T(8,128)(2,1)S(1)}, bf16[4,208,384]{2,1,0:T(8,128)(2,1)S(1)}, u32[]{:S(2)}, u32[]{:S(2)}) %collective-permute-start.29) | collective-permute-done | bytes 639008 | tf_op jit(solution)/shard_map/ppermute | solution.py:749
  140.6 3.4 %collective-permute-start.32 = (bf16[288,384]{1,0:T(8,128)(2,1)S(1)}, bf16[288,384]{1,0:T(8,128)(2,1)S(1)}, u32[]{:S(2)}, u32[]{:S(2)}) collective-permute-start(bf16[288,384]{1,0:T(8,128)(2,1)S(1)} %get-tuple-element.216), channel_id=1, source_target_pairs={{0,12},{4,0},{8,4},{12,8},{1,13},{5,1},{9,5},{13,9},{2,14},{6,2},{... | collective-permute-start | bytes 663560 | tf_op jit(solution)/shard_map/ppermute | solution.py:743
  144.6 1.3 restore_kernel.1
  145.9 1.5 collective-permute-done.35.refs_1_
  147.4 1.1 finish_hidden_kernel.1
  148.5 10.6 %collective-permute-done.33.refs_2_ = bf16[288,384]{1,0:T(8,128)(2,1)S(1)} collective-permute-done((bf16[288,384]{1,0:T(8,128)(2,1)S(1)}, bf16[288,384]{1,0:T(8,128)(2,1)S(1)}, u32[]{:S(2)}, u32[]{:S(2)}) %collective-permute-start.33) | collective-permute-done | bytes 221216 | tf_op jit(solution)/shard_map/ppermute | solution.py:743
  160.2 1.4 restore_wide_kernel.1
  161.5 3.3 %collective-permute-done.36.refs_1_ = bf16[224,384]{1,0:T(8,128)(2,1)S(1)} collective-permute-done((bf16[224,384]{1,0:T(8,128)(2,1)S(1)}, bf16[224,384]{1,0:T(8,128)(2,1)S(1)}, u32[]{:S(2)}, u32[]{:S(2)}) %collective-permute-start.36) | collective-permute-done | bytes 172064 | tf_op jit(solution)/shard_map/ppermute | solution.py:749
  (90 shorter events, 11.4 us)
Async XLA Ops:
  0.6 10.4 %copy-start.10 = (s32[24,24]{1,0:T(8,128)S(1)}, s32[24,24]{1,0:T(8,128)}, u32[]{:S(2)}) copy-start(s32[24,24]{1,0:T(8,128)} %param.21) | copy-start | bytes 6916
  0.7 10.7 %copy-start.9 = (s32[144,144]{1,0:T(8,128)S(1)}, s32[144,144]{1,0:T(8,128)}, u32[]{:S(2)}) copy-start(s32[144,144]{1,0:T(8,128)} %param.22) | copy-start | bytes 248836
  0.7 10.8 %copy-start.5 = (f32[529,6]{0,1:T(8,128)S(1)}, f32[529,6]{0,1:T(8,128)}, u32[]{:S(2)}) copy-start(f32[529,6]{0,1:T(8,128)} %param.27) | copy-start | bytes 38092
  4.1 12.7 %collective-permute-start = (bf16[352,384]{1,0:T(8,128)(2,1)}, bf16[352,384]{1,0:T(8,128)(2,1)S(1)}, u32[]{:S(2)}, u32[]{:S(2)}) collective-permute-start(bf16[352,384]{1,0:T(8,128)(2,1)} %get-tuple-element.128), channel_id=1, source_target_pairs={{0,4},{4,8},{8,12},{12,0},{1,5},{5,9},{9,13},{13,1},{2,6},{6,10},{... | collective-permute-start | bytes 811016 | tf_op jit(solution)/shard_map/ppermute | solution.py:743
  7.1 20.4 %collective-permute-start.1 = (bf16[352,384]{1,0:T(8,128)(2,1)}, bf16[352,384]{1,0:T(8,128)(2,1)S(1)}, u32[]{:S(2)}, u32[]{:S(2)}) collective-permute-start(bf16[352,384]{1,0:T(8,128)(2,1)} %get-tuple-element.129), channel_id=1, source_target_pairs={{0,8},{4,12},{8,0},{12,4},{1,9},{5,13},{9,1},{13,5},{2,10},{6,14},... | collective-permute-start | bytes 811016 | tf_op jit(solution)/shard_map/ppermute | solution.py:743
  9.7 17.9 %collective-permute-start.2 = (bf16[352,384]{1,0:T(8,128)(2,1)}, bf16[352,384]{1,0:T(8,128)(2,1)S(1)}, u32[]{:S(2)}, u32[]{:S(2)}) collective-permute-start(bf16[352,384]{1,0:T(8,128)(2,1)} %get-tuple-element.130), channel_id=1, source_target_pairs={{0,12},{4,0},{8,4},{12,8},{1,13},{5,1},{9,5},{13,9},{2,14},{6,2},{... | collective-permute-start | bytes 811016 | tf_op jit(solution)/shard_map/ppermute | solution.py:743
  12.1 15.4 %copy-start.6 = (s32[8]{0:T(128)S(1)}, s32[8]{0:T(128)}, u32[]{:S(2)}) copy-start(s32[8]{0:T(128)} %refs_0_.3) | copy-start | bytes 100
  12.1 15.4 %copy-start.7 = (bf16[352,384]{1,0:T(8,128)(2,1)S(1)}, bf16[352,384]{1,0:T(8,128)(2,1)}, u32[]{:S(2)}) copy-start(bf16[352,384]{1,0:T(8,128)(2,1)} %get-tuple-element.127.refs_1_) | copy-start | bytes 811012
  27.5 4.0 %copy-start.1 = (bf16[192,768]{1,0:T(8,128)(2,1)S(1)}, bf16[192,768]{1,0:T(8,128)(2,1)}, u32[]{:S(2)}) copy-start(bf16[192,768]{1,0:T(8,128)(2,1)} %refs_0_.5) | copy-start | bytes 884740
  28.5 12.1 %collective-permute-start.3 = (bf16[288,768]{1,0:T(8,128)(2,1)S(1)}, bf16[288,768]{1,0:T(8,128)(2,1)S(1)}, u32[]{:S(2)}, u32[]{:S(2)}) collective-permute-start(bf16[288,768]{1,0:T(8,128)(2,1)S(1)} %get-tuple-element.133.refs_0_), channel_id=1, source_target_pairs={{0,2},{1,3},{2,0},{3,1},{4,6},{5,7},{6,4},{7,5},{8,10},{9,11},{10,... | collective-permute-start | bytes 1327112 | tf_op jit(solution)/shard_map/ppermute | solution.py:746
  30.1 11.7 %collective-permute-start.5 = (bf16[3,192,384]{2,1,0:T(8,128)(2,1)S(1)}, bf16[3,192,384]{2,1,0:T(8,128)(2,1)S(1)}, u32[]{:S(2)}, u32[]{:S(2)}) collective-permute-start(bf16[3,192,384]{2,1,0:T(8,128)(2,1)S(1)} %get-tuple-element.137.refs_2_), channel_id=1, source_target_pairs={{0,16},{16,0},{1,17},{17,1},{2,18},{18,2},{3,19},{19,3},{4,20},{20... | collective-permute-start | bytes 1327112 | tf_op jit(solution)/shard_map/ppermute | solution.py:749
  31.6 10.2 %copy-start.2 = (bf16[96,3,1,384]{3,0,2,1:T(8,128)(2,1)S(1)}, bf16[96,3,1,384]{3,0,2,1:T(8,128)(2,1)}, u32[]{:S(2)}) copy-start(bf16[96,3,1,384]{3,0,2,1:T(8,128)(2,1)} %param.25) | copy-start | bytes 663556
  31.6 10.2 %copy-start.3 = (bf16[96,1,384]{2,0,1:T(8,128)(2,1)S(1)}, bf16[96,1,384]{2,0,1:T(8,128)(2,1)}, u32[]{:S(2)}) copy-start(bf16[96,1,384]{2,0,1:T(8,128)(2,1)} %param.28) | copy-start | bytes 221188
  31.6 11.9 %copy-start = (bf16[384,1,384]{2,0,1:T(8,128)(2,1)S(1)}, bf16[384,1,384]{2,0,1:T(8,128)(2,1)}, u32[]{:S(2)}) copy-start(bf16[384,1,384]{2,0,1:T(8,128)(2,1)} %param.34) | copy-start | bytes 884740
  31.6 11.9 %collective-permute-start.11 = (bf16[96,768]{1,0:T(8,128)(2,1)S(1)}, bf16[96,768]{1,0:T(8,128)(2,1)S(1)}, u32[]{:S(2)}, u32[]{:S(2)}) collective-permute-start(bf16[96,768]{1,0:T(8,128)(2,1)S(1)} %get-tuple-element.144), channel_id=1, source_target_pairs={{0,12},{4,0},{8,4},{12,8},{1,13},{5,1},{9,5},{13,9},{2,14},{6,2},{... | collective-permute-start | bytes 442376 | tf_op jit(solution)/shard_map/ppermute | solution.py:743
  38.9 13.1 %collective-permute-start.10 = (bf16[96,768]{1,0:T(8,128)(2,1)S(1)}, bf16[96,768]{1,0:T(8,128)(2,1)S(1)}, u32[]{:S(2)}, u32[]{:S(2)}) collective-permute-start(bf16[96,768]{1,0:T(8,128)(2,1)S(1)} %get-tuple-element.144), channel_id=1, source_target_pairs={{0,8},{4,12},{8,0},{12,4},{1,9},{5,13},{9,1},{13,5},{2,10},{6,14},... | collective-permute-start | bytes 442376 | tf_op jit(solution)/shard_map/ppermute | solution.py:743
  39.4 12.7 %collective-permute-start.9 = (bf16[96,768]{1,0:T(8,128)(2,1)S(1)}, bf16[96,768]{1,0:T(8,128)(2,1)S(1)}, u32[]{:S(2)}, u32[]{:S(2)}) collective-permute-start(bf16[96,768]{1,0:T(8,128)(2,1)S(1)} %get-tuple-element.144), channel_id=1, source_target_pairs={{0,4},{4,8},{8,12},{12,0},{1,5},{5,9},{9,13},{13,1},{2,6},{6,10},{... | collective-permute-start | bytes 442376 | tf_op jit(solution)/shard_map/ppermute | solution.py:743
  42.9 16.6 %collective-permute-start.14 = (bf16[192,768]{1,0:T(8,128)(2,1)S(1)}, bf16[192,768]{1,0:T(8,128)(2,1)S(1)}, u32[]{:S(2)}, u32[]{:S(2)}) collective-permute-start(bf16[192,768]{1,0:T(8,128)(2,1)S(1)} %get-tuple-element.149.refs_0_.refs_5_), channel_id=1, source_target_pairs={{0,2},{1,3},{2,0},{3,1},{4,6},{5,7},{6,4},{7,5},{8,10},{9,11},{10,... | collective-permute-start | bytes 884744 | tf_op jit(solution)/shard_map/ppermute | solution.py:746
  43.5 10.1 %collective-permute-start.4 = (bf16[2,288,768]{2,1,0:T(8,128)(2,1)S(1)}, bf16[2,288,768]{2,1,0:T(8,128)(2,1)S(1)}, u32[]{:S(2)}, u32[]{:S(2)}) collective-permute-start(bf16[2,288,768]{2,1,0:T(8,128)(2,1)S(1)} %get-tuple-element.136.refs_0_), channel_id=1, source_target_pairs={{0,1},{1,0},{2,3},{3,2},{4,5},{5,4},{6,7},{7,6},{8,9},{9,8},{10,11... | collective-permute-start | bytes 2654216 | tf_op jit(solution)/shard_map/ppermute | solution.py:746
  52.0 3.5 %copy-start.4 = (f32[2,192]{1,0:T(2,128)S(1)}, f32[2,192]{1,0:T(2,128)}, u32[]{:S(2)}) copy-start(f32[2,192]{1,0:T(2,128)} %refs_4_.1) | copy-start | bytes 4612
  52.1 11.0 %collective-permute-start.13 = (bf16[3,96,768]{2,1,0:T(8,128)(2,1)S(1)}, bf16[3,96,768]{2,1,0:T(8,128)(2,1)S(1)}, u32[]{:S(2)}, u32[]{:S(2)}) collective-permute-start(bf16[3,96,768]{2,1,0:T(8,128)(2,1)S(1)} %get-tuple-element.148.refs_1_), channel_id=1, source_target_pairs={{0,16},{16,0},{1,17},{17,1},{2,18},{18,2},{3,19},{19,3},{4,20},{20... | collective-permute-start | bytes 1327112 | tf_op jit(solution)/shard_map/ppermute | solution.py:749
  52.7 13.0 %collective-permute-start.8 = (bf16[384,384]{1,0:T(8,128)(2,1)S(1)}, bf16[384,384]{1,0:T(8,128)(2,1)S(1)}, u32[]{:S(2)}, u32[]{:S(2)}) collective-permute-start(bf16[384,384]{1,0:T(8,128)(2,1)S(1)} %get-tuple-element.140), channel_id=1, source_target_pairs={{0,12},{4,0},{8,4},{12,8},{1,13},{5,1},{9,5},{13,9},{2,14},{6,2},{... | collective-permute-start | bytes 884744 | tf_op jit(solution)/shard_map/ppermute | solution.py:743
  52.7 26.4 %collective-permute-start.7 = (bf16[384,384]{1,0:T(8,128)(2,1)S(1)}, bf16[384,384]{1,0:T(8,128)(2,1)S(1)}, u32[]{:S(2)}, u32[]{:S(2)}) collective-permute-start(bf16[384,384]{1,0:T(8,128)(2,1)S(1)} %get-tuple-element.140), channel_id=1, source_target_pairs={{0,8},{4,12},{8,0},{12,4},{1,9},{5,13},{9,1},{13,5},{2,10},{6,14},... | collective-permute-start | bytes 884744 | tf_op jit(solution)/shard_map/ppermute | solution.py:743
  53.5 25.5 %collective-permute-start.6 = (bf16[384,384]{1,0:T(8,128)(2,1)S(1)}, bf16[384,384]{1,0:T(8,128)(2,1)S(1)}, u32[]{:S(2)}, u32[]{:S(2)}) collective-permute-start(bf16[384,384]{1,0:T(8,128)(2,1)S(1)} %get-tuple-element.140), channel_id=1, source_target_pairs={{0,4},{4,8},{8,12},{12,0},{1,5},{5,9},{9,13},{13,1},{2,6},{6,10},{... | collective-permute-start | bytes 884744 | tf_op jit(solution)/shard_map/ppermute | solution.py:743
  55.6 4.5 %copy-start.11 = (f32[768]{0:T(1024)S(1)}, f32[768]{0:T(1024)}, u32[]{:S(2)}) copy-start(f32[768]{0:T(1024)} %param.33) | copy-start | bytes 9220
  59.5 6.0 %collective-permute-start.12 = (bf16[288,384]{1,0:T(8,128)(2,1)S(1)}, bf16[288,384]{1,0:T(8,128)(2,1)S(1)}, u32[]{:S(2)}, u32[]{:S(2)}) collective-permute-start(bf16[288,384]{1,0:T(8,128)(2,1)S(1)} %get-tuple-element.147.refs_0_.refs_2_), channel_id=1, source_target_pairs={{0,2},{1,3},{2,0},{3,1},{4,6},{5,7},{6,4},{7,5},{8,10},{9,11},{10,... | collective-permute-start | bytes 663560 | tf_op jit(solution)/shard_map/ppermute | solution.py:746
  63.1 16.2 %collective-permute-start.16 = (bf16[2,192,768]{2,1,0:T(8,128)(2,1)S(1)}, bf16[2,192,768]{2,1,0:T(8,128)(2,1)S(1)}, u32[]{:S(2)}, u32[]{:S(2)}) collective-permute-start(bf16[2,192,768]{2,1,0:T(8,128)(2,1)S(1)} %get-tuple-element.157.refs_3_), channel_id=1, source_target_pairs={{0,1},{1,0},{2,3},{3,2},{4,5},{5,4},{6,7},{7,6},{8,9},{9,8},{10,11... | collective-permute-start | bytes 1769480 | tf_op jit(solution)/shard_map/ppermute | solution.py:746
  65.6 13.8 %collective-permute-start.15 = (bf16[2,288,384]{2,1,0:T(8,128)(2,1)S(1)}, bf16[2,288,384]{2,1,0:T(8,128)(2,1)S(1)}, u32[]{:S(2)}, u32[]{:S(2)}) collective-permute-start(bf16[2,288,384]{2,1,0:T(8,128)(2,1)S(1)} %get-tuple-element.156.refs_1_), channel_id=1, source_target_pairs={{0,1},{1,0},{2,3},{3,2},{4,5},{5,4},{6,7},{7,6},{8,9},{9,8},{10,11... | collective-permute-start | bytes 1327112 | tf_op jit(solution)/shard_map/ppermute | solution.py:746
  85.7 3.6 %collective-permute-start.17 = (bf16[288,768]{1,0:T(8,128)(2,1)S(1)}, bf16[288,768]{1,0:T(8,128)(2,1)S(1)}, u32[]{:S(2)}, u32[]{:S(2)}) collective-permute-start(bf16[288,768]{1,0:T(8,128)(2,1)S(1)} %get-tuple-element.169), channel_id=1, source_target_pairs={{0,1},{1,0},{2,3},{3,2},{4,5},{5,4},{6,7},{7,6},{8,9},{9,8},{10,11... | collective-permute-start | bytes 1327112 | tf_op jit(solution)/shard_map/ppermute | solution.py:746
  85.8 24.2 %collective-permute-start.22 = (bf16[384,384]{1,0:T(8,128)(2,1)S(1)}, bf16[384,384]{1,0:T(8,128)(2,1)S(1)}, u32[]{:S(2)}, u32[]{:S(2)}) collective-permute-start(bf16[384,384]{1,0:T(8,128)(2,1)S(1)} %get-tuple-element.182), channel_id=1, source_target_pairs={{0,12},{4,0},{8,4},{12,8},{1,13},{5,1},{9,5},{13,9},{2,14},{6,2},{... | collective-permute-start | bytes 884744 | tf_op jit(solution)/shard_map/ppermute | solution.py:743
  85.8 28.0 %collective-permute-start.23 = (bf16[384,384]{1,0:T(8,128)(2,1)S(1)}, bf16[384,384]{1,0:T(8,128)(2,1)S(1)}, u32[]{:S(2)}, u32[]{:S(2)}) collective-permute-start(bf16[384,384]{1,0:T(8,128)(2,1)S(1)} %get-tuple-element.183), channel_id=1, source_target_pairs={{0,8},{4,12},{8,0},{12,4},{1,9},{5,13},{9,1},{13,5},{2,10},{6,14},... | collective-permute-start | bytes 884744 | tf_op jit(solution)/shard_map/ppermute | solution.py:743
  87.4 26.5 %collective-permute-start.24 = (bf16[384,384]{1,0:T(8,128)(2,1)S(1)}, bf16[384,384]{1,0:T(8,128)(2,1)S(1)}, u32[]{:S(2)}, u32[]{:S(2)}) collective-permute-start(bf16[384,384]{1,0:T(8,128)(2,1)S(1)} %get-tuple-element.184), channel_id=1, source_target_pairs={{0,4},{4,8},{8,12},{12,0},{1,5},{5,9},{9,13},{13,1},{2,6},{6,10},{... | collective-permute-start | bytes 884744 | tf_op jit(solution)/shard_map/ppermute | solution.py:743
  89.4 11.7 %collective-permute-start.20 = (bf16[288,768]{1,0:T(8,128)(2,1)S(1)}, bf16[288,768]{1,0:T(8,128)(2,1)S(1)}, u32[]{:S(2)}, u32[]{:S(2)}) collective-permute-start(bf16[288,768]{1,0:T(8,128)(2,1)S(1)} %get-tuple-element.177.refs_0_), channel_id=1, source_target_pairs={{0,2},{1,3},{2,0},{3,1},{4,6},{5,7},{6,4},{7,5},{8,10},{9,11},{10,... | collective-permute-start | bytes 1327112 | tf_op jit(solution)/shard_map/ppermute | solution.py:746
  94.6 8.1 %collective-permute-start.19 = (bf16[288,768]{1,0:T(8,128)(2,1)S(1)}, bf16[288,768]{1,0:T(8,128)(2,1)S(1)}, u32[]{:S(2)}, u32[]{:S(2)}) collective-permute-start(bf16[288,768]{1,0:T(8,128)(2,1)S(1)} %get-tuple-element.176), channel_id=1, source_target_pairs={{0,1},{1,0},{2,3},{3,2},{4,5},{5,4},{6,7},{7,6},{8,9},{9,8},{10,11... | collective-permute-start | bytes 1327112 | tf_op jit(solution)/shard_map/ppermute | solution.py:746
  101.2 13.9 %collective-permute-start.18 = (bf16[4,96,768]{2,1,0:T(8,128)(2,1)S(1)}, bf16[4,96,768]{2,1,0:T(8,128)(2,1)S(1)}, u32[]{:S(2)}, u32[]{:S(2)}) collective-permute-start(bf16[4,96,768]{2,1,0:T(8,128)(2,1)S(1)} %get-tuple-element.173), channel_id=1, source_target_pairs={{0,16},{16,0},{1,17},{17,1},{2,18},{18,2},{3,19},{19,3},{4,20},{20... | collective-permute-start | bytes 1769480 | tf_op jit(solution)/shard_map/ppermute | solution.py:749
  102.7 1.9 %collective-permute-start.25 = (bf16[288,768]{1,0:T(8,128)(2,1)S(1)}, bf16[288,768]{1,0:T(8,128)(2,1)S(1)}, u32[]{:S(2)}, u32[]{:S(2)}) collective-permute-start(bf16[288,768]{1,0:T(8,128)(2,1)S(1)} %get-tuple-element.185.refs_0_), channel_id=1, source_target_pairs={{0,1},{1,0},{2,3},{3,2},{4,5},{5,4},{6,7},{7,6},{8,9},{9,8},{10,11... | collective-permute-start | bytes 1327112 | tf_op jit(solution)/shard_map/ppermute | solution.py:746
  104.5 10.6 %collective-permute-start.21 = (bf16[144,768]{1,0:T(8,128)(2,1)S(1)}, bf16[144,768]{1,0:T(8,128)(2,1)S(1)}, u32[]{:S(2)}, u32[]{:S(2)}) collective-permute-start(bf16[144,768]{1,0:T(8,128)(2,1)S(1)} %slice.6), channel_id=1, source_target_pairs={{0,2},{1,3},{2,0},{3,1},{4,6},{5,7},{6,4},{7,5},{8,10},{9,11},{10,... | collective-permute-start | bytes 663560 | tf_op jit(solution)/shard_map/ppermute | solution.py:746
  110.0 14.3 %collective-permute-start.30 = (bf16[304,768]{1,0:T(8,128)(2,1)S(1)}, bf16[304,768]{1,0:T(8,128)(2,1)S(1)}, u32[]{:S(2)}, u32[]{:S(2)}) collective-permute-start(bf16[304,768]{1,0:T(8,128)(2,1)S(1)} %get-tuple-element.206), channel_id=1, source_target_pairs={{0,1},{1,0},{2,3},{3,2},{4,5},{5,4},{6,7},{7,6},{8,9},{9,8},{10,11... | collective-permute-start | bytes 1400840 | tf_op jit(solution)/shard_map/ppermute | solution.py:746
  115.4 10.0 %collective-permute-start.26 = (bf16[272,384]{1,0:T(8,128)(2,1)S(1)}, bf16[272,384]{1,0:T(8,128)(2,1)S(1)}, u32[]{:S(2)}, u32[]{:S(2)}) collective-permute-start(bf16[272,384]{1,0:T(8,128)(2,1)S(1)} %get-tuple-element.195), channel_id=1, source_target_pairs={{0,12},{4,0},{8,4},{12,8},{1,13},{5,1},{9,5},{13,9},{2,14},{6,2},{... | collective-permute-start | bytes 626696 | tf_op jit(solution)/shard_map/ppermute | solution.py:743
  117.8 17.2 %collective-permute-start.27 = (bf16[272,384]{1,0:T(8,128)(2,1)S(1)}, bf16[272,384]{1,0:T(8,128)(2,1)S(1)}, u32[]{:S(2)}, u32[]{:S(2)}) collective-permute-start(bf16[272,384]{1,0:T(8,128)(2,1)S(1)} %get-tuple-element.196), channel_id=1, source_target_pairs={{0,8},{4,12},{8,0},{12,4},{1,9},{5,13},{9,1},{13,5},{2,10},{6,14},... | collective-permute-start | bytes 626696 | tf_op jit(solution)/shard_map/ppermute | solution.py:743
  117.8 17.2 %collective-permute-start.28 = (bf16[272,384]{1,0:T(8,128)(2,1)S(1)}, bf16[272,384]{1,0:T(8,128)(2,1)S(1)}, u32[]{:S(2)}, u32[]{:S(2)}) collective-permute-start(bf16[272,384]{1,0:T(8,128)(2,1)S(1)} %get-tuple-element.197), channel_id=1, source_target_pairs={{0,4},{4,8},{8,12},{12,0},{1,5},{5,9},{9,13},{13,1},{2,6},{6,10},{... | collective-permute-start | bytes 626696 | tf_op jit(solution)/shard_map/ppermute | solution.py:743
  123.1 16.7 %collective-permute-start.29 = (bf16[4,208,384]{2,1,0:T(8,128)(2,1)S(1)}, bf16[4,208,384]{2,1,0:T(8,128)(2,1)S(1)}, u32[]{:S(2)}, u32[]{:S(2)}) collective-permute-start(bf16[4,208,384]{2,1,0:T(8,128)(2,1)S(1)} %get-tuple-element.204), channel_id=1, source_target_pairs={{0,16},{16,0},{1,17},{17,1},{2,18},{18,2},{3,19},{19,3},{4,20},{20... | collective-permute-start | bytes 1916936 | tf_op jit(solution)/shard_map/ppermute | solution.py:749
  124.5 15.4 %collective-permute-start.31 = (bf16[160,768]{1,0:T(8,128)(2,1)S(1)}, bf16[160,768]{1,0:T(8,128)(2,1)S(1)}, u32[]{:S(2)}, u32[]{:S(2)}) collective-permute-start(bf16[160,768]{1,0:T(8,128)(2,1)S(1)} %slice.7), channel_id=1, source_target_pairs={{0,2},{1,3},{2,0},{3,1},{4,6},{5,7},{6,4},{7,5},{8,10},{9,11},{10,... | collective-permute-start | bytes 737288 | tf_op jit(solution)/shard_map/ppermute | solution.py:746
  135.2 12.2 %collective-permute-start.35 = (bf16[576,384]{1,0:T(8,128)(2,1)S(1)}, bf16[576,384]{1,0:T(8,128)(2,1)S(1)}, u32[]{:S(2)}, u32[]{:S(2)}) collective-permute-start(bf16[576,384]{1,0:T(8,128)(2,1)S(1)} %get-tuple-element.219.refs_0_), channel_id=1, source_target_pairs={{0,16},{16,0},{1,17},{17,1},{2,18},{18,2},{3,19},{19,3},{4,20},{20... | collective-permute-start | bytes 1327112 | tf_op jit(solution)/shard_map/ppermute | solution.py:749
  140.6 7.9 %collective-permute-start.32 = (bf16[288,384]{1,0:T(8,128)(2,1)S(1)}, bf16[288,384]{1,0:T(8,128)(2,1)S(1)}, u32[]{:S(2)}, u32[]{:S(2)}) collective-permute-start(bf16[288,384]{1,0:T(8,128)(2,1)S(1)} %get-tuple-element.216), channel_id=1, source_target_pairs={{0,12},{4,0},{8,4},{12,8},{1,13},{5,1},{9,5},{13,9},{2,14},{6,2},{... | collective-permute-start | bytes 663560 | tf_op jit(solution)/shard_map/ppermute | solution.py:743
  144.0 15.2 %collective-permute-start.33 = (bf16[288,384]{1,0:T(8,128)(2,1)S(1)}, bf16[288,384]{1,0:T(8,128)(2,1)S(1)}, u32[]{:S(2)}, u32[]{:S(2)}) collective-permute-start(bf16[288,384]{1,0:T(8,128)(2,1)S(1)} %get-tuple-element.217), channel_id=1, source_target_pairs={{0,8},{4,12},{8,0},{12,4},{1,9},{5,13},{9,1},{13,5},{2,10},{6,14},... | collective-permute-start | bytes 663560 | tf_op jit(solution)/shard_map/ppermute | solution.py:743
  144.0 15.2 %collective-permute-start.34 = (bf16[288,384]{1,0:T(8,128)(2,1)S(1)}, bf16[288,384]{1,0:T(8,128)(2,1)S(1)}, u32[]{:S(2)}, u32[]{:S(2)}) collective-permute-start(bf16[288,384]{1,0:T(8,128)(2,1)S(1)} %get-tuple-element.218), channel_id=1, source_target_pairs={{0,4},{4,8},{8,12},{12,0},{1,5},{5,9},{9,13},{13,1},{2,6},{6,10},{... | collective-permute-start | bytes 663560 | tf_op jit(solution)/shard_map/ppermute | solution.py:743
  159.4 5.5 %collective-permute-start.36 = (bf16[224,384]{1,0:T(8,128)(2,1)S(1)}, bf16[224,384]{1,0:T(8,128)(2,1)S(1)}, u32[]{:S(2)}, u32[]{:S(2)}) collective-permute-start(bf16[224,384]{1,0:T(8,128)(2,1)S(1)} %get-tuple-element.224.refs_0_), channel_id=1, source_target_pairs={{0,16},{16,0},{1,17},{17,1},{2,18},{18,2},{3,19},{19,3},{4,20},{20... | collective-permute-start | bytes 516104 | tf_op jit(solution)/shard_map/ppermute | solution.py:749
  (1 other events, 0.7 us)

commit v2 on v1

--- a/solution.py
+++ b/solution.py
@@ -497,6 +497,11 @@
     found = dot_nt(sums[...].astype(BF), perm)
     sums[0:1, :] = found[0:1] + found[1:2] + found[2:3]
     sums[1:2, :] = jnp.sum(upstream[0:CELLS, :].astype(F32), axis=0, keepdims=True)
+
+
+def expand_both_kernel(ids, *refs):
+    expand_kernel(ids, *refs[0:8], *refs[10:14], *refs[18:20])
+    contract_grads_kernel(ids, *refs[8:10], refs[12], *refs[14:18], refs[20])
 
 
 def attend_back_kernel(ids, *refs):
@@ -756,10 +761,10 @@
         return value
 
     def turn_all(value):
-        return [turn(value, s) for s in range(1, row_size)]
+        return [turn(value, s) for s in range(row_size - 1, 0, -1)][::-1]
 
     def give_back(slots):
-        return [slots[0]] + [turn(slots[s], -s) for s in range(1, row_size)]
+        return [slots[0]] + [turn(slots[s], -s) for s in range(row_size - 1, 0, -1)][::-1]
 
     def local(
         inputs, cotangent, slot_mask, region_ids, offset_index, first_gain, first_shift,
@@ -792,7 +797,7 @@
                 *vectors_own, inputs.reshape(2 * CELLS, HALF), cotangent.reshape(2 * CELLS, HALF),
                 joined_own, out_own, mib=ORDER_MIB,
             )
-            v.slots = [slots[0]] + [turn(slots[s], s) for s in range(1, row_size)]
+            v.slots = [slots[0]] + [turn(slots[s], s) for s in range(row_size - 1, 0, -1)][::-1]
 
         def stage_bias():
             labels = region_ids.reshape(2, WIN, 2, WIN).transpose(0, 2, 1, 3).reshape(GROUP, CELLS)
@@ -860,15 +865,10 @@
             v.attended = (both, flip(both, 1))
 
         def stage_expand():
-            v.middle, v.n2, v.hidden, v.slope = step(
-                expand_kernel, [(wide, F32), (wide, BF), (wide, BF), (wide, F32)],
-                [(wide, BF), ((WIDTH, WIDTH), BF)],
-                v.x, *v.attended, *v.out_square, v.vectors, v.expand_w, v.hidden_bias,
-            )
-
-        def stage_contract_g():
-            parts = step(
-                contract_grads_kernel, [((HALF, HALF), BF)] * GROUP, [(wide, BF)], *v.tokens, v.hidden
+            v.middle, v.n2, v.hidden, v.slope, *parts = step(
+                expand_both_kernel, [(wide, F32), (wide, BF), (wide, BF), (wide, F32)] + [((HALF, HALF), BF)] * GROUP,
+                [(wide, BF), ((WIDTH, WIDTH), BF), (wide, BF)],
+                v.x, *v.attended, *v.out_square, v.vectors, v.expand_w, v.hidden_bias, *v.tokens,
             )
             v.parts_c = give_back(parts)
 
@@ -992,8 +992,8 @@
 
         stage_order()
         stage_bias()
+        stage_half()
         stage_unpack()
-        stage_half()
         stage_couple()
         stage_first()
         stage_pass()
@@ -1004,7 +1004,6 @@
         stage_couple_att()
         stage_contract_w()
         stage_expand()
-        stage_contract_g()
         stage_hidden()
         stage_half_sum()
         stage_expand_g()

time: 166 us -> 166 us (level)
    pallas_call x32 -> x31, Pallas kernels: 38.9 us -> 38.7 us  [run(): pl.pallas_call(body, out_shape=[jax.ShapeDtypeStruct(shape, dtype) for sh...]
where the time goes in v2:
time: 166 us
  waiting for transfers between devices  83.2 us (50%)
  starting transfers between devices  41.7 us (25%)
  Pallas kernels  38.7 us (23%)
    ppermute x18, waiting for transfers between devices, turn(): lax.ppermute(value, 'row', [(i, (i + shift) % row_size) for i in range(ro...  59.4 us
    pallas_call x31, Pallas kernels, run(): pl.pallas_call(body, out_shape=[jax.ShapeDtypeStruct(shape, dtype) for sh...  38.7 us
    ppermute x18, starting transfers between devices, turn(): lax.ppermute(value, 'row', [(i, (i + shift) % row_size) for i in range(ro...  28.8 us
    ppermute x6, waiting for transfers between devices, swap(): return lax.ppermute(value, 'dp', [(i, i ^ bits) for i in range(dp_size)])  13.3 us
    ppermute x13, waiting for transfers between devices, flip(): return lax.ppermute(value, 'col', [(i, i ^ bits) for i in range(col_size)])  10.4 us
    ppermute x13, starting transfers between devices, flip(): return lax.ppermute(value, 'col', [(i, i ^ bits) for i in range(col_size)])  6.42 us
    ppermute x6, starting transfers between devices, swap(): return lax.ppermute(value, 'dp', [(i, i ^ bits) for i in range(dp_size)])  6.42 us
  transfers between devices with their start and end apart: 37, of which 17 were waited for; matrix products, arithmetic and copies ran while one was open for 0% of the time, Pallas kernels for 16%

profile of v2, /device:TPU:0, one launch (start us, length us, event | category | flops | bytes accessed | tf_op | source)
XLA Modules:
  0.0 165.9 jit_solution(953654148261585116)
XLA Ops:
  0.7 3.4 %order_kernel.1 = (bf16[352,384]{1,0:T(8,128)(2,1)}, bf16[352,384]{1,0:T(8,128)(2,1)}, bf16[352,384]{1,0:T(8,128)(2,1)}, bf16[352,384]{1,0:T(8,128)(2,1)}, f32[8,128]{1,0:T(8,128)}) custom-call(f32[1,192]{1,0:T(1,128)} %bitcast.45, f32[1,192]{1,0:T(1,128)} %bitcast.46, f32[1,192]{1,0:T(1,128)} %bitcast.47, f32[1,192]{1,0:T(1,128)} %bitcast.48, ...), custom_call_target="tpu_custom_call" | custom-call | flops 11000000512 | bytes 36000000 | tf_op jit(solution)/shard_map/order_kernel/pallas_call | solution.py:76
  4.1 3.0 %collective-permute-start = (bf16[352,384]{1,0:T(8,128)(2,1)}, bf16[352,384]{1,0:T(8,128)(2,1)S(1)}, u32[]{:S(2)}, u32[]{:S(2)}) collective-permute-start(bf16[352,384]{1,0:T(8,128)(2,1)} %get-tuple-element.127), channel_id=1, source_target_pairs={{0,4},{4,8},{8,12},{12,0},{1,5},{5,9},{9,13},{13,1},{2,6},{6,10},{... | collective-permute-start | bytes 811016 | tf_op jit(solution)/shard_map/ppermute | solution.py:748
  7.1 2.6 %collective-permute-start.1 = (bf16[352,384]{1,0:T(8,128)(2,1)}, bf16[352,384]{1,0:T(8,128)(2,1)S(1)}, u32[]{:S(2)}, u32[]{:S(2)}) collective-permute-start(bf16[352,384]{1,0:T(8,128)(2,1)} %get-tuple-element.128), channel_id=1, source_target_pairs={{0,8},{4,12},{8,0},{12,4},{1,9},{5,13},{9,1},{13,5},{2,10},{6,14},... | collective-permute-start | bytes 811016 | tf_op jit(solution)/shard_map/ppermute | solution.py:748
  9.7 1.4 collective-permute-start.2
  12.1 1.9 %bias_kernel.1 = (f32[144,896]{1,0:T(8,128)S(1)}, f32[8,128]{1,0:T(8,128)S(1)}) custom-call(f32[6,529]{1,0:T(8,128)S(1)} %bitcast.41, s32[144,144]{1,0:T(8,128)S(1)} %bitcast.36, s32[4,144]{1,0:T(4,128)S(1)} %reshape.119.refs_2_, s32[144,4]{1,0:T(8,128)S(1)} %bitcast.40, f32[8,128]{1,0:T(8,128)S(1)} %copy-done.8), custom_call_target="tpu_custom_call" | custom-call | flops 11000000512 | bytes 36000000 | tf_op jit(solution)/shard_map/bias_kernel/pallas_call | solution.py:76
  14.1 2.6 %collective-permute-done.refs_2_ = bf16[352,384]{1,0:T(8,128)(2,1)S(1)} collective-permute-done((bf16[352,384]{1,0:T(8,128)(2,1)}, bf16[352,384]{1,0:T(8,128)(2,1)S(1)}, u32[]{:S(2)}, u32[]{:S(2)}) %collective-permute-start) | collective-permute-done | bytes 270368 | tf_op jit(solution)/shard_map/ppermute | solution.py:748
  16.8 10.8 %collective-permute-done.1.refs_3_ = bf16[352,384]{1,0:T(8,128)(2,1)S(1)} collective-permute-done((bf16[352,384]{1,0:T(8,128)(2,1)}, bf16[352,384]{1,0:T(8,128)(2,1)S(1)}, u32[]{:S(2)}, u32[]{:S(2)}) %collective-permute-start.1) | collective-permute-done | bytes 270368 | tf_op jit(solution)/shard_map/ppermute | solution.py:748
  27.5 0.9 unpack_kernel.1
  28.5 1.6 collective-permute-start.3
  30.1 1.5 collective-permute-start.5
  31.6 7.3 %collective-permute-start.11 = (bf16[96,768]{1,0:T(8,128)(2,1)S(1)}, bf16[96,768]{1,0:T(8,128)(2,1)S(1)}, u32[]{:S(2)}, u32[]{:S(2)}) collective-permute-start(bf16[96,768]{1,0:T(8,128)(2,1)S(1)} %get-tuple-element.143), channel_id=1, source_target_pairs={{0,12},{4,0},{8,4},{12,8},{1,13},{5,1},{9,5},{13,9},{2,14},{6,2},{... | collective-permute-start | bytes 442376 | tf_op jit(solution)/shard_map/ppermute | solution.py:748
  39.4 1.1 collective-permute-done.3.refs_1_
  40.6 1.2 collective-permute-done.5.refs_3_
  41.8 1.1 first_weights_kernel.1
  43.5 8.4 %collective-permute-done.10.refs_1_ = bf16[96,768]{1,0:T(8,128)(2,1)S(1)} collective-permute-done((bf16[96,768]{1,0:T(8,128)(2,1)S(1)}, bf16[96,768]{1,0:T(8,128)(2,1)S(1)}, u32[]{:S(2)}, u32[]{:S(2)}) %collective-permute-start.10) | collective-permute-done | bytes 147488 | tf_op jit(solution)/shard_map/ppermute | solution.py:748
  53.5 2.0 %collective-permute-start.6 = (bf16[384,384]{1,0:T(8,128)(2,1)S(1)}, bf16[384,384]{1,0:T(8,128)(2,1)S(1)}, u32[]{:S(2)}, u32[]{:S(2)}) collective-permute-start(bf16[384,384]{1,0:T(8,128)(2,1)S(1)} %get-tuple-element.139), channel_id=1, source_target_pairs={{0,4},{4,8},{8,12},{12,0},{1,5},{5,9},{9,13},{13,1},{2,6},{6,10},{... | collective-permute-start | bytes 884744 | tf_op jit(solution)/shard_map/ppermute | solution.py:748
  55.5 3.9 %attend_kernel.1 = (bf16[576,768]{1,0:T(8,128)(2,1)S(1)}, bf16[576,768]{1,0:T(8,128)(2,1)S(1)}, bf16[576,192]{1,0:T(8,128)(2,1)S(1)}, bf16[576,192]{1,0:T(8,128)...) custom-call(bf16[2,288,768]{2,1,0:T(8,128)(2,1)S(1)} %get-tuple-elem, ...), custom_call_target="tpu_custom_call" | custom-call | flops 11000000 | bytes 36000 | tf_op jit(solution)/shard_map/attend_kernel/pallas_call | solution.py:76
  60.0 3.0 %collective-permute-done.13.refs_2_ = bf16[3,96,768]{2,1,0:T(8,128)(2,1)S(1)} collective-permute-done((bf16[3,96,768]{2,1,0:T(8,128)(2,1)S(1)}, bf16[3,96,768]{2,1,0:T(8,128)(2,1)S(1)}, u32[]{:S(2)}, u32[]{:S(2)}) %collective-permute-start.13) | collective-permute-done | bytes 442400 | tf_op jit(solution)/shard_map/ppermute | solution.py:754
  63.1 1.4 expand_weights_kernel.1
  64.5 0.9 collective-permute-done.12.refs_1_
  65.6 13.5 %collective-permute-done.7.refs_2_ = bf16[384,384]{1,0:T(8,128)(2,1)S(1)} collective-permute-done((bf16[384,384]{1,0:T(8,128)(2,1)S(1)}, bf16[384,384]{1,0:T(8,128)(2,1)S(1)}, u32[]{:S(2)}, u32[]{:S(2)}) %collective-permute-start.7) | collective-permute-done | bytes 294944 | tf_op jit(solution)/shard_map/ppermute | solution.py:748
  79.4 4.6 %expand_both_kernel.1 = (f32[576,768]{1,0:T(8,128)S(1)}, bf16[576,768]{1,0:T(8,128)(2,1)S(1)}, bf16[576,768]{1,0:T(8,128)(2,1)S(1)}, f32[576,768]{1,0:T(8,128)S(...) custom-call(bf16[576,768]{1,0:T(8,128)(2,1)S(1)} %get-tuple-element., ...), custom_call_target="tpu_custom_call" | custom-call | flops 11000000512 | bytes 36000000 | tf_op jit(solution)/shard_map/expand_both_kernel/pallas_call | solution.py:76
  84.0 1.7 %hidden_back_kernel.1 = (bf16[576,768]{1,0:T(8,128)(2,1)S(1)}, bf16[576,768]{1,0:T(8,128)(2,1)S(1)}, f32[288,768]{1,0:T(8,128)S(1)}, bf16[288,768]{1,0:T(8,128)(2,1)S(1)}, f32[8,128]{1,0:T(8,128)S(1)}) custom-call(bf16[2,288,768]{2,1,0:T(8,128)(2,1)S(1)} %get-tuple-element.135.refs_0_.refs_8_, ...), custom_call_target="tpu_custom_call" | custom-call | flops 11000000512 | bytes 36000000 | tf_op jit(solution)/shard_map/hidden_back_kernel/pallas_call | solution.py:76
  85.8 1.6 collective-permute-start.23
  87.4 1.9 %collective-permute-start.24 = (bf16[384,384]{1,0:T(8,128)(2,1)S(1)}, bf16[384,384]{1,0:T(8,128)(2,1)S(1)}, u32[]{:S(2)}, u32[]{:S(2)}) collective-permute-start(bf16[384,384]{1,0:T(8,128)(2,1)S(1)} %get-tuple-element.182), channel_id=1, source_target_pairs={{0,4},{4,8},{8,12},{12,0},{1,5},{5,9},{9,13},{13,1},{2,6},{6,10},{... | collective-permute-start | bytes 884744 | tf_op jit(solution)/shard_map/ppermute | solution.py:748
  89.4 1.6 collective-permute-start.20
  91.0 3.4 %expand_grads_kernel.1 = (bf16[4,96,768]{2,1,0:T(8,128)(2,1)S(1)}, bf16[4,96,768]{2,1,0:T(8,128)(2,1)S(1)}, f32[288,768]{1,0:T(8,128)S(1)}, bf16[288,768]{1,0:T(...) custom-call(bf16[576,768]{1,0:T(8,128)(2,1)S(1)} %get-tuple-element.162.refs_0_.refs_3_, ...), custom_call_target="tpu_custom_call" | custom-call | flops 11000000512 | bytes 36000000 | tf_op jit(solution)/shard_map/expand_grads_kernel/pallas_call | solution.py:76
  94.5 6.7 %collective-permute-done.20.refs_1_ = bf16[288,768]{1,0:T(8,128)(2,1)S(1)} collective-permute-done((bf16[288,768]{1,0:T(8,128)(2,1)S(1)}, bf16[288,768]{1,0:T(8,128)(2,1)S(1)}, u32[]{:S(2)}, u32[]{:S(2)}) %collective-permute-start.20) | collective-permute-done | bytes 442400 | tf_op jit(solution)/shard_map/ppermute | solution.py:751
  101.1 1.3 collective-permute-start.18
  102.7 1.7 %collective-permute-done.25.refs_1_ = bf16[288,768]{1,0:T(8,128)(2,1)S(1)} collective-permute-done((bf16[288,768]{1,0:T(8,128)(2,1)S(1)}, bf16[288,768]{1,0:T(8,128)(2,1)S(1)}, u32[]{:S(2)}, u32[]{:S(2)}) %collective-permute-start.25) | collective-permute-done | bytes 442400 | tf_op jit(solution)/shard_map/ppermute | solution.py:751
  105.1 4.7 %attend_back_kernel.1 = (f32[144,768]{1,0:T(8,128)S(1)}, bf16[576,768]{1,0:T(8,128)(2,1)S(1)}, bf16[3,576,192]{2,1,0:T(8,128)(2,1)S(1)}, f32[144,896]{1,0:T(8,12...) custom-call(bf16[288,768]{1,0:T(8,128)(2,1)S(1)} %get-tuple-element.183.refs_0_, ...), custom_call_target="tpu_custom_call" | custom-call | flops 11000000512 | bytes 36000000 | tf_op jit(solution)/shard_map/attend_back_kernel/pallas_call | solution.py:76
  109.9 3.9 %collective-permute-done.23.refs_2_ = bf16[384,384]{1,0:T(8,128)(2,1)S(1)} collective-permute-done((bf16[384,384]{1,0:T(8,128)(2,1)S(1)}, bf16[384,384]{1,0:T(8,128)(2,1)S(1)}, u32[]{:S(2)}, u32[]{:S(2)}) %collective-permute-start.23) | collective-permute-done | bytes 294944 | tf_op jit(solution)/shard_map/ppermute | solution.py:748
  115.4 2.3 %collective-permute-start.26 = (bf16[272,384]{1,0:T(8,128)(2,1)S(1)}, bf16[272,384]{1,0:T(8,128)(2,1)S(1)}, u32[]{:S(2)}, u32[]{:S(2)}) collective-permute-start(bf16[272,384]{1,0:T(8,128)(2,1)S(1)} %get-tuple-element.193), channel_id=1, source_target_pairs={{0,12},{4,0},{8,4},{12,8},{1,13},{5,1},{9,5},{13,9},{2,14},{6,2},{... | collective-permute-start | bytes 626696 | tf_op jit(solution)/shard_map/ppermute | solution.py:748
  117.8 1.2 collective-permute-start.28
  118.9 4.2 %joined_grads_kernel.1 = (bf16[4,208,384]{2,1,0:T(8,128)(2,1)S(1)}, bf16[4,208,384]{2,1,0:T(8,128)(2,1)S(1)}, f32[8,128]{1,0:T(8,128)S(1)}) custom-call(bf16[576,768]{1,0:T(8,128)(2,1)S(1)} %get-tuple-element.196.refs_0_, bf16[3,576,192]{2,1,0:T(8,128)(2,1)S(1)} %get-tuple-element.197.refs_1_, bf16[288,384]{1,0:T(8,128)(2,1)S(1)} %get-tuple-element.146.refs_0_.refs_2_, ...), custom_call_target="tpu_custom_call" | custom-call | flops 11000000512 | bytes 36000000 | tf_op jit(solution)/shard_map/joined_grads_kernel/pallas_call | solution.py:76
  123.1 1.1 collective-permute-start.29
  124.4 1.1 collective-permute-start.31
  125.4 9.5 %collective-permute-done.27.refs_3_.refs_2_ = bf16[272,384]{1,0:T(8,128)(2,1)S(1)} collective-permute-done((bf16[272,384]{1,0:T(8,128)(2,1)S(1)}, bf16[272,384]{1,0:T(8,128)(2,1)S(1)}, u32[]{:S(2)}, u32[]{:S(2)}) %collective-permute-start.27) | collective-permute-done | bytes 208928 | tf_op jit(solution)/shard_map/ppermute | solution.py:748
  135.2 1.1 collective-permute-start.35
  136.3 3.5 %collective-permute-done.29.refs_1_ = bf16[4,208,384]{2,1,0:T(8,128)(2,1)S(1)} collective-permute-done((bf16[4,208,384]{2,1,0:T(8,128)(2,1)S(1)}, bf16[4,208,384]{2,1,0:T(8,128)(2,1)S(1)}, u32[]{:S(2)}, u32[]{:S(2)}) %collective-permute-start.29) | collective-permute-done | bytes 639008 | tf_op jit(solution)/shard_map/ppermute | solution.py:754
  140.5 3.4 %collective-permute-start.32 = (bf16[288,384]{1,0:T(8,128)(2,1)S(1)}, bf16[288,384]{1,0:T(8,128)(2,1)S(1)}, u32[]{:S(2)}, u32[]{:S(2)}) collective-permute-start(bf16[288,384]{1,0:T(8,128)(2,1)S(1)} %get-tuple-element.214), channel_id=1, source_target_pairs={{0,12},{4,0},{8,4},{12,8},{1,13},{5,1},{9,5},{13,9},{2,14},{6,2},{... | collective-permute-start | bytes 663560 | tf_op jit(solution)/shard_map/ppermute | solution.py:748
  144.6 1.3 restore_kernel.1
  145.9 1.5 collective-permute-done.35.refs_1_
  147.4 1.1 finish_hidden_kernel.1
  148.5 10.6 %collective-permute-done.33.refs_2_ = bf16[288,384]{1,0:T(8,128)(2,1)S(1)} collective-permute-done((bf16[288,384]{1,0:T(8,128)(2,1)S(1)}, bf16[288,384]{1,0:T(8,128)(2,1)S(1)}, u32[]{:S(2)}, u32[]{:S(2)}) %collective-permute-start.33) | collective-permute-done | bytes 221216 | tf_op jit(solution)/shard_map/ppermute | solution.py:748
  160.1 1.4 restore_wide_kernel.1
  161.5 3.3 %collective-permute-done.36.refs_1_ = bf16[224,384]{1,0:T(8,128)(2,1)S(1)} collective-permute-done((bf16[224,384]{1,0:T(8,128)(2,1)S(1)}, bf16[224,384]{1,0:T(8,128)(2,1)S(1)}, u32[]{:S(2)}, u32[]{:S(2)}) %collective-permute-start.36) | collective-permute-done | bytes 172064 | tf_op jit(solution)/shard_map/ppermute | solution.py:754
  164.8 0.9 finish_joined_kernel.1
  (89 shorter events, 10.5 us)
Async XLA Ops:
  0.6 10.4 %copy-start.10 = (s32[24,24]{1,0:T(8,128)S(1)}, s32[24,24]{1,0:T(8,128)}, u32[]{:S(2)}) copy-start(s32[24,24]{1,0:T(8,128)} %param.21) | copy-start | bytes 6916
  0.7 10.7 %copy-start.9 = (s32[144,144]{1,0:T(8,128)S(1)}, s32[144,144]{1,0:T(8,128)}, u32[]{:S(2)}) copy-start(s32[144,144]{1,0:T(8,128)} %param.22) | copy-start | bytes 248836
  0.7 10.8 %copy-start.5 = (f32[529,6]{0,1:T(8,128)S(1)}, f32[529,6]{0,1:T(8,128)}, u32[]{:S(2)}) copy-start(f32[529,6]{0,1:T(8,128)} %param.27) | copy-start | bytes 38092
  4.1 12.7 %collective-permute-start = (bf16[352,384]{1,0:T(8,128)(2,1)}, bf16[352,384]{1,0:T(8,128)(2,1)S(1)}, u32[]{:S(2)}, u32[]{:S(2)}) collective-permute-start(bf16[352,384]{1,0:T(8,128)(2,1)} %get-tuple-element.127), channel_id=1, source_target_pairs={{0,4},{4,8},{8,12},{12,0},{1,5},{5,9},{9,13},{13,1},{2,6},{6,10},{... | collective-permute-start | bytes 811016 | tf_op jit(solution)/shard_map/ppermute | solution.py:748
  7.1 20.4 %collective-permute-start.1 = (bf16[352,384]{1,0:T(8,128)(2,1)}, bf16[352,384]{1,0:T(8,128)(2,1)S(1)}, u32[]{:S(2)}, u32[]{:S(2)}) collective-permute-start(bf16[352,384]{1,0:T(8,128)(2,1)} %get-tuple-element.128), channel_id=1, source_target_pairs={{0,8},{4,12},{8,0},{12,4},{1,9},{5,13},{9,1},{13,5},{2,10},{6,14},... | collective-permute-start | bytes 811016 | tf_op jit(solution)/shard_map/ppermute | solution.py:748
  9.7 17.9 %collective-permute-start.2 = (bf16[352,384]{1,0:T(8,128)(2,1)}, bf16[352,384]{1,0:T(8,128)(2,1)S(1)}, u32[]{:S(2)}, u32[]{:S(2)}) collective-permute-start(bf16[352,384]{1,0:T(8,128)(2,1)} %get-tuple-element.129), channel_id=1, source_target_pairs={{0,12},{4,0},{8,4},{12,8},{1,13},{5,1},{9,5},{13,9},{2,14},{6,2},{... | collective-permute-start | bytes 811016 | tf_op jit(solution)/shard_map/ppermute | solution.py:748
  12.1 1.9 %copy-start.1 = (bf16[192,768]{1,0:T(8,128)(2,1)S(1)}, bf16[192,768]{1,0:T(8,128)(2,1)}, u32[]{:S(2)}) copy-start(bf16[192,768]{1,0:T(8,128)(2,1)} %refs_0_.5) | copy-start | bytes 884740
  14.0 13.5 %copy-start.6 = (s32[8]{0:T(128)S(1)}, s32[8]{0:T(128)}, u32[]{:S(2)}) copy-start(s32[8]{0:T(128)} %refs_0_.4) | copy-start | bytes 100
  14.1 13.5 %copy-start.7 = (bf16[352,384]{1,0:T(8,128)(2,1)S(1)}, bf16[352,384]{1,0:T(8,128)(2,1)}, u32[]{:S(2)}) copy-start(bf16[352,384]{1,0:T(8,128)(2,1)} %get-tuple-element.126.refs_1_) | copy-start | bytes 811012
  27.5 14.3 %copy-start.2 = (bf16[96,3,1,384]{3,0,2,1:T(8,128)(2,1)S(1)}, bf16[96,3,1,384]{3,0,2,1:T(8,128)(2,1)}, u32[]{:S(2)}) copy-start(bf16[96,3,1,384]{3,0,2,1:T(8,128)(2,1)} %param.25) | copy-start | bytes 663556
  27.5 14.3 %copy-start.3 = (bf16[96,1,384]{2,0,1:T(8,128)(2,1)S(1)}, bf16[96,1,384]{2,0,1:T(8,128)(2,1)}, u32[]{:S(2)}) copy-start(bf16[96,1,384]{2,0,1:T(8,128)(2,1)} %param.28) | copy-start | bytes 221188
  28.5 15.0 %copy-start = (bf16[384,1,384]{2,0,1:T(8,128)(2,1)S(1)}, bf16[384,1,384]{2,0,1:T(8,128)(2,1)}, u32[]{:S(2)}) copy-start(bf16[384,1,384]{2,0,1:T(8,128)(2,1)} %param.34) | copy-start | bytes 884740
  28.5 12.1 %collective-permute-start.3 = (bf16[288,768]{1,0:T(8,128)(2,1)S(1)}, bf16[288,768]{1,0:T(8,128)(2,1)S(1)}, u32[]{:S(2)}, u32[]{:S(2)}) collective-permute-start(bf16[288,768]{1,0:T(8,128)(2,1)S(1)} %get-tuple-element.133.refs_0_), channel_id=1, source_target_pairs={{0,2},{1,3},{2,0},{3,1},{4,6},{5,7},{6,4},{7,5},{8,10},{9,11},{10,... | collective-permute-start | bytes 1327112 | tf_op jit(solution)/shard_map/ppermute | solution.py:751
  30.1 11.7 %collective-permute-start.5 = (bf16[3,192,384]{2,1,0:T(8,128)(2,1)S(1)}, bf16[3,192,384]{2,1,0:T(8,128)(2,1)S(1)}, u32[]{:S(2)}, u32[]{:S(2)}) collective-permute-start(bf16[3,192,384]{2,1,0:T(8,128)(2,1)S(1)} %get-tuple-element.136.refs_2_), channel_id=1, source_target_pairs={{0,16},{16,0},{1,17},{17,1},{2,18},{18,2},{3,19},{19,3},{4,20},{20... | collective-permute-start | bytes 1327112 | tf_op jit(solution)/shard_map/ppermute | solution.py:754
  31.6 12.0 %collective-permute-start.11 = (bf16[96,768]{1,0:T(8,128)(2,1)S(1)}, bf16[96,768]{1,0:T(8,128)(2,1)S(1)}, u32[]{:S(2)}, u32[]{:S(2)}) collective-permute-start(bf16[96,768]{1,0:T(8,128)(2,1)S(1)} %get-tuple-element.143), channel_id=1, source_target_pairs={{0,12},{4,0},{8,4},{12,8},{1,13},{5,1},{9,5},{13,9},{2,14},{6,2},{... | collective-permute-start | bytes 442376 | tf_op jit(solution)/shard_map/ppermute | solution.py:748
  38.9 13.1 %collective-permute-start.10 = (bf16[96,768]{1,0:T(8,128)(2,1)S(1)}, bf16[96,768]{1,0:T(8,128)(2,1)S(1)}, u32[]{:S(2)}, u32[]{:S(2)}) collective-permute-start(bf16[96,768]{1,0:T(8,128)(2,1)S(1)} %get-tuple-element.143), channel_id=1, source_target_pairs={{0,8},{4,12},{8,0},{12,4},{1,9},{5,13},{9,1},{13,5},{2,10},{6,14},... | collective-permute-start | bytes 442376 | tf_op jit(solution)/shard_map/ppermute | solution.py:748
  39.3 12.7 %collective-permute-start.9 = (bf16[96,768]{1,0:T(8,128)(2,1)S(1)}, bf16[96,768]{1,0:T(8,128)(2,1)S(1)}, u32[]{:S(2)}, u32[]{:S(2)}) collective-permute-start(bf16[96,768]{1,0:T(8,128)(2,1)S(1)} %get-tuple-element.143), channel_id=1, source_target_pairs={{0,4},{4,8},{8,12},{12,0},{1,5},{5,9},{9,13},{13,1},{2,6},{6,10},{... | collective-permute-start | bytes 442376 | tf_op jit(solution)/shard_map/ppermute | solution.py:748
  42.9 16.5 %collective-permute-start.14 = (bf16[192,768]{1,0:T(8,128)(2,1)S(1)}, bf16[192,768]{1,0:T(8,128)(2,1)S(1)}, u32[]{:S(2)}, u32[]{:S(2)}) collective-permute-start(bf16[192,768]{1,0:T(8,128)(2,1)S(1)} %get-tuple-element.148.refs_0_.refs_5_), channel_id=1, source_target_pairs={{0,2},{1,3},{2,0},{3,1},{4,6},{5,7},{6,4},{7,5},{8,10},{9,11},{10,... | collective-permute-start | bytes 884744 | tf_op jit(solution)/shard_map/ppermute | solution.py:751
  43.5 10.0 %collective-permute-start.4 = (bf16[2,288,768]{2,1,0:T(8,128)(2,1)S(1)}, bf16[2,288,768]{2,1,0:T(8,128)(2,1)S(1)}, u32[]{:S(2)}, u32[]{:S(2)}) collective-permute-start(bf16[2,288,768]{2,1,0:T(8,128)(2,1)S(1)} %get-tuple-element.135.refs_0_.refs_8_), channel_id=1, source_target_pairs={{0,1},{1,0},{2,3},{3,2},{4,5},{5,4},{6,7},{7,6},{8,9},{9,8},{10,11... | collective-permute-start | bytes 2654216 | tf_op jit(solution)/shard_map/ppermute | solution.py:751
  51.9 3.5 %copy-start.4 = (f32[2,192]{1,0:T(2,128)S(1)}, f32[2,192]{1,0:T(2,128)}, u32[]{:S(2)}) copy-start(f32[2,192]{1,0:T(2,128)} %refs_4_.1) | copy-start | bytes 4612
  52.0 11.1 %collective-permute-start.13 = (bf16[3,96,768]{2,1,0:T(8,128)(2,1)S(1)}, bf16[3,96,768]{2,1,0:T(8,128)(2,1)S(1)}, u32[]{:S(2)}, u32[]{:S(2)}) collective-permute-start(bf16[3,96,768]{2,1,0:T(8,128)(2,1)S(1)} %get-tuple-element.147.refs_1_), channel_id=1, source_target_pairs={{0,16},{16,0},{1,17},{17,1},{2,18},{18,2},{3,19},{19,3},{4,20},{20... | collective-permute-start | bytes 1327112 | tf_op jit(solution)/shard_map/ppermute | solution.py:754
  52.6 13.0 %collective-permute-start.8 = (bf16[384,384]{1,0:T(8,128)(2,1)S(1)}, bf16[384,384]{1,0:T(8,128)(2,1)S(1)}, u32[]{:S(2)}, u32[]{:S(2)}) collective-permute-start(bf16[384,384]{1,0:T(8,128)(2,1)S(1)} %get-tuple-element.139), channel_id=1, source_target_pairs={{0,12},{4,0},{8,4},{12,8},{1,13},{5,1},{9,5},{13,9},{2,14},{6,2},{... | collective-permute-start | bytes 884744 | tf_op jit(solution)/shard_map/ppermute | solution.py:748
  52.6 26.5 %collective-permute-start.7 = (bf16[384,384]{1,0:T(8,128)(2,1)S(1)}, bf16[384,384]{1,0:T(8,128)(2,1)S(1)}, u32[]{:S(2)}, u32[]{:S(2)}) collective-permute-start(bf16[384,384]{1,0:T(8,128)(2,1)S(1)} %get-tuple-element.139), channel_id=1, source_target_pairs={{0,8},{4,12},{8,0},{12,4},{1,9},{5,13},{9,1},{13,5},{2,10},{6,14},... | collective-permute-start | bytes 884744 | tf_op jit(solution)/shard_map/ppermute | solution.py:748
  53.5 25.6 %collective-permute-start.6 = (bf16[384,384]{1,0:T(8,128)(2,1)S(1)}, bf16[384,384]{1,0:T(8,128)(2,1)S(1)}, u32[]{:S(2)}, u32[]{:S(2)}) collective-permute-start(bf16[384,384]{1,0:T(8,128)(2,1)S(1)} %get-tuple-element.139), channel_id=1, source_target_pairs={{0,4},{4,8},{8,12},{12,0},{1,5},{5,9},{9,13},{13,1},{2,6},{6,10},{... | collective-permute-start | bytes 884744 | tf_op jit(solution)/shard_map/ppermute | solution.py:748
  55.5 4.5 %copy-start.11 = (f32[768]{0:T(1024)S(1)}, f32[768]{0:T(1024)}, u32[]{:S(2)}) copy-start(f32[768]{0:T(1024)} %param.33) | copy-start | bytes 9220
  59.4 6.0 %collective-permute-start.12 = (bf16[288,384]{1,0:T(8,128)(2,1)S(1)}, bf16[288,384]{1,0:T(8,128)(2,1)S(1)}, u32[]{:S(2)}, u32[]{:S(2)}) collective-permute-start(bf16[288,384]{1,0:T(8,128)(2,1)S(1)} %get-tuple-element.146.refs_0_.refs_2_), channel_id=1, source_target_pairs={{0,2},{1,3},{2,0},{3,1},{4,6},{5,7},{6,4},{7,5},{8,10},{9,11},{10,... | collective-permute-start | bytes 663560 | tf_op jit(solution)/shard_map/ppermute | solution.py:751
  63.1 16.3 %collective-permute-start.16 = (bf16[2,192,768]{2,1,0:T(8,128)(2,1)S(1)}, bf16[2,192,768]{2,1,0:T(8,128)(2,1)S(1)}, u32[]{:S(2)}, u32[]{:S(2)}) collective-permute-start(bf16[2,192,768]{2,1,0:T(8,128)(2,1)S(1)} %get-tuple-element.156.refs_3_), channel_id=1, source_target_pairs={{0,1},{1,0},{2,3},{3,2},{4,5},{5,4},{6,7},{7,6},{8,9},{9,8},{10,11... | collective-permute-start | bytes 1769480 | tf_op jit(solution)/shard_map/ppermute | solution.py:751
  65.5 13.9 %collective-permute-start.15 = (bf16[2,288,384]{2,1,0:T(8,128)(2,1)S(1)}, bf16[2,288,384]{2,1,0:T(8,128)(2,1)S(1)}, u32[]{:S(2)}, u32[]{:S(2)}) collective-permute-start(bf16[2,288,384]{2,1,0:T(8,128)(2,1)S(1)} %get-tuple-element.155.refs_1_), channel_id=1, source_target_pairs={{0,1},{1,0},{2,3},{3,2},{4,5},{5,4},{6,7},{7,6},{8,9},{9,8},{10,11... | collective-permute-start | bytes 1327112 | tf_op jit(solution)/shard_map/ppermute | solution.py:751
  85.7 3.6 %collective-permute-start.17 = (bf16[288,768]{1,0:T(8,128)(2,1)S(1)}, bf16[288,768]{1,0:T(8,128)(2,1)S(1)}, u32[]{:S(2)}, u32[]{:S(2)}) collective-permute-start(bf16[288,768]{1,0:T(8,128)(2,1)S(1)} %get-tuple-element.167), channel_id=1, source_target_pairs={{0,1},{1,0},{2,3},{3,2},{4,5},{5,4},{6,7},{7,6},{8,9},{9,8},{10,11... | collective-permute-start | bytes 1327112 | tf_op jit(solution)/shard_map/ppermute | solution.py:751
  85.7 24.1 %collective-permute-start.22 = (bf16[384,384]{1,0:T(8,128)(2,1)S(1)}, bf16[384,384]{1,0:T(8,128)(2,1)S(1)}, u32[]{:S(2)}, u32[]{:S(2)}) collective-permute-start(bf16[384,384]{1,0:T(8,128)(2,1)S(1)} %get-tuple-element.180), channel_id=1, source_target_pairs={{0,12},{4,0},{8,4},{12,8},{1,13},{5,1},{9,5},{13,9},{2,14},{6,2},{... | collective-permute-start | bytes 884744 | tf_op jit(solution)/shard_map/ppermute | solution.py:748
  85.8 28.0 %collective-permute-start.23 = (bf16[384,384]{1,0:T(8,128)(2,1)S(1)}, bf16[384,384]{1,0:T(8,128)(2,1)S(1)}, u32[]{:S(2)}, u32[]{:S(2)}) collective-permute-start(bf16[384,384]{1,0:T(8,128)(2,1)S(1)} %get-tuple-element.181), channel_id=1, source_target_pairs={{0,8},{4,12},{8,0},{12,4},{1,9},{5,13},{9,1},{13,5},{2,10},{6,14},... | collective-permute-start | bytes 884744 | tf_op jit(solution)/shard_map/ppermute | solution.py:748
  87.4 26.5 %collective-permute-start.24 = (bf16[384,384]{1,0:T(8,128)(2,1)S(1)}, bf16[384,384]{1,0:T(8,128)(2,1)S(1)}, u32[]{:S(2)}, u32[]{:S(2)}) collective-permute-start(bf16[384,384]{1,0:T(8,128)(2,1)S(1)} %get-tuple-element.182), channel_id=1, source_target_pairs={{0,4},{4,8},{8,12},{12,0},{1,5},{5,9},{9,13},{13,1},{2,6},{6,10},{... | collective-permute-start | bytes 884744 | tf_op jit(solution)/shard_map/ppermute | solution.py:748
  89.4 11.7 %collective-permute-start.20 = (bf16[288,768]{1,0:T(8,128)(2,1)S(1)}, bf16[288,768]{1,0:T(8,128)(2,1)S(1)}, u32[]{:S(2)}, u32[]{:S(2)}) collective-permute-start(bf16[288,768]{1,0:T(8,128)(2,1)S(1)} %get-tuple-element.175.refs_0_), channel_id=1, source_target_pairs={{0,2},{1,3},{2,0},{3,1},{4,6},{5,7},{6,4},{7,5},{8,10},{9,11},{10,... | collective-permute-start | bytes 1327112 | tf_op jit(solution)/shard_map/ppermute | solution.py:751
  94.5 8.1 %collective-permute-start.19 = (bf16[288,768]{1,0:T(8,128)(2,1)S(1)}, bf16[288,768]{1,0:T(8,128)(2,1)S(1)}, u32[]{:S(2)}, u32[]{:S(2)}) collective-permute-start(bf16[288,768]{1,0:T(8,128)(2,1)S(1)} %get-tuple-element.174), channel_id=1, source_target_pairs={{0,1},{1,0},{2,3},{3,2},{4,5},{5,4},{6,7},{7,6},{8,9},{9,8},{10,11... | collective-permute-start | bytes 1327112 | tf_op jit(solution)/shard_map/ppermute | solution.py:751
  101.1 13.9 %collective-permute-start.18 = (bf16[4,96,768]{2,1,0:T(8,128)(2,1)S(1)}, bf16[4,96,768]{2,1,0:T(8,128)(2,1)S(1)}, u32[]{:S(2)}, u32[]{:S(2)}) collective-permute-start(bf16[4,96,768]{2,1,0:T(8,128)(2,1)S(1)} %get-tuple-element.171), channel_id=1, source_target_pairs={{0,16},{16,0},{1,17},{17,1},{2,18},{18,2},{3,19},{19,3},{4,20},{20... | collective-permute-start | bytes 1769480 | tf_op jit(solution)/shard_map/ppermute | solution.py:754
  102.6 1.9 %collective-permute-start.25 = (bf16[288,768]{1,0:T(8,128)(2,1)S(1)}, bf16[288,768]{1,0:T(8,128)(2,1)S(1)}, u32[]{:S(2)}, u32[]{:S(2)}) collective-permute-start(bf16[288,768]{1,0:T(8,128)(2,1)S(1)} %get-tuple-element.183.refs_0_), channel_id=1, source_target_pairs={{0,1},{1,0},{2,3},{3,2},{4,5},{5,4},{6,7},{7,6},{8,9},{9,8},{10,11... | collective-permute-start | bytes 1327112 | tf_op jit(solution)/shard_map/ppermute | solution.py:751
  104.4 10.7 %collective-permute-start.21 = (bf16[144,768]{1,0:T(8,128)(2,1)S(1)}, bf16[144,768]{1,0:T(8,128)(2,1)S(1)}, u32[]{:S(2)}, u32[]{:S(2)}) collective-permute-start(bf16[144,768]{1,0:T(8,128)(2,1)S(1)} %slice.6), channel_id=1, source_target_pairs={{0,2},{1,3},{2,0},{3,1},{4,6},{5,7},{6,4},{7,5},{8,10},{9,11},{10,... | collective-permute-start | bytes 663560 | tf_op jit(solution)/shard_map/ppermute | solution.py:751
  109.8 14.4 %collective-permute-start.30 = (bf16[304,768]{1,0:T(8,128)(2,1)S(1)}, bf16[304,768]{1,0:T(8,128)(2,1)S(1)}, u32[]{:S(2)}, u32[]{:S(2)}) collective-permute-start(bf16[304,768]{1,0:T(8,128)(2,1)S(1)} %get-tuple-element.204), channel_id=1, source_target_pairs={{0,1},{1,0},{2,3},{3,2},{4,5},{5,4},{6,7},{7,6},{8,9},{9,8},{10,11... | collective-permute-start | bytes 1400840 | tf_op jit(solution)/shard_map/ppermute | solution.py:751
  115.4 10.0 %collective-permute-start.26 = (bf16[272,384]{1,0:T(8,128)(2,1)S(1)}, bf16[272,384]{1,0:T(8,128)(2,1)S(1)}, u32[]{:S(2)}, u32[]{:S(2)}) collective-permute-start(bf16[272,384]{1,0:T(8,128)(2,1)S(1)} %get-tuple-element.193), channel_id=1, source_target_pairs={{0,12},{4,0},{8,4},{12,8},{1,13},{5,1},{9,5},{13,9},{2,14},{6,2},{... | collective-permute-start | bytes 626696 | tf_op jit(solution)/shard_map/ppermute | solution.py:748
  117.8 17.2 %collective-permute-start.27 = (bf16[272,384]{1,0:T(8,128)(2,1)S(1)}, bf16[272,384]{1,0:T(8,128)(2,1)S(1)}, u32[]{:S(2)}, u32[]{:S(2)}) collective-permute-start(bf16[272,384]{1,0:T(8,128)(2,1)S(1)} %get-tuple-element.194), channel_id=1, source_target_pairs={{0,8},{4,12},{8,0},{12,4},{1,9},{5,13},{9,1},{13,5},{2,10},{6,14},... | collective-permute-start | bytes 626696 | tf_op jit(solution)/shard_map/ppermute | solution.py:748
  117.8 17.2 %collective-permute-start.28 = (bf16[272,384]{1,0:T(8,128)(2,1)S(1)}, bf16[272,384]{1,0:T(8,128)(2,1)S(1)}, u32[]{:S(2)}, u32[]{:S(2)}) collective-permute-start(bf16[272,384]{1,0:T(8,128)(2,1)S(1)} %get-tuple-element.195), channel_id=1, source_target_pairs={{0,4},{4,8},{8,12},{12,0},{1,5},{5,9},{9,13},{13,1},{2,6},{6,10},{... | collective-permute-start | bytes 626696 | tf_op jit(solution)/shard_map/ppermute | solution.py:748
  123.1 16.7 %collective-permute-start.29 = (bf16[4,208,384]{2,1,0:T(8,128)(2,1)S(1)}, bf16[4,208,384]{2,1,0:T(8,128)(2,1)S(1)}, u32[]{:S(2)}, u32[]{:S(2)}) collective-permute-start(bf16[4,208,384]{2,1,0:T(8,128)(2,1)S(1)} %get-tuple-element.202), channel_id=1, source_target_pairs={{0,16},{16,0},{1,17},{17,1},{2,18},{18,2},{3,19},{19,3},{4,20},{20... | collective-permute-start | bytes 1916936 | tf_op jit(solution)/shard_map/ppermute | solution.py:754
  124.4 15.4 %collective-permute-start.31 = (bf16[160,768]{1,0:T(8,128)(2,1)S(1)}, bf16[160,768]{1,0:T(8,128)(2,1)S(1)}, u32[]{:S(2)}, u32[]{:S(2)}) collective-permute-start(bf16[160,768]{1,0:T(8,128)(2,1)S(1)} %slice.7), channel_id=1, source_target_pairs={{0,2},{1,3},{2,0},{3,1},{4,6},{5,7},{6,4},{7,5},{8,10},{9,11},{10,... | collective-permute-start | bytes 737288 | tf_op jit(solution)/shard_map/ppermute | solution.py:751
  135.2 12.2 %collective-permute-start.35 = (bf16[576,384]{1,0:T(8,128)(2,1)S(1)}, bf16[576,384]{1,0:T(8,128)(2,1)S(1)}, u32[]{:S(2)}, u32[]{:S(2)}) collective-permute-start(bf16[576,384]{1,0:T(8,128)(2,1)S(1)} %get-tuple-element.217.refs_0_), channel_id=1, source_target_pairs={{0,16},{16,0},{1,17},{17,1},{2,18},{18,2},{3,19},{19,3},{4,20},{20... | collective-permute-start | bytes 1327112 | tf_op jit(solution)/shard_map/ppermute | solution.py:754
  140.5 8.0 %collective-permute-start.32 = (bf16[288,384]{1,0:T(8,128)(2,1)S(1)}, bf16[288,384]{1,0:T(8,128)(2,1)S(1)}, u32[]{:S(2)}, u32[]{:S(2)}) collective-permute-start(bf16[288,384]{1,0:T(8,128)(2,1)S(1)} %get-tuple-element.214), channel_id=1, source_target_pairs={{0,12},{4,0},{8,4},{12,8},{1,13},{5,1},{9,5},{13,9},{2,14},{6,2},{... | collective-permute-start | bytes 663560 | tf_op jit(solution)/shard_map/ppermute | solution.py:748
  143.9 15.2 %collective-permute-start.33 = (bf16[288,384]{1,0:T(8,128)(2,1)S(1)}, bf16[288,384]{1,0:T(8,128)(2,1)S(1)}, u32[]{:S(2)}, u32[]{:S(2)}) collective-permute-start(bf16[288,384]{1,0:T(8,128)(2,1)S(1)} %get-tuple-element.215), channel_id=1, source_target_pairs={{0,8},{4,12},{8,0},{12,4},{1,9},{5,13},{9,1},{13,5},{2,10},{6,14},... | collective-permute-start | bytes 663560 | tf_op jit(solution)/shard_map/ppermute | solution.py:748
  143.9 15.2 %collective-permute-start.34 = (bf16[288,384]{1,0:T(8,128)(2,1)S(1)}, bf16[288,384]{1,0:T(8,128)(2,1)S(1)}, u32[]{:S(2)}, u32[]{:S(2)}) collective-permute-start(bf16[288,384]{1,0:T(8,128)(2,1)S(1)} %get-tuple-element.216), channel_id=1, source_target_pairs={{0,4},{4,8},{8,12},{12,0},{1,5},{5,9},{9,13},{13,1},{2,6},{6,10},{... | collective-permute-start | bytes 663560 | tf_op jit(solution)/shard_map/ppermute | solution.py:748
  159.3 5.5 %collective-permute-start.36 = (bf16[224,384]{1,0:T(8,128)(2,1)S(1)}, bf16[224,384]{1,0:T(8,128)(2,1)S(1)}, u32[]{:S(2)}, u32[]{:S(2)}) collective-permute-start(bf16[224,384]{1,0:T(8,128)(2,1)S(1)} %get-tuple-element.222.refs_0_), channel_id=1, source_target_pairs={{0,16},{16,0},{1,17},{17,1},{2,18},{18,2},{3,19},{19,3},{4,20},{20... | collective-permute-start | bytes 516104 | tf_op jit(solution)/shard_map/ppermute | solution.py:754
  (1 other events, 0.7 us)
